TPU v7x, 32 devices: a whole 2x2x4 slice. The times are simulated.
32 devices in a mesh: ens: 2 (over y), row: 4 (over x, core), col: 4 (over z).
Axes of the slice: x: 2, y: 2, z: 4, core: 2. Of those that a mesh axis runs over, the one named last changes fastest.
Arguments:
- left_proj: bfloat16 [128, 1024, 1024], P('ens', 'row', 'col'), parts along dimension 0, may hold values from -6 to 6
- right_proj: bfloat16 [128, 1024, 1024], P('ens', 'col', 'row'), parts along dimension 0, may hold values from -0.1875 to 0.1875
Outputs:
- update: float32 [128, 1024, 1024], P('ens', 'row', 'col'), parts along dimension 0
There are 2 independent parts, one for each index of `ens`. A program takes and returns all parts, laid end to end along the dimension named above; each array names one. Nothing has to cross between parts.
All inputs are finite; a program needn't handle non-finite values.
Results may differ from a plain program's by a relative error of at most 0.0003.
Values may be sent and summed in bfloat16 or wider, within the bound.
No kernel may reach another device: no remote copies, remote signals or barrier semaphores. Data moves between devices by JAX's collectives and lax.ppermute only.
A program may use at most 192 MiB of HBM per device.

v0:
```python
import jax
import jax.numpy as jnp
from jax import lax
from jax.sharding import PartitionSpec as P


def add_block(full_left, piece):
    return jnp.einsum("cik,cjk->cij", full_left, piece, preferred_element_type=jnp.float32)


def channel_norm(triangle):
    channel_mean = jnp.mean(triangle, axis=0, keepdims=True)
    centered = triangle - channel_mean
    channel_var = jnp.mean(centered * centered, axis=0, keepdims=True)
    return centered / jnp.sqrt(channel_var + 1e-05)


def per_device(left_proj, right_proj):
    full_left = lax.all_gather(left_proj, "col", axis=2, tiled=True)
    triangle = add_block(full_left, lax.all_gather(right_proj, "row", axis=2, tiled=True))
    return channel_norm(triangle)


def solution(mesh):
    placed = (P("ens", "row", "col"), P("ens", "col", "row"))
    return jax.shard_map(
        per_device, mesh=mesh, in_specs=placed, out_specs=P("ens", "row", "col"), check_vma=False
    )
```

profile of v0, /device:TPU:0, one launch (start us, length us, event | category | flops | bytes accessed | tf_op | source)
XLA Modules:
  0.0 834.2 jit_solution(9214821747951553466)
XLA Ops:
  6.5 0.0 all-gather.3.cloned.1.call-start
  6.5 0.7 all-gather.3.cloned.1.call-update
  7.3 0.0 all-gather.5.cloned.1.call-start
  7.3 0.7 all-gather.5.cloned.1.call-update
  8.0 564.5 %all-gather.3.cloned.1.call-done = bf16[64,256,1024]{2,1,0:T(8,128)(2,1)} async-done(((bf16[64,256,256]{2,1,0:T(8,128)(2,1)}), bf16[64,256,1024]{2,1,0:T(8,128)(2,1)}) %all-gather.3.cloned.1.call-update) | async-done | bytes 33554448 | tf_op jit(solution)/shard_map/all_gather | solution.py:19
  572.6 205.8 %all-gather.5.cloned.1.call-done = bf16[64,256,1024]{2,1,0:T(8,128)(2,1)} async-done(((bf16[64,256,256]{2,1,0:T(8,128)(2,1)}), bf16[64,256,1024]{2,1,0:T(8,128)(2,1)}) %all-gather.5.cloned.1.call-update) | async-done | bytes 33554448 | tf_op jit(solution)/shard_map/all_gather | solution.py:20
  778.4 29.0 %fusion = (f32[256,256]{1,0:T(8,128)S(1)}, f32[64,256,256]{2,1,0:T(8,128)}) fusion(bf16[64,256,1024]{2,1,0:T(8,128)(2,1)} %all-gather.3.cloned.1.call-done, bf16[64,256,1024]{2,1,0:T(8,128)(2,1)} %all-gather.5.cloned.1.call-done), kind=kOutput, calls=%fused_computation.4 | convolution fusion | flops 8594063360 | bytes 84148224 | tf_op jit(solution)/shard_map/cik,cjk->cij/dot_general | solution.py:8
  807.4 7.4 multiply_reduce_fusion
  814.9 0.1 add_sqrt_fusion
  815.0 12.4 %subtract_divide_fusion = f32[64,256,256]{2,1,0:T(8,128)} fusion(f32[64,256,256]{2,1,0:T(8,128)} %get-tuple-element.6, f32[256,256]{1,0:T(8,128)S(1)} %add_sqrt_fusion, f32[256,256]{1,0:T(8,128)S(1)} %broadcast_multiply_fusion), kind=kLoop, calls=%fused_computation.1 | loop fusion | flops 8388608 | bytes 34078720 | tf_op jit(solution)/shard_map/div | solution.py:15
  (1 shorter events, 0.0 us)
Async XLA Ops:
  6.5 566.0 %all-gather.3.cloned.1.call-start = ((), (), s32[]{:S(2)}) async-start(), calls=%async_computation | async-start | bytes 41943040 | tf_op jit(solution)/shard_map/all_gather | solution.py:19
  7.3 771.1 %all-gather.5.cloned.1.call-start = ((), (), s32[]{:S(2)}) async-start(), calls=%async_computation.1 | async-start | bytes 41943040 | tf_op jit(solution)/shard_map/all_gather | solution.py:20
Sparse Core Ops, SparseCore 0:
  8.9 563.5 all-gather.2
  574.1 204.1 all-gather.4
where the time goes:
time: 834 us
  waiting for transfers between devices  772 us (93%)
  matrix products  29 us (3%)
  other arithmetic  19.9 us (2%)
  between operations  13.4 us (2%)
    all_gather x1, waiting for transfers between devices, per_device(): full_left = lax.all_gather(left_proj, 'col', axis=2, tiled=True)  565 us
    all_gather x1, waiting for transfers between devices, per_device(): lax.all_gather(right_proj, 'row', axis=2, tiled=True)  206 us
    dot_general x1, matrix products, add_block(): jnp.einsum('cik,cjk->cij', full_left, piece, preferred_element_type=jnp.f...  29 us
  transfers between devices with their start and end apart: 2, of which 2 were waited for; matrix products, arithmetic and copies ran while one was open for 0% of the time, Pallas kernels for 0%

commit v1 on v0

v1 whole, which is shorter than its diff:
```python
import functools

import jax
import jax.numpy as jnp
from jax import lax
from jax.experimental import pallas as pl
from jax.experimental.pallas import tpu as pltpu
from jax.sharding import PartitionSpec as P

EPS = 1e-5
HALF_SCALE = 16.0
VMEM = 48 * 1024 * 1024


def gathered(left_proj, right_proj):
    full_left = lax.all_gather(left_proj, "col", axis=2, tiled=True)
    full_right = lax.all_gather(right_proj, "row", axis=2, tiled=True)
    triangle = jnp.einsum("cik,cjk->cij", full_left, full_right, preferred_element_type=jnp.float32)
    channel_mean = jnp.mean(triangle, axis=0, keepdims=True)
    centered = triangle - channel_mean
    channel_var = jnp.mean(centered * centered, axis=0, keepdims=True)
    return centered / jnp.sqrt(channel_var + EPS)


def dot_nt(a, b):
    return lax.dot_general(a, b, (((1,), (1,)), ((), ())), preferred_element_type=jnp.float32)


def params():
    return pltpu.CompilerParams(vmem_limit_bytes=VMEM, dimension_semantics=("arbitrary",))


def tiles_kernel(step, choices, order, inner, *refs):
    *lefts, right, out = refs
    for c in range(step):
        acc, at = None, 0
        for turn, count in enumerate(choices):
            one = lefts[at][c]
            if count == 2:
                one = jnp.where(inner[0] == 1, one, lefts[at + 1][c])
            at += count
            term = dot_nt(one, right[order[turn], c])
            acc = term if acc is None else acc + term
        out[c] = acc


def tiles(order, inner, lefts, right, right_at, n):
    step = 4 if n % 4 == 0 and right_at % 4 == 0 and all(at % 4 == 0 for group in lefts for _, at in group) else 1
    flat = [pair for group in lefts for pair in group]
    rows, depth = flat[0][0].shape[1:]
    cols = right.shape[2]
    specs = [pl.BlockSpec((step, rows, depth), functools.partial(lambda off, c, *_: (off + c, 0, 0), at // step)) for _, at in flat]
    specs.append(pl.BlockSpec((4, step, cols, depth), lambda c, *_: (0, right_at // step + c, 0, 0)))
    return pl.pallas_call(
        functools.partial(tiles_kernel, step, tuple(len(group) for group in lefts)),
        grid_spec=pltpu.PrefetchScalarGridSpec(
            num_scalar_prefetch=2,
            grid=(n // step,),
            in_specs=specs,
            out_specs=pl.BlockSpec((step, rows, cols), lambda c, *_: (c, 0, 0)),
        ),
        out_shape=jax.ShapeDtypeStruct((n, rows, cols), jnp.float32),
        compiler_params=params(),
        cost_estimate=pl.CostEstimate(
            flops=8 * n * rows * cols * depth,
            bytes_accessed=n * ((len(flat) * rows + 4 * cols) * depth * 2 + rows * cols * 4),
            transcendentals=0,
        ),
        name="tiles",
    )(order, inner, *[array for array, _ in flat], right)


def norm_kernel(both, pairs, inner, *refs):
    *refs, out = refs
    shared, own, sent = refs[:both], refs[both : both + pairs], refs[both + pairs :]

    def write(parts):
        total = sum(jnp.sum(part[...], axis=0) for part in parts)
        channel_mean = total * (1.0 / out.shape[0])
        squares = 0.0
        for part in parts:
            centered = part[...] - channel_mean
            squares += jnp.sum(centered * centered, axis=0)
        factor = 1.0 / jnp.sqrt(squares * (1.0 / out.shape[0]) + EPS)
        at = 0
        for part in parts:
            n = part.shape[0]
            out[at : at + n] = (part[...] - channel_mean) * factor
            at += n

    @pl.when(inner[0] == 1)
    def _():
        write([*shared, *own])

    @pl.when(inner[0] != 1)
    def _():
        write([*shared, *sent])


def norm(inner, shared, own, sent):
    rows, cols = shared[0].shape[1:]
    channels = sum(part.shape[0] for part in [*shared, *own])
    step = 32
    spec = lambda part, used: pl.BlockSpec((part.shape[0], step, cols), lambda i, inner: (0, i * used(inner[0]), 0))
    specs = [spec(part, lambda flag: 1) for part in shared]
    specs += [spec(part, lambda flag: flag) for part in own]
    specs += [spec(part, lambda flag: 1 - flag) for part in sent]
    size = channels * rows * cols
    return pl.pallas_call(
        functools.partial(norm_kernel, len(shared), len(own)),
        grid_spec=pltpu.PrefetchScalarGridSpec(
            num_scalar_prefetch=1,
            grid=(rows // step,),
            in_specs=specs,
            out_specs=pl.BlockSpec((channels, step, cols), lambda i, inner: (0, i, 0)),
        ),
        out_shape=jax.ShapeDtypeStruct((channels, rows, cols), jnp.float32),
        compiler_params=params(),
        cost_estimate=pl.CostEstimate(flops=5 * size, bytes_accessed=8 * size, transcendentals=0),
        name="norm",
    )(inner, *shared, *own, *sent)


SWAP = [(0, 1), (1, 0), (2, 3), (3, 2)]
INWARD = [(0, 1), (3, 2)]
OUTWARD = [(1, 0), (2, 3)]
MIDDLE = [(1, 2), (2, 1)]


def after(block, *done):
    return lax.optimization_barrier((block, *done))[0] if done else block


class Slots:
    def __init__(self):
        self.ended = {}

    def held(self, k, block):
        return after(block, *self.ended.get(k - 2, []), *self.ended.get(k - 3, []))

    def go(self, k, block, pairs, *also):
        arrived = lax.ppermute(after(self.held(k, block), *also), "col", pairs)
        self.ended.setdefault(k, []).append(arrived)
        return arrived


def line(left, right):
    col = lax.axis_index("col")
    is_inner = (col == 1) | (col == 2)
    inner = is_inner.astype(jnp.int32).reshape(1)
    order = (col ^ jnp.where(is_inner, jnp.array([0, 1, 3, 2], jnp.int32), jnp.array([0, 1, 2, 3], jnp.int32))).astype(jnp.int32)
    quarter = left.shape[0] // 4
    half, eighth = 2 * quarter, quarter // 2

    slots = Slots()
    cut = lambda array, at, n: lax.slice_in_dim(array, at, at + n, axis=0)
    part = lambda k, array, at, n: cut(slots.held(k, array), at, n)
    rows_of = lambda block: lax.all_gather(block, "row", axis=0, tiled=False)
    na, nb, fa, fb = (0, quarter), (quarter, quarter), (half, quarter), (half + quarter, quarter)

    right_own = rows_of(right)
    first = cut(left, *na)
    p2_na, e_na = slots.go(0, first, MIDDLE), slots.go(0, first, SWAP)
    p2_nb, r_fa = slots.go(1, cut(left, *nb), MIDDLE), slots.go(1, cut(right, *fa), INWARD)
    p3_na, e_nb = slots.go(2, e_na, MIDDLE), slots.go(2, part(2, left, *nb), SWAP)
    q2_na = slots.go(2, p2_na, OUTWARD)
    p2_fa, r_fb = slots.go(3, part(3, left, *fa), MIDDLE), slots.go(3, part(3, right, *fb), INWARD)
    q2_nb = slots.go(3, p2_nb, OUTWARD, q2_na)
    p3_nb, e_fa = slots.go(4, e_nb, MIDDLE), slots.go(4, part(4, left, *fa), INWARD)
    q3_na = slots.go(4, p3_na, OUTWARD, q2_nb)
    p2_fb, e_fb = slots.go(5, part(5, left, *fb), MIDDLE, right_own), slots.go(5, part(5, left, *fb), INWARD)
    right_fa = rows_of(after(r_fa, p2_na, e_na))
    right_fb = rows_of(after(r_fb, p3_na, e_nb, q2_na))

    def near(at, e, p2, q2, p3, q3, *done):
        lefts = [[(after(left, *done), at)], [(e, 0)], [(p2, 0), (q2, 0)], [(p3, 0), (q3, 0)]]
        return tiles(order, inner, lefts, right_own, at, quarter)

    sizes = [eighth, eighth, eighth, eighth // 2, eighth // 2]
    starts = [sum(sizes[:k]) for k in range(len(sizes))]
    e_of = lambda at: (e_fa, at) if at < quarter else (e_fb, at - quarter)
    p2_of = lambda at: (p2_fa, at) if at < quarter else (p2_fb, at - quarter)
    right_of = lambda at: (right_fa, at) if at < quarter else (right_fb, at - quarter)
    lefts_of = lambda at, p3: [[(left, half + at)], [e_of(at)], [p2_of(at)], [(p3, 0)]]
    p3, shared, own, sent, payloads = [], [], [], [], []
    for k in range(len(sizes) + 2):
        if k >= 2:
            j = k - 2
            at, n = starts[j], sizes[j]
            tile = tiles(order, inner, lefts_of(at, p3[j]), *right_of(at), n) * HALF_SCALE
            if j == 0:
                offset = jnp.mean(tile, axis=0, keepdims=True).astype(jnp.float16)
            payload = (tile - offset.astype(jnp.float32)).astype(jnp.float16)
            if j == 0:
                payload = jnp.concatenate([payload, offset], axis=0)
            payloads.append(payload)
            ties = [last] if j != 1 else [last, shared[1]]
            if 2 <= j <= 3:
                ties.append(own[j - 2])
            last = arrived = lax.ppermute(after(payload, *ties), "col", OUTWARD)
            if j == 0:
                there = arrived[n:].astype(jnp.float32)
                arrived = arrived[:n]
                shared.append(near(quarter, e_nb, p2_nb, q2_nb, p3_nb, q3_nb, payload))
            sent.append((arrived.astype(jnp.float32) + there) * (1.0 / HALF_SCALE))
            own.append(tiles(order, inner, lefts_of(at, after(p3[j], payload)), right_own, half + at, n))
        if k < len(sizes):
            e, here = e_of(starts[k])
            block = cut(slots.held(6 + k, e), here, sizes[k])
            p3.append(slots.go(6 + k, block, MIDDLE, *payloads[-1:], *(shared[:1] if k == 1 else [])))
        if k == 0:
            q3_nb = last = slots.go(6, p3_nb, OUTWARD, q3_na)
            shared.append(near(0, e_na, p2_na, q2_na, p3_na, q3_na, p3_nb))
    return norm(inner, shared, own, sent)


def solution(mesh):
    placed = (P("ens", "row", "col"), P("ens", "col", "row"))
    per_device = line if mesh.shape["col"] == 4 and mesh.shape["row"] == 4 else gathered
    return jax.shard_map(
        per_device, mesh=mesh, in_specs=placed, out_specs=P("ens", "row", "col"), check_vma=False
    )
```

time: 834 us -> 536 us (0.64)
  waiting for transfers between devices: 772 us -> 303 us
  starting transfers between devices: 0.04 us -> 103 us
  Pallas kernels: 0 us -> 75.3 us
  local copies, waits for them, and re-layouts: 0 us -> 32.2 us
  matrix products: 29 us -> 0 us
  other arithmetic: 19.9 us -> 7.95 us
    all_gather x2 -> x3, waiting for transfers between devices: 770 us -> 0.04 us  [line(): rows_of = lambda block: lax.all_gather(block, 'row', axis=0, tiled=False)]
    ppermute x0 -> x26, waiting for transfers between devices: none -> 302 us  [the longest x21 210 us: go(): arrived = lax.ppermute(after(self.held(k, block), *also), 'col', pairs)]
    ppermute x0 -> x26, starting transfers between devices: none -> 103 us  [the longest x21 96.7 us: go(): arrived = lax.ppermute(after(self.held(k, block), *also), 'col', pairs)]
    pallas_call x0 -> x13, Pallas kernels: none -> 75.3 us  [the longest x12 60.4 us: tiles(): pl.pallas_call(functools.partial(tiles_kernel, step, tuple((len(group) fo...]
    dot_general x1 -> x0, matrix products: 29 us -> none  [add_block(): jnp.einsum('cik,cjk->cij', full_left, piece, preferred_element_type=jnp.f...]
    slice x0 -> x12, local copies, waits for them, and re-layouts: none -> 23.8 us  [line(): cut = lambda array, at, n: lax.slice_in_dim(array, at, at + n, axis=0)]
    div x2 -> x0, other arithmetic: 12.4 us -> none  [the longest x1 12.4 us: channel_norm(): return centered / jnp.sqrt(channel_var + 1e-05)]
    unnamed x0 -> x32, local copies, waits for them, and re-layouts: none -> 8.38 us
  transfers between devices with their start and end apart: 2 -> 29, of which waited for: 2 -> 11; matrix products, arithmetic and copies ran while one was open for 0% -> 6% of each run, Pallas kernels for 0% -> 11%
where the time goes in v1:
time: 536 us; the launch traced here: 535 us
  waiting for transfers between devices  303 us (57%)
  starting transfers between devices  103 us (19%)
  Pallas kernels  75.3 us (14%)
  local copies, waits for them, and re-layouts  32.2 us (6%)
  between operations  13.6 us (3%)
  other arithmetic  7.95 us (1%)
    ppermute x21, waiting for transfers between devices, go(): arrived = lax.ppermute(after(self.held(k, block), *also), 'col', pairs)  210 us
    ppermute x21, starting transfers between devices, go(): arrived = lax.ppermute(after(self.held(k, block), *also), 'col', pairs)  96.7 us
    ppermute x5, waiting for transfers between devices, line(): last = arrived = lax.ppermute(after(payload, *ties), 'col', OUTWARD)  91.8 us
    pallas_call x12, Pallas kernels, tiles(): pl.pallas_call(functools.partial(tiles_kernel, step, tuple((len(group) fo...  60.4 us
    slice x12, local copies, waits for them, and re-layouts, line(): cut = lambda array, at, n: lax.slice_in_dim(array, at, at + n, axis=0)  23.8 us
    pallas_call x1, Pallas kernels, norm(): pl.pallas_call(functools.partial(norm_kernel, len(shared), len(own)), gri...  14.9 us
  transfers between devices with their start and end apart: 29, of which 11 were waited for; matrix products, arithmetic and copies ran while one was open for 6% of the time, Pallas kernels for 11%

profile of v1, /device:TPU:0, one launch (start us, length us, event | category | flops | bytes accessed | tf_op | source)
XLA Modules:
  0.0 534.8 jit_solution(1232154013560992340)
XLA Ops:
  7.3 4.0 fusion.4
  12.1 5.8 %collective-permute-start.1 = (bf16[16,256,256]{2,1,0:T(8,128)(2,1)S(1)}, bf16[16,256,256]{2,1,0:T(8,128)(2,1)}, u32[]{:S(2)}, u32[]{:S(2)}) collective-permute-start(bf16[16,256,256]{2,1,0:T(8,128)(2,1)S(1)} %get-tuple-element.102), channel_id=1, source_target_pairs={{0,1},{1,0},{2,3},{3,2},{4,5},{5,4},{6,7},{7,6},{8,9},{9,8},{10,11... | collective-permute-start | bytes 6291464 | tf_op jit(solution)/shard_map/ppermute | solution.py:142
  17.9 2.2 slice.49
  20.1 3.0 collective-permute-start.6
  23.1 40.8 %collective-permute-done.1.refs_1_ = bf16[16,256,256]{2,1,0:T(8,128)(2,1)} collective-permute-done((bf16[16,256,256]{2,1,0:T(8,128)(2,1)S(1)}, bf16[16,256,256]{2,1,0:T(8,128)(2,1)}, u32[]{:S(2)}, u32[]{:S(2)}) %collective-permute-start.1) | collective-permute-done | bytes 2097184 | tf_op jit(solution)/shard_map/ppermute | solution.py:142
  63.9 43.5 %collective-permute-done.6 = bf16[16,256,256]{2,1,0:T(8,128)(2,1)} collective-permute-done((bf16[16,256,256]{2,1,0:T(8,128)(2,1)S(1)}, bf16[16,256,256]{2,1,0:T(8,128)(2,1)}, u32[]{:S(2)}, u32[]{:S(2)}) %collective-permute-start.6) | collective-permute-done | bytes 2097184 | tf_op jit(solution)/shard_map/ppermute | solution.py:142
  108.3 1.7 slice.47
  110.0 4.2 collective-permute-start.2
  114.2 2.0 collective-permute-start.3
  117.6 2.5 slice.52
  120.1 46.4 %collective-permute-start.12 = (bf16[16,256,256]{2,1,0:T(8,128)(2,1)S(1)}, bf16[16,256,256]{2,1,0:T(8,128)(2,1)}, u32[]{:S(2)}, u32[]{:S(2)}) collective-permute-start(bf16[16,256,256]{2,1,0:T(8,128)(2,1)S(1)} %slice.52), channel_id=1, source_target_pairs={{0,1},{3,2},{4,5},{7,6},{8,9},{11,10},{12,13},{15,14},{16,17},{19,... | collective-permute-start | bytes 6291464 | tf_op jit(solution)/shard_map/ppermute | solution.py:142
  166.5 36.8 %collective-permute-done.4.refs_3_ = bf16[16,256,256]{2,1,0:T(8,128)(2,1)S(1)} collective-permute-done((bf16[16,256,256]{2,1,0:T(8,128)(2,1)S(1)}, bf16[16,256,256]{2,1,0:T(8,128)(2,1)S(1)}, u32[]{:S(2)}, u32[]{:S(2)}) %collective-permute-start.4) | collective-permute-done | bytes 2097184 | tf_op jit(solution)/shard_map/ppermute | solution.py:142
  203.3 1.3 copy-done.13
  207.5 1.7 slice.51
  210.1 2.0 collective-permute-start.7
  212.1 3.1 slice.50
  215.2 9.1 %collective-permute-start.10 = (bf16[16,256,256]{2,1,0:T(8,128)(2,1)}, bf16[16,256,256]{2,1,0:T(8,128)(2,1)}, u32[]{:S(2)}, u32[]{:S(2)}) collective-permute-start(bf16[16,256,256]{2,1,0:T(8,128)(2,1)} %slice.50), channel_id=1, source_target_pairs={{0,1},{3,2},{4,5},{7,6},{8,9},{11,10},{12,13},{15,14},{16,17},{19,... | collective-permute-start | bytes 6291464 | tf_op jit(solution)/shard_map/ppermute | solution.py:142
  224.3 29.2 %collective-permute-done.8.refs_3_ = bf16[16,256,256]{2,1,0:T(8,128)(2,1)S(1)} collective-permute-done((bf16[16,256,256]{2,1,0:T(8,128)(2,1)S(1)}, bf16[16,256,256]{2,1,0:T(8,128)(2,1)S(1)}, u32[]{:S(2)}, u32[]{:S(2)}) %collective-permute-start.8) | collective-permute-done | bytes 2097184 | tf_op jit(solution)/shard_map/ppermute | solution.py:142
  254.8 3.9 slice.54
  258.7 9.9 %collective-permute-start.16 = (bf16[16,256,256]{2,1,0:T(8,128)(2,1)}, bf16[16,256,256]{2,1,0:T(8,128)(2,1)S(1)}, u32[]{:S(2)}, u32[]{:S(2)}) collective-permute-start(bf16[16,256,256]{2,1,0:T(8,128)(2,1)} %slice.54), channel_id=1, source_target_pairs={{0,1},{3,2},{4,5},{7,6},{8,9},{11,10},{12,13},{15,14},{16,17},{19,... | collective-permute-start | bytes 6291464 | tf_op jit(solution)/shard_map/ppermute | solution.py:142
  268.6 2.0 collective-permute-start.15
  270.6 29.6 %collective-permute-done.9.refs_5_ = bf16[16,256,256]{2,1,0:T(8,128)(2,1)} collective-permute-done((bf16[16,256,256]{2,1,0:T(8,128)(2,1)}, bf16[16,256,256]{2,1,0:T(8,128)(2,1)}, u32[]{:S(2)}, u32[]{:S(2)}) %collective-permute-start.9) | collective-permute-done | bytes 2097184 | tf_op jit(solution)/shard_map/ppermute | solution.py:142
  300.2 2.3 slice.53
  304.6 4.5 tiles.13
  309.6 1.4 copy-done.8
  311.0 10.2 %tiles.12.refs_0_ = f32[16,256,256]{2,1,0:T(8,128)} custom-call(s32[4]{0:T(128)S(1)} %fusion.3.order, s32[1]{0:T(128)} %bitcast.inner, bf16[64,256,256]{2,1,0:T(8,128)(2,1)} %refs_0_.21, bf16[16,256,256]{2,1,0:T(8,128)(2,1)} %collective-permute-done.1.refs_1_, bf16[16,256,256]{2,1,0:T(8,128)(2,1)S(1)} %copy-done.8, bf16[16,256,256]{2,1,0:T(8,128)(2,1)} %copy-done.13, ...), custom_call_target="tpu_custom_call" | custom-call | flops 2147483648 | bytes 25165824 | tf_op jit(solution)/shard_map/tiles/pallas_call | solution.py:54
  323.2 1.3 pad_maximum_fusion
  324.5 29.0 %collective-permute-done.14.refs_5_ = bf16[16,256,256]{2,1,0:T(8,128)(2,1)} collective-permute-done((bf16[16,256,256]{2,1,0:T(8,128)(2,1)}, bf16[16,256,256]{2,1,0:T(8,128)(2,1)}, u32[]{:S(2)}, u32[]{:S(2)}) %collective-permute-start.14) | collective-permute-done | bytes 2097184 | tf_op jit(solution)/shard_map/ppermute | solution.py:142
  354.6 1.7 collective-permute-start.18
  357.6 10.2 %tiles.14.refs_1_ = f32[16,256,256]{2,1,0:T(8,128)} custom-call(s32[4]{0:T(128)S(1)} %fusion.3.order, s32[1]{0:T(128)} %bitcast.inner, bf16[64,256,256]{2,1,0:T(8,128)(2,1)} %refs_0_.21, bf16[16,256,256]{2,1,0:T(8,128)(2,1)} %collective-permute-done.2.refs_1_, bf16[16,256,256]{2,1,0:T(8,128)(2,1)S(1)} %copy-done.11, bf16[16,256,256]{2,1,0:T(8,128)(2,1)} %copy-done.14, ...), custom_call_target="tpu_custom_call" | custom-call | flops 2147483648 | bytes 25165824 | tf_op jit(solution)/shard_map/tiles/pallas_call | solution.py:54
  367.8 4.5 tiles.16
  372.4 1.3 copy-done
  374.7 4.6 tiles.18
  379.9 41.2 %collective-permute-done.21 = f16[9,256,256]{2,1,0:T(8,128)(2,1)} collective-permute-done((f16[9,256,256]{2,1,0:T(8,128)(2,1)}, f16[9,256,256]{2,1,0:T(8,128)(2,1)}, u32[]{:S(2)}, u32[]{:S(2)}) %collective-permute-start.21) | collective-permute-done | bytes 1179680 | tf_op jit(solution)/shard_map/ppermute | solution.py:200
  422.4 4.5 tiles.15.refs_2_
  427.0 1.3 copy-done.2
  428.3 32.8 %collective-permute-done.22 = f16[8,256,256]{2,1,0:T(8,128)(2,1)S(1)} collective-permute-done((f16[8,256,256]{2,1,0:T(8,128)(2,1)S(1)}, f16[8,256,256]{2,1,0:T(8,128)(2,1)S(1)}, u32[]{:S(2)}, u32[]{:S(2)}) %collective-permute-start.22) | collective-permute-done | bytes 1048608 | tf_op jit(solution)/shard_map/ppermute | solution.py:200
  464.1 4.5 tiles.17.refs_3_
  468.6 1.4 copy-done.3
  470.0 3.2 tiles.22
  473.2 3.2 tiles.20
  476.7 6.5 %collective-permute-done.23 = f16[8,256,256]{2,1,0:T(8,128)(2,1)S(1)} collective-permute-done((f16[8,256,256]{2,1,0:T(8,128)(2,1)S(1)}, f16[8,256,256]{2,1,0:T(8,128)(2,1)S(1)}, u32[]{:S(2)}, u32[]{:S(2)}) %collective-permute-start.23) | collective-permute-done | bytes 1048608 | tf_op jit(solution)/shard_map/ppermute | solution.py:200
  485.4 4.5 tiles.19.refs_4_
  489.9 11.3 %collective-permute-done.24 = f16[4,256,256]{2,1,0:T(8,128)(2,1)S(1)} collective-permute-done((f16[4,256,256]{2,1,0:T(8,128)(2,1)S(1)}, f16[4,256,256]{2,1,0:T(8,128)(2,1)S(1)}, u32[]{:S(2)}, u32[]{:S(2)}) %collective-permute-start.24) | collective-permute-done | bytes 524320 | tf_op jit(solution)/shard_map/ppermute | solution.py:200
  502.6 3.2 tiles.21.refs_5_
  505.8 3.2 tiles.23.refs_6_
  509.0 4.2 add_multiply_fusion
  513.4 14.9 %norm.1 = f32[64,256,256]{2,1,0:T(8,128)} custom-call(s32[1]{0:T(128)} %bitcast.inner, f32[16,256,256]{2,1,0:T(8,128)} %tiles.12.refs_0_, f32[16,256,256]{2,1,0:T(8,128)} %tiles.14.refs_1_, f32[8,256,256]{2,1,0:T(8,128)} %copy-done.2, f32[8,256,256]{2,1,0:T(8,128)} %copy-done.3, f32[8,256,256]{2,1,0:T(8,128)} %copy-done.4, ...), custom_call_target="tpu_custom_call" | custom-call | flops 20971520 | bytes 33554432 | tf_op jit(solution)/shard_map/norm/pallas_call | solution.py:109
  (80 shorter events, 25.3 us)
Async XLA Ops:
  6.5 262.0 %all-gather.7.cloned.1.call-start = ((), (), s32[]{:S(2)}) async-start(), calls=%async_computation | async-start | bytes 41943040 | tf_op jit(solution)/shard_map/all_gather | solution.py:158
  7.3 297.3 %all-gather.9.cloned.1.call-start = ((), (), s32[]{:S(2)}) async-start(), calls=%async_computation.1 | async-start | bytes 10485760 | tf_op jit(solution)/shard_map/all_gather | solution.py:158
  11.3 11.8 %collective-permute-start = (bf16[16,256,256]{2,1,0:T(8,128)(2,1)S(1)}, bf16[16,256,256]{2,1,0:T(8,128)(2,1)S(1)}, u32[]{:S(2)}, u32[]{:S(2)}) collective-permute-start(bf16[16,256,256]{2,1,0:T(8,128)(2,1)S(1)} %get-tuple-element.102), channel_id=1, source_target_pairs={{1,2},{2,1},{5,6},{6,5},{9,10},{10,9},{13,14},{14,13},{17,18},{18,... | collective-permute-start | bytes 6291464 | tf_op jit(solution)/shard_map/ppermute | solution.py:142
  12.1 51.9 %collective-permute-start.1 = (bf16[16,256,256]{2,1,0:T(8,128)(2,1)S(1)}, bf16[16,256,256]{2,1,0:T(8,128)(2,1)}, u32[]{:S(2)}, u32[]{:S(2)}) collective-permute-start(bf16[16,256,256]{2,1,0:T(8,128)(2,1)S(1)} %get-tuple-element.102), channel_id=1, source_target_pairs={{0,1},{1,0},{2,3},{3,2},{4,5},{5,4},{6,7},{7,6},{8,9},{9,8},{10,11... | collective-permute-start | bytes 6291464 | tf_op jit(solution)/shard_map/ppermute | solution.py:142
  20.1 87.3 %collective-permute-start.6 = (bf16[16,256,256]{2,1,0:T(8,128)(2,1)S(1)}, bf16[16,256,256]{2,1,0:T(8,128)(2,1)}, u32[]{:S(2)}, u32[]{:S(2)}) collective-permute-start(bf16[16,256,256]{2,1,0:T(8,128)(2,1)S(1)} %slice.49), channel_id=1, source_target_pairs={{0,1},{3,2},{4,5},{7,6},{8,9},{11,10},{12,13},{15,14},{16,17},{19,... | collective-permute-start | bytes 6291464 | tf_op jit(solution)/shard_map/ppermute | solution.py:142
  23.1 93.1 %copy-start.7 = (bf16[16,256,256]{2,1,0:T(8,128)(2,1)}, bf16[16,256,256]{2,1,0:T(8,128)(2,1)S(1)}, u32[]{:S(2)}) copy-start(bf16[16,256,256]{2,1,0:T(8,128)(2,1)S(1)} %collective-permute-done.refs_2_) | copy-start | bytes 6291460
  107.4 267.3 %all-gather.11.cloned.1.call-start = ((), (), s32[]{:S(2)}) async-start(), calls=%async_computation.2 | async-start | bytes 10485760 | tf_op jit(solution)/shard_map/all_gather | solution.py:158
  107.5 10.1 %collective-permute-start.5 = (bf16[16,256,256]{2,1,0:T(8,128)(2,1)}, bf16[16,256,256]{2,1,0:T(8,128)(2,1)S(1)}, u32[]{:S(2)}, u32[]{:S(2)}) collective-permute-start(bf16[16,256,256]{2,1,0:T(8,128)(2,1)} %get-tuple-element.101), channel_id=1, source_target_pairs={{1,2},{2,1},{5,6},{6,5},{9,10},{10,9},{13,14},{14,13},{17,18},{18,... | collective-permute-start | bytes 6291464 | tf_op jit(solution)/shard_map/ppermute | solution.py:142
  110.0 56.5 %collective-permute-start.2 = (bf16[16,256,256]{2,1,0:T(8,128)(2,1)S(1)}, bf16[16,256,256]{2,1,0:T(8,128)(2,1)}, u32[]{:S(2)}, u32[]{:S(2)}) collective-permute-start(bf16[16,256,256]{2,1,0:T(8,128)(2,1)S(1)} %slice.47), channel_id=1, source_target_pairs={{0,1},{1,0},{2,3},{3,2},{4,5},{5,4},{6,7},{7,6},{8,9},{9,8},{10,11... | collective-permute-start | bytes 6291464 | tf_op jit(solution)/shard_map/ppermute | solution.py:142
  114.2 52.3 %collective-permute-start.3 = (bf16[16,256,256]{2,1,0:T(8,128)(2,1)}, bf16[16,256,256]{2,1,0:T(8,128)(2,1)}, u32[]{:S(2)}, u32[]{:S(2)}) collective-permute-start(bf16[16,256,256]{2,1,0:T(8,128)(2,1)} %collective-permute-done.1.refs_1_), channel_id=1, source_target_pairs={{1,2},{2,1},{5,6},{6,5},{9,10},{10,9},{13,14},{14,13},{17,18},{18,... | collective-permute-start | bytes 6291464 | tf_op jit(solution)/shard_map/ppermute | solution.py:142
  116.3 87.1 %collective-permute-start.4 = (bf16[16,256,256]{2,1,0:T(8,128)(2,1)S(1)}, bf16[16,256,256]{2,1,0:T(8,128)(2,1)S(1)}, u32[]{:S(2)}, u32[]{:S(2)}) collective-permute-start(bf16[16,256,256]{2,1,0:T(8,128)(2,1)S(1)} %collective-permute-done.refs_2_), channel_id=1, source_target_pairs={{1,0},{2,3},{5,4},{6,7},{9,8},{10,11},{13,12},{14,15},{17,16},{18,... | collective-permute-start | bytes 6291464 | tf_op jit(solution)/shard_map/ppermute | solution.py:142
  117.6 2.5 copy-start.9
  120.1 85.6 %collective-permute-start.12 = (bf16[16,256,256]{2,1,0:T(8,128)(2,1)S(1)}, bf16[16,256,256]{2,1,0:T(8,128)(2,1)}, u32[]{:S(2)}, u32[]{:S(2)}) collective-permute-start(bf16[16,256,256]{2,1,0:T(8,128)(2,1)S(1)} %slice.52), channel_id=1, source_target_pairs={{0,1},{3,2},{4,5},{7,6},{8,9},{11,10},{12,13},{15,14},{16,17},{19,... | collective-permute-start | bytes 6291464 | tf_op jit(solution)/shard_map/ppermute | solution.py:142
  203.3 1.3 copy-start.13
  204.7 1.6 copy-start.10
  206.2 47.2 %collective-permute-start.8 = (bf16[16,256,256]{2,1,0:T(8,128)(2,1)S(1)}, bf16[16,256,256]{2,1,0:T(8,128)(2,1)S(1)}, u32[]{:S(2)}, u32[]{:S(2)}) collective-permute-start(bf16[16,256,256]{2,1,0:T(8,128)(2,1)S(1)} %copy-done.10), channel_id=1, source_target_pairs={{1,0},{2,3},{5,4},{6,7},{9,8},{10,11},{13,12},{14,15},{17,16},{18,... | collective-permute-start | bytes 6291464 | tf_op jit(solution)/shard_map/ppermute | solution.py:142
  209.3 45.5 %collective-permute-start.11 = (bf16[16,256,256]{2,1,0:T(8,128)(2,1)S(1)}, bf16[16,256,256]{2,1,0:T(8,128)(2,1)S(1)}, u32[]{:S(2)}, u32[]{:S(2)}) collective-permute-start(bf16[16,256,256]{2,1,0:T(8,128)(2,1)S(1)} %slice.51), channel_id=1, source_target_pairs={{1,2},{2,1},{5,6},{6,5},{9,10},{10,9},{13,14},{14,13},{17,18},{18,... | collective-permute-start | bytes 6291464 | tf_op jit(solution)/shard_map/ppermute | solution.py:142
  210.1 60.5 %collective-permute-start.7 = (bf16[16,256,256]{2,1,0:T(8,128)(2,1)}, bf16[16,256,256]{2,1,0:T(8,128)(2,1)}, u32[]{:S(2)}, u32[]{:S(2)}) collective-permute-start(bf16[16,256,256]{2,1,0:T(8,128)(2,1)} %collective-permute-done.2.refs_1_), channel_id=1, source_target_pairs={{1,2},{2,1},{5,6},{6,5},{9,10},{10,9},{13,14},{14,13},{17,18},{18,... | collective-permute-start | bytes 6291464 | tf_op jit(solution)/shard_map/ppermute | solution.py:142
  215.2 55.4 %collective-permute-start.10 = (bf16[16,256,256]{2,1,0:T(8,128)(2,1)}, bf16[16,256,256]{2,1,0:T(8,128)(2,1)}, u32[]{:S(2)}, u32[]{:S(2)}) collective-permute-start(bf16[16,256,256]{2,1,0:T(8,128)(2,1)} %slice.50), channel_id=1, source_target_pairs={{0,1},{3,2},{4,5},{7,6},{8,9},{11,10},{12,13},{15,14},{16,17},{19,... | collective-permute-start | bytes 6291464 | tf_op jit(solution)/shard_map/ppermute | solution.py:142
  253.5 5.2 copy-start.14
  253.5 46.7 %collective-permute-start.9 = (bf16[16,256,256]{2,1,0:T(8,128)(2,1)}, bf16[16,256,256]{2,1,0:T(8,128)(2,1)}, u32[]{:S(2)}, u32[]{:S(2)}) collective-permute-start(bf16[16,256,256]{2,1,0:T(8,128)(2,1)} %collective-permute-done.3.refs_4_), channel_id=1, source_target_pairs={{1,0},{2,3},{5,4},{6,7},{9,8},{10,11},{13,12},{14,15},{17,16},{18,... | collective-permute-start | bytes 6291464 | tf_op jit(solution)/shard_map/ppermute | solution.py:142
  254.8 3.9 copy-start.12
  258.7 45.9 %copy-start.15 = (s32[4]{0:T(128)S(1)}, s32[4]{0:T(128)}, u32[]{:S(2)}) copy-start(s32[4]{0:T(128)} %constant.7.clone) | copy-start | bytes 52
  258.7 62.4 %collective-permute-start.16 = (bf16[16,256,256]{2,1,0:T(8,128)(2,1)}, bf16[16,256,256]{2,1,0:T(8,128)(2,1)S(1)}, u32[]{:S(2)}, u32[]{:S(2)}) collective-permute-start(bf16[16,256,256]{2,1,0:T(8,128)(2,1)} %slice.54), channel_id=1, source_target_pairs={{0,1},{3,2},{4,5},{7,6},{8,9},{11,10},{12,13},{15,14},{16,17},{19,... | collective-permute-start | bytes 6291464 | tf_op jit(solution)/shard_map/ppermute | solution.py:142
  268.6 52.6 %collective-permute-start.15 = (bf16[16,256,256]{2,1,0:T(8,128)(2,1)}, bf16[16,256,256]{2,1,0:T(8,128)(2,1)}, u32[]{:S(2)}, u32[]{:S(2)}) collective-permute-start(bf16[16,256,256]{2,1,0:T(8,128)(2,1)} %slice.54), channel_id=1, source_target_pairs={{1,2},{2,1},{5,6},{6,5},{9,10},{10,9},{13,14},{14,13},{17,18},{18,... | collective-permute-start | bytes 6291464 | tf_op jit(solution)/shard_map/ppermute | solution.py:142
  302.5 2.1 collective-permute-start.13
  303.2 50.3 %collective-permute-start.14 = (bf16[16,256,256]{2,1,0:T(8,128)(2,1)}, bf16[16,256,256]{2,1,0:T(8,128)(2,1)}, u32[]{:S(2)}, u32[]{:S(2)}) collective-permute-start(bf16[16,256,256]{2,1,0:T(8,128)(2,1)} %collective-permute-done.7.refs_4_), channel_id=1, source_target_pairs={{1,0},{2,3},{5,4},{6,7},{9,8},{10,11},{13,12},{14,15},{17,16},{18,... | collective-permute-start | bytes 6291464 | tf_op jit(solution)/shard_map/ppermute | solution.py:142
  309.3 1.7 copy-start.8
  322.4 45.4 %collective-permute-start.17 = (bf16[8,256,256]{2,1,0:T(8,128)(2,1)S(1)}, bf16[8,256,256]{2,1,0:T(8,128)(2,1)S(1)}, u32[]{:S(2)}, u32[]{:S(2)}) collective-permute-start(bf16[8,256,256]{2,1,0:T(8,128)(2,1)S(1)} %slice.55), channel_id=1, source_target_pairs={{1,2},{2,1},{5,6},{6,5},{9,10},{10,9},{13,14},{14,13},{17,18},{18,... | collective-permute-start | bytes 3145736 | tf_op jit(solution)/shard_map/ppermute | solution.py:142
  323.2 34.5 %copy-start.11 = (bf16[16,256,256]{2,1,0:T(8,128)(2,1)S(1)}, bf16[16,256,256]{2,1,0:T(8,128)(2,1)}, u32[]{:S(2)}) copy-start(bf16[16,256,256]{2,1,0:T(8,128)(2,1)} %copy-done.9) | copy-start | bytes 6291460
  354.6 20.1 %collective-permute-start.18 = (bf16[8,256,256]{2,1,0:T(8,128)(2,1)}, bf16[8,256,256]{2,1,0:T(8,128)(2,1)}, u32[]{:S(2)}, u32[]{:S(2)}) collective-permute-start(bf16[8,256,256]{2,1,0:T(8,128)(2,1)} %slice.56), channel_id=1, source_target_pairs={{1,2},{2,1},{5,6},{6,5},{9,10},{10,9},{13,14},{14,13},{17,18},{18,... | collective-permute-start | bytes 3145736 | tf_op jit(solution)/shard_map/ppermute | solution.py:142
  356.3 64.8 %collective-permute-start.21 = (f16[9,256,256]{2,1,0:T(8,128)(2,1)}, f16[9,256,256]{2,1,0:T(8,128)(2,1)}, u32[]{:S(2)}, u32[]{:S(2)}) collective-permute-start(f16[9,256,256]{2,1,0:T(8,128)(2,1)} %pad_maximum_fusion), channel_id=1, source_target_pairs={{1,0},{2,3},{5,4},{6,7},{9,8},{10,11},{13,12},{14,15},{17,16},{18,... | collective-permute-start | bytes 3538952 | tf_op jit(solution)/shard_map/ppermute | solution.py:200
  372.4 1.3 copy-start
  373.7 1.1 copy-start.5
  374.7 4.6 copy-start.1
  421.1 40.0 %collective-permute-start.22 = (f16[8,256,256]{2,1,0:T(8,128)(2,1)S(1)}, f16[8,256,256]{2,1,0:T(8,128)(2,1)S(1)}, u32[]{:S(2)}, u32[]{:S(2)}) collective-permute-start(f16[8,256,256]{2,1,0:T(8,128)(2,1)S(1)} %get-tuple-element.97), channel_id=1, source_target_pairs={{1,0},{2,3},{5,4},{6,7},{9,8},{10,11},{13,12},{14,15},{17,16},{18,... | collective-permute-start | bytes 3145736 | tf_op jit(solution)/shard_map/ppermute | solution.py:200
  427.0 1.3 copy-start.2
  428.3 35.8 %copy-start.6 = (bf16[8,256,256]{2,1,0:T(8,128)(2,1)S(1)}, bf16[8,256,256]{2,1,0:T(8,128)(2,1)}, u32[]{:S(2)}) copy-start(bf16[8,256,256]{2,1,0:T(8,128)(2,1)} %copy-done.5) | copy-start | bytes 3145732
  461.1 22.1 %collective-permute-start.23 = (f16[8,256,256]{2,1,0:T(8,128)(2,1)S(1)}, f16[8,256,256]{2,1,0:T(8,128)(2,1)S(1)}, u32[]{:S(2)}, u32[]{:S(2)}) collective-permute-start(f16[8,256,256]{2,1,0:T(8,128)(2,1)S(1)} %get-tuple-element.98), channel_id=1, source_target_pairs={{1,0},{2,3},{5,4},{6,7},{9,8},{10,11},{13,12},{14,15},{17,16},{18,... | collective-permute-start | bytes 3145736 | tf_op jit(solution)/shard_map/ppermute | solution.py:200
  462.4 7.6 %collective-permute-start.20 = (bf16[4,256,256]{2,1,0:T(8,128)(2,1)S(1)}, bf16[4,256,256]{2,1,0:T(8,128)(2,1)S(1)}, u32[]{:S(2)}, u32[]{:S(2)}) collective-permute-start(bf16[4,256,256]{2,1,0:T(8,128)(2,1)S(1)} %slice.58), channel_id=1, source_target_pairs={{1,2},{2,1},{5,6},{6,5},{9,10},{10,9},{13,14},{14,13},{17,18},{18,... | collective-permute-start | bytes 1572872 | tf_op jit(solution)/shard_map/ppermute | solution.py:142
  463.2 10.0 %collective-permute-start.19 = (bf16[4,256,256]{2,1,0:T(8,128)(2,1)S(1)}, bf16[4,256,256]{2,1,0:T(8,128)(2,1)S(1)}, u32[]{:S(2)}, u32[]{:S(2)}) collective-permute-start(bf16[4,256,256]{2,1,0:T(8,128)(2,1)S(1)} %slice.57), channel_id=1, source_target_pairs={{1,2},{2,1},{5,6},{6,5},{9,10},{10,9},{13,14},{14,13},{17,18},{18,... | collective-permute-start | bytes 1572872 | tf_op jit(solution)/shard_map/ppermute | solution.py:142
  468.6 1.4 copy-start.3
  483.2 18.1 %collective-permute-start.24 = (f16[4,256,256]{2,1,0:T(8,128)(2,1)S(1)}, f16[4,256,256]{2,1,0:T(8,128)(2,1)S(1)}, u32[]{:S(2)}, u32[]{:S(2)}) collective-permute-start(f16[4,256,256]{2,1,0:T(8,128)(2,1)S(1)} %get-tuple-element.99), channel_id=1, source_target_pairs={{1,0},{2,3},{5,4},{6,7},{9,8},{10,11},{13,12},{14,15},{17,16},{18,... | collective-permute-start | bytes 1572872 | tf_op jit(solution)/shard_map/ppermute | solution.py:200
  489.9 15.8 %copy-start.4 = (f32[8,256,256]{2,1,0:T(8,128)}, f32[8,256,256]{2,1,0:T(8,128)S(1)}, u32[]{:S(2)}) copy-start(f32[8,256,256]{2,1,0:T(8,128)S(1)} %tiles.19.refs_4_) | copy-start | bytes 6291460
  501.3 11.9 %collective-permute-start.25 = (f16[4,256,256]{2,1,0:T(8,128)(2,1)S(1)}, f16[4,256,256]{2,1,0:T(8,128)(2,1)S(1)}, u32[]{:S(2)}, u32[]{:S(2)}) collective-permute-start(f16[4,256,256]{2,1,0:T(8,128)(2,1)S(1)} %get-tuple-element.100), channel_id=1, source_target_pairs={{1,0},{2,3},{5,4},{6,7},{9,8},{10,11},{13,12},{14,15},{17,16},{18,... | collective-permute-start | bytes 1572872 | tf_op jit(solution)/shard_map/ppermute | solution.py:200
Sparse Core Ops, SparseCore 0:
  8.9 204.2 all-gather.6
  214.7 58.2 all-gather.8
  274.6 58.2 all-gather.10

commit v2 on v1

v2 whole, which is shorter than its diff:
```python
import functools

import jax
import jax.numpy as jnp
from jax import lax
from jax.experimental import pallas as pl
from jax.experimental.pallas import tpu as pltpu
from jax.sharding import PartitionSpec as P

EPS = 1e-5
HALF_SCALE = 16.0


def gathered(left_proj, right_proj):
    full_left = lax.all_gather(left_proj, "col", axis=2, tiled=True)
    full_right = lax.all_gather(right_proj, "row", axis=2, tiled=True)
    triangle = jnp.einsum("cik,cjk->cij", full_left, full_right, preferred_element_type=jnp.float32)
    channel_mean = jnp.mean(triangle, axis=0, keepdims=True)
    centered = triangle - channel_mean
    channel_var = jnp.mean(centered * centered, axis=0, keepdims=True)
    return centered / jnp.sqrt(channel_var + EPS)


def dot_nt(a, b):
    return lax.dot_general(a, b, (((1,), (1,)), ((), ())), preferred_element_type=jnp.float32)


def params(limit):
    return pltpu.CompilerParams(vmem_limit_bytes=limit * 1024 * 1024, dimension_semantics=("arbitrary",))


def tiles_kernel(step, choices, order, inner, *refs):
    *lefts, right, out = refs
    for c in range(step):
        acc, at = None, 0
        for turn, count in enumerate(choices):
            one = lefts[at][c]
            if count == 2:
                one = jnp.where(inner[0] == 1, one, lefts[at + 1][c])
            at += count
            term = dot_nt(one, right[order[turn], c])
            acc = term if acc is None else acc + term
        out[c] = acc


def tiles(order, inner, lefts, right, right_at, n):
    step = 4 if n % 4 == 0 and right_at % 4 == 0 and all(at % 4 == 0 for group in lefts for _, at in group) else 1
    flat = [pair for group in lefts for pair in group]
    rows, depth = flat[0][0].shape[1:]
    cols = right.shape[2]
    specs = [pl.BlockSpec((step, rows, depth), functools.partial(lambda off, c, *_: (off + c, 0, 0), at // step)) for _, at in flat]
    specs.append(pl.BlockSpec((4, step, cols, depth), lambda c, *_: (0, right_at // step + c, 0, 0)))
    return pl.pallas_call(
        functools.partial(tiles_kernel, step, tuple(len(group) for group in lefts)),
        grid_spec=pltpu.PrefetchScalarGridSpec(
            num_scalar_prefetch=2,
            grid=(n // step,),
            in_specs=specs,
            out_specs=pl.BlockSpec((step, rows, cols), lambda c, *_: (c, 0, 0)),
        ),
        out_shape=jax.ShapeDtypeStruct((n, rows, cols), jnp.float32),
        compiler_params=params(32),
        cost_estimate=pl.CostEstimate(
            flops=8 * n * rows * cols * depth,
            bytes_accessed=n * ((len(flat) * rows + 4 * cols) * depth * 2 + rows * cols * 4),
            transcendentals=0,
        ),
        name="tiles",
    )(order, inner, *[array for array, _ in flat], right)


def norm_kernel(both, pairs, inner, *refs):
    *refs, out = refs
    shared, own, sent = refs[:both], refs[both : both + pairs], refs[both + pairs :]

    def write(parts):
        total = sum(jnp.sum(part[...], axis=0) for part in parts)
        channel_mean = total * (1.0 / out.shape[0])
        squares = 0.0
        for part in parts:
            centered = part[...] - channel_mean
            squares += jnp.sum(centered * centered, axis=0)
        factor = 1.0 / jnp.sqrt(squares * (1.0 / out.shape[0]) + EPS)
        at = 0
        for part in parts:
            n = part.shape[0]
            out[at : at + n] = (part[...] - channel_mean) * factor
            at += n

    @pl.when(inner[0] == 1)
    def _():
        write([*shared, *own])

    @pl.when(inner[0] != 1)
    def _():
        write([*shared, *sent])


def norm(inner, shared, own, sent):
    rows, cols = shared[0].shape[1:]
    channels = sum(part.shape[0] for part in [*shared, *own])
    step = 32
    spec = lambda part, used: pl.BlockSpec((part.shape[0], step, cols), lambda i, inner: (0, i * used(inner[0]), 0))
    specs = [spec(part, lambda flag: 1) for part in shared]
    specs += [spec(part, lambda flag: flag) for part in own]
    specs += [spec(part, lambda flag: 1 - flag) for part in sent]
    size = channels * rows * cols
    return pl.pallas_call(
        functools.partial(norm_kernel, len(shared), len(own)),
        grid_spec=pltpu.PrefetchScalarGridSpec(
            num_scalar_prefetch=1,
            grid=(rows // step,),
            in_specs=specs,
            out_specs=pl.BlockSpec((channels, step, cols), lambda i, inner: (0, i, 0)),
        ),
        out_shape=jax.ShapeDtypeStruct((channels, rows, cols), jnp.float32),
        compiler_params=params(20),
        cost_estimate=pl.CostEstimate(flops=5 * size, bytes_accessed=8 * size, transcendentals=0),
        name="norm",
    )(inner, *shared, *own, *sent)


SWAP = [(0, 1), (1, 0), (2, 3), (3, 2)]
INWARD = [(0, 1), (3, 2)]
OUTWARD = [(1, 0), (2, 3)]
MIDDLE = [(1, 2), (2, 1)]


def after(block, *done):
    return lax.optimization_barrier((block, *done))[0] if done else block


def find(parts, at):
    first, array = [part for part in parts if part[0] <= at][-1]
    return array, at - first


def line(left, right):
    col = lax.axis_index("col")
    is_inner = (col == 1) | (col == 2)
    inner = is_inner.astype(jnp.int32).reshape(1)
    order = (col ^ jnp.where(is_inner, jnp.array([0, 1, 3, 2], jnp.int32), jnp.array([0, 1, 2, 3], jnp.int32))).astype(jnp.int32)
    half, quarter, unit = left.shape[0] // 2, left.shape[0] // 4, left.shape[0] // 16

    cut = lambda array, at, n: lax.slice_in_dim(array, at, at + n, axis=0)
    go = lambda block, pairs: lax.ppermute(block, "col", pairs)
    rows_of = lambda block: lax.all_gather(block, "row", axis=0, tiled=False)

    right_own = rows_of(right)
    first = cut(left, 0, half)
    e_n, p2_n = go(first, SWAP), go(first, MIDDLE)
    left_on, right_on = after(left, first), after(right, first)
    second, f0, f1 = cut(left_on, half, half), cut(left_on, half, unit), cut(left_on, half + unit, half - unit)
    fa, fb = cut(right_on, half, 3 * unit), cut(right_on, half + 3 * unit, 5 * unit)
    ended = (e_n, p2_n, second, f0, f1, fa, fb)

    p3_n = go(after(e_n, *ended), MIDDLE)
    r_fa, r_fb = go(after(fa, *ended), INWARD), go(after(fb, *ended), INWARD)
    q2_n = go(after(p2_n, *ended), OUTWARD)
    ended = (p3_n, r_fa, r_fb, q2_n)

    right_f = [(0, rows_of(after(r_fa, *ended))), (3 * unit, rows_of(after(r_fb, *ended)))]
    p2_f = go(after(second, *ended), MIDDLE)
    e_f = [(0, go(after(f0, *ended), INWARD)), (unit, go(after(f1, *ended), INWARD))]
    q3_na = go(cut(after(p3_n, *ended), 0, quarter), OUTWARD)
    q3_nb = go(cut(after(p3_n, *ended, q3_na), quarter, quarter), OUTWARD)

    def near(at, q3, *done):
        lefts = [[(after(left, *done), at)], [(e_n, at)], [(p2_n, at), (q2_n, at)], [(p3_n, at), (q3, 0)]]
        return tiles(order, inner, lefts, right_own, at, quarter)

    near_a = near(0, q3_na)
    ended = (p2_f, e_f[0][1], e_f[1][1], q3_nb, near_a)

    sizes = [unit, 2 * unit, 2 * unit, 2 * unit, unit]
    starts = [sum(sizes[:k]) for k in range(len(sizes))]
    lefts_of = lambda at, p3: [[(left, half + at)], [find(e_f, at)], [(p2_f, at)], [(p3, 0)]]
    held = [(first, after(array, *ended)) for first, array in e_f]
    p3 = []
    for at, n in zip(starts, sizes):
        array, here = find(held, at)
        p3.append(go(cut(array, here, n) if n < array.shape[0] else array, MIDDLE))
    own, sent, payloads, outward = [], [], [], [None, q3_nb]
    for j, (at, n) in enumerate(zip(starts, sizes)):
        tile = tiles(order, inner, lefts_of(at, after(p3[j], *payloads[-1:], *outward[j : j + 1][: j - 1 if j > 1 else 0])), *find(right_f, at), n) * HALF_SCALE
        if j == 0:
            offset = jnp.mean(tile, axis=0, keepdims=True).astype(jnp.float16)
        payload = (after(tile, *payloads[-1:]) - offset.astype(jnp.float32)).astype(jnp.float16)
        payloads.append(payload)
        if j == 0:
            payload = jnp.concatenate([payload, offset], axis=0)
        if j == 1:
            near_b = near(quarter, q3_nb, payload)
        ties = outward[j : j + 1] if j else []
        if j == 3:
            ties += [near_b, own[0]]
        if j == 4:
            ties += own[1:3]
        arrived = go(after(payload, *ties, *sent[: max(j - 1, 0)]), OUTWARD)
        outward.append(arrived)
        if j == 0:
            there = arrived[n:].astype(jnp.float32)
            arrived = arrived[:n]
        sent.append((arrived.astype(jnp.float32) + there) * (1.0 / HALF_SCALE))
        own.append(tiles(order, inner, lefts_of(at, after(p3[j], payload)), right_own, half + at, n))
    return norm(inner, [near_a, near_b], own, sent)


def solution(mesh):
    placed = (P("ens", "row", "col"), P("ens", "col", "row"))
    per_device = line if mesh.shape["col"] == 4 and mesh.shape["row"] == 4 else gathered
    return jax.shard_map(
        per_device, mesh=mesh, in_specs=placed, out_specs=P("ens", "row", "col"), check_vma=False
    )
```

time: 536 us -> 457 us (0.85)
  starting transfers between devices: 103 us -> 51.2 us
  waiting for transfers between devices: 303 us -> 264 us
  local copies, waits for them, and re-layouts: 32.2 us -> 47.4 us
  Pallas kernels: 75.3 us -> 66.5 us
    ppermute x26 -> x21, starting transfers between devices: 103 us -> 51.1 us  [line(): go = lambda block, pairs: lax.ppermute(block, 'col', pairs)]
    ppermute x26 -> x21, waiting for transfers between devices: 302 us -> 264 us  [line(): go = lambda block, pairs: lax.ppermute(block, 'col', pairs)]
    unnamed x32 -> x58, local copies, waits for them, and re-layouts: 8.38 us -> 27.7 us
    slice x12 -> x10, local copies, waits for them, and re-layouts: 23.8 us -> 19.7 us  [line(): cut = lambda array, at, n: lax.slice_in_dim(array, at, at + n, axis=0)]
  transfers between devices with their start and end apart: 29 -> 24, of which waited for: 11 -> 10; matrix products, arithmetic and copies ran while one was open for 6% -> 6% of each run, Pallas kernels for 11% -> 12%
where the time goes in v2:
time: 457 us; the launch traced here: 456 us
  waiting for transfers between devices  264 us (58%)
  Pallas kernels  66.5 us (15%)
  starting transfers between devices  51.2 us (11%)
  local copies, waits for them, and re-layouts  47.4 us (10%)
  between operations  13.6 us (3%)
  other arithmetic  12.6 us (3%)
    ppermute x21, waiting for transfers between devices, line(): go = lambda block, pairs: lax.ppermute(block, 'col', pairs)  264 us
    pallas_call x12, Pallas kernels, tiles(): pl.pallas_call(functools.partial(tiles_kernel, step, tuple((len(group) fo...  56.8 us
    ppermute x21, starting transfers between devices, line(): go = lambda block, pairs: lax.ppermute(block, 'col', pairs)  51.1 us
    unnamed x58, local copies, waits for them, and re-layouts  27.7 us
    slice x10, local copies, waits for them, and re-layouts, line(): cut = lambda array, at, n: lax.slice_in_dim(array, at, at + n, axis=0)  19.7 us
    pallas_call x1, Pallas kernels, norm(): pl.pallas_call(functools.partial(norm_kernel, len(shared), len(own)), gri...  9.66 us
  transfers between devices with their start and end apart: 24, of which 10 were waited for; matrix products, arithmetic and copies ran while one was open for 6% of the time, Pallas kernels for 12%

profile of v2, /device:TPU:0, one launch (start us, length us, event | category | flops | bytes accessed | tf_op | source)
XLA Modules:
  0.0 455.7 jit_solution(5556128929320504683)
XLA Ops:
  7.3 2.6 slice.42
  9.9 3.1 collective-permute-start
  13.0 2.7 collective-permute-start.1
  15.7 2.5 slice.43
  18.3 2.4 slice.45
  20.7 3.1 slice-done.3
  23.9 1.7 slice.47
  25.6 78.1 %collective-permute-done.refs_1_ = bf16[32,256,256]{2,1,0:T(8,128)(2,1)} collective-permute-done((bf16[32,256,256]{2,1,0:T(8,128)(2,1)S(1)}, bf16[32,256,256]{2,1,0:T(8,128)(2,1)}, u32[]{:S(2)}, u32[]{:S(2)}) %collective-permute-start) | collective-permute-done | bytes 4194336 | tf_op jit(solution)/shard_map/ppermute | solution.py:146
  105.0 2.7 collective-permute-start.3
  107.7 9.7 %collective-permute-start.5 = (bf16[20,256,256]{2,1,0:T(8,128)(2,1)}, bf16[20,256,256]{2,1,0:T(8,128)(2,1)S(1)}, u32[]{:S(2)}, u32[]{:S(2)}) collective-permute-start(bf16[20,256,256]{2,1,0:T(8,128)(2,1)} %slice.47), channel_id=1, source_target_pairs={{0,1},{3,2},{4,5},{7,6},{8,9},{11,10},{12,13},{15,14},{16,17},{19,... | collective-permute-start | bytes 7864328 | tf_op jit(solution)/shard_map/ppermute | solution.py:146
  117.4 2.5 collective-permute-start.4
  119.9 85.9 %collective-permute-done.4 = bf16[12,256,256]{2,1,0:T(8,128)(2,1)} collective-permute-done((bf16[12,256,256]{2,1,0:T(8,128)(2,1)S(1)}, bf16[12,256,256]{2,1,0:T(8,128)(2,1)}, u32[]{:S(2)}, u32[]{:S(2)}) %collective-permute-start.4) | collective-permute-done | bytes 1572896 | tf_op jit(solution)/shard_map/ppermute | solution.py:146
  207.4 1.7 slice.48
  210.4 2.7 collective-permute-start.8
  213.1 6.3 %collective-permute-start.7 = (bf16[28,256,256]{2,1,0:T(8,128)(2,1)}, bf16[28,256,256]{2,1,0:T(8,128)(2,1)}, u32[]{:S(2)}, u32[]{:S(2)}) collective-permute-start(bf16[28,256,256]{2,1,0:T(8,128)(2,1)} %slice.45), channel_id=1, source_target_pairs={{0,1},{3,2},{4,5},{7,6},{8,9},{11,10},{12,13},{15,14},{16,17},{19,... | collective-permute-start | bytes 11010056 | tf_op jit(solution)/shard_map/ppermute | solution.py:146
  219.5 36.7 %collective-permute-done.6.refs_5_ = bf16[16,256,256]{2,1,0:T(8,128)(2,1)S(1)} collective-permute-done((bf16[16,256,256]{2,1,0:T(8,128)(2,1)S(1)}, bf16[16,256,256]{2,1,0:T(8,128)(2,1)S(1)}, u32[]{:S(2)}, u32[]{:S(2)}) %collective-permute-start.6) | collective-permute-done | bytes 2097184 | tf_op jit(solution)/shard_map/ppermute | solution.py:146
  257.5 3.1 slice.49
  261.9 5.5 %collective-permute-start.9 = (bf16[4,256,256]{2,1,0:T(8,128)(2,1)S(1)}, bf16[4,256,256]{2,1,0:T(8,128)(2,1)}, u32[]{:S(2)}, u32[]{:S(2)}) collective-permute-start(bf16[4,256,256]{2,1,0:T(8,128)(2,1)S(1)} %slice.44), channel_id=1, source_target_pairs={{0,1},{3,2},{4,5},{7,6},{8,9},{11,10},{12,13},{15,14},{16,17},{19,... | collective-permute-start | bytes 1572872 | tf_op jit(solution)/shard_map/ppermute | solution.py:146
  267.4 1.8 copy-done.20
  269.3 10.7 %tiles.12.refs_0_ = f32[16,256,256]{2,1,0:T(8,128)S(1)} custom-call(s32[4]{0:T(128)S(1)} %fusion.3.order, s32[1]{0:T(128)} %bitcast.inner, bf16[64,256,256]{2,1,0:T(8,128)(2,1)} %refs_0_.22, bf16[32,256,256]{2,1,0:T(8,128)(2,1)} %collective-permute-done.refs_1_, bf16[32,256,256]{2,1,0:T(8,128)(2,1)} %collective-permute-done.1.refs_2_, ...), custom_call_target="tpu_custom_call" | custom-call | flops 2147483648 | bytes 25165824 | tf_op jit(solution)/shard_map/tiles/pallas_call | solution.py:53
  280.0 25.2 %collective-permute-done.9.refs_1_ = bf16[4,256,256]{2,1,0:T(8,128)(2,1)} collective-permute-done((bf16[4,256,256]{2,1,0:T(8,128)(2,1)S(1)}, bf16[4,256,256]{2,1,0:T(8,128)(2,1)}, u32[]{:S(2)}, u32[]{:S(2)}) %collective-permute-start.9) | collective-permute-done | bytes 524320 | tf_op jit(solution)/shard_map/ppermute | solution.py:146
  305.2 1.9 collective-permute-done.10.refs_5_
  308.7 3.6 fusion.4
  313.1 1.9 slice.53
  317.9 3.4 copy-done.1
  321.3 2.8 copy-done.3
  324.1 2.7 tiles.13
  328.8 3.4 tiles.16.refs_2_
  333.2 3.5 tiles.14
  339.4 8.5 %tiles.15.refs_1_ = f32[16,256,256]{2,1,0:T(8,128)S(1)} custom-call(s32[4]{0:T(128)S(1)} %fusion.3.order, s32[1]{0:T(128)} %bitcast.inner, bf16[64,256,256]{2,1,0:T(8,128)(2,1)} %refs_0_.22, bf16[32,256,256]{2,1,0:T(8,128)(2,1)} %collective-permute-done.refs_1_, bf16[32,256,256]{2,1,0:T(8,128)(2,1)} %collective-permute-done.1.refs_2_, ...), custom_call_target="tpu_custom_call" | custom-call | flops 2147483648 | bytes 25165824 | tf_op jit(solution)/shard_map/tiles/pallas_call | solution.py:53
  347.9 2.0 copy-done.6
  351.1 3.4 copy-done.2
  354.4 4.2 tiles.18
  359.8 2.3 add_multiply_fusion.4.refs_7_
  363.7 7.5 %collective-permute-done.16 = f16[8,256,256]{2,1,0:T(8,128)(2,1)} collective-permute-done((f16[8,256,256]{2,1,0:T(8,128)(2,1)}, f16[8,256,256]{2,1,0:T(8,128)(2,1)}, u32[]{:S(2)}, u32[]{:S(2)}) %collective-permute-start.16) | collective-permute-done | bytes 1048608 | tf_op jit(solution)/shard_map/ppermute | solution.py:146
  371.2 4.2 tiles.20
  375.8 2.8 add_multiply_fusion.2.refs_8_
  380.1 4.2 tiles.17.refs_3_
  384.3 4.2 tiles.19.refs_4_
  388.6 11.9 %collective-permute-done.18 = f16[8,256,256]{2,1,0:T(8,128)(2,1)S(1)} collective-permute-done((f16[8,256,256]{2,1,0:T(8,128)(2,1)S(1)}, f16[8,256,256]{2,1,0:T(8,128)(2,1)S(1)}, u32[]{:S(2)}, u32[]{:S(2)}) %collective-permute-start.18) | collective-permute-done | bytes 1048608 | tf_op jit(solution)/shard_map/ppermute | solution.py:146
  400.4 3.4 tiles.22
  404.8 14.4 %collective-permute-done.19 = f16[8,256,256]{2,1,0:T(8,128)(2,1)S(1)} collective-permute-done((f16[8,256,256]{2,1,0:T(8,128)(2,1)S(1)}, f16[8,256,256]{2,1,0:T(8,128)(2,1)S(1)}, u32[]{:S(2)}, u32[]{:S(2)}) %collective-permute-start.19) | collective-permute-done | bytes 1048608 | tf_op jit(solution)/shard_map/ppermute | solution.py:146
  419.2 1.8 add_multiply_fusion
  422.2 4.2 tiles.21.refs_5_
  427.8 3.6 tiles.23.refs_6_
  435.1 1.6 copy-done.10
  436.7 1.6 copy-done.11
  439.5 9.7 %norm.1 = f32[64,256,256]{2,1,0:T(8,128)} custom-call(s32[1]{0:T(128)} %bitcast.inner, f32[16,256,256]{2,1,0:T(8,128)S(1)} %copy-done.5, f32[16,256,256]{2,1,0:T(8,128)S(1)} %copy-done.7, f32[4,256,256]{2,1,0:T(8,128)S(1)} %copy-done.16, f32[8,256,256]{2,1,0:T(8,128)S(1)} %tiles.17.refs_3_, f32[8,256,256]{2,1,0:T(8,128)S(1)} %tiles.19.refs_4_, ...), custom_call_target="tpu_custom_call" | custom-call | flops 20971520 | bytes 33554432 | tf_op jit(solution)/shard_map/norm/pallas_call | solution.py:108
  (104 shorter events, 32.6 us)
Async XLA Ops:
  6.5 260.9 %all-gather.7.cloned.1.call-start = ((), (), s32[]{:S(2)}) async-start(), calls=%async_computation | async-start | bytes 41943040 | tf_op jit(solution)/shard_map/all_gather | solution.py:147
  7.3 310.6 %all-gather.9.cloned.1.call-start = ((), (), s32[]{:S(2)}) async-start(), calls=%async_computation.1 | async-start | bytes 7864320 | tf_op jit(solution)/shard_map/all_gather | solution.py:147
  7.3 8.4 %copy-start = (bf16[64,256,256]{2,1,0:T(8,128)(2,1)S(1)}, bf16[64,256,256]{2,1,0:T(8,128)(2,1)}, u32[]{:S(2)}) copy-start(bf16[64,256,256]{2,1,0:T(8,128)(2,1)} %refs_0_.22) | copy-start | bytes 25165828
  9.9 93.8 %collective-permute-start = (bf16[32,256,256]{2,1,0:T(8,128)(2,1)S(1)}, bf16[32,256,256]{2,1,0:T(8,128)(2,1)}, u32[]{:S(2)}, u32[]{:S(2)}) collective-permute-start(bf16[32,256,256]{2,1,0:T(8,128)(2,1)S(1)} %slice.42), channel_id=1, source_target_pairs={{0,1},{1,0},{2,3},{3,2},{4,5},{5,4},{6,7},{7,6},{8,9},{9,8},{10,11... | collective-permute-start | bytes 12582920 | tf_op jit(solution)/shard_map/ppermute | solution.py:146
  13.0 90.7 %collective-permute-start.1 = (bf16[32,256,256]{2,1,0:T(8,128)(2,1)S(1)}, bf16[32,256,256]{2,1,0:T(8,128)(2,1)}, u32[]{:S(2)}, u32[]{:S(2)}) collective-permute-start(bf16[32,256,256]{2,1,0:T(8,128)(2,1)S(1)} %slice.42), channel_id=1, source_target_pairs={{1,2},{2,1},{5,6},{6,5},{9,10},{10,9},{13,14},{14,13},{17,18},{18,... | collective-permute-start | bytes 12582920 | tf_op jit(solution)/shard_map/ppermute | solution.py:146
  15.7 4.9 %slice-start.2 = ((s8[8388608]{0:T(1024)(128)(4,1)}), s8[4194304]{0:T(1024)(128)(4,1)S(1)}, s32[]{:S(2)}) async-start(s8[8388608]{0:T(1024)(128)(4,1)} %bitcast.25), calls=%async_computation.5 | async-start | bytes 8388608
  18.2 5.6 %slice-start.3 = ((s8[8388608]{0:T(1024)(128)(4,1)}), s8[4194304]{0:T(1024)(128)(4,1)S(1)}, s32[]{:S(2)}) async-start(s8[8388608]{0:T(1024)(128)(4,1)} %bitcast.25), calls=%async_computation.6 | async-start | bytes 8388608
  103.7 102.1 %collective-permute-start.2 = (bf16[32,256,256]{2,1,0:T(8,128)(2,1)}, bf16[32,256,256]{2,1,0:T(8,128)(2,1)}, u32[]{:S(2)}, u32[]{:S(2)}) collective-permute-start(bf16[32,256,256]{2,1,0:T(8,128)(2,1)} %collective-permute-done.1.refs_2_), channel_id=1, source_target_pairs={{1,0},{2,3},{5,4},{6,7},{9,8},{10,11},{13,12},{14,15},{17,16},{18,... | collective-permute-start | bytes 12582920 | tf_op jit(solution)/shard_map/ppermute | solution.py:146
  105.0 100.8 %collective-permute-start.3 = (bf16[32,256,256]{2,1,0:T(8,128)(2,1)}, bf16[32,256,256]{2,1,0:T(8,128)(2,1)}, u32[]{:S(2)}, u32[]{:S(2)}) collective-permute-start(bf16[32,256,256]{2,1,0:T(8,128)(2,1)} %collective-permute-done.refs_1_), channel_id=1, source_target_pairs={{1,2},{2,1},{5,6},{6,5},{9,10},{10,9},{13,14},{14,13},{17,18},{18,... | collective-permute-start | bytes 12582920 | tf_op jit(solution)/shard_map/ppermute | solution.py:146
  107.7 98.1 %collective-permute-start.5 = (bf16[20,256,256]{2,1,0:T(8,128)(2,1)}, bf16[20,256,256]{2,1,0:T(8,128)(2,1)S(1)}, u32[]{:S(2)}, u32[]{:S(2)}) collective-permute-start(bf16[20,256,256]{2,1,0:T(8,128)(2,1)} %slice.47), channel_id=1, source_target_pairs={{0,1},{3,2},{4,5},{7,6},{8,9},{11,10},{12,13},{15,14},{16,17},{19,... | collective-permute-start | bytes 7864328 | tf_op jit(solution)/shard_map/ppermute | solution.py:146
  117.4 88.4 %collective-permute-start.4 = (bf16[12,256,256]{2,1,0:T(8,128)(2,1)S(1)}, bf16[12,256,256]{2,1,0:T(8,128)(2,1)}, u32[]{:S(2)}, u32[]{:S(2)}) collective-permute-start(bf16[12,256,256]{2,1,0:T(8,128)(2,1)S(1)} %slice.46), channel_id=1, source_target_pairs={{0,1},{3,2},{4,5},{7,6},{8,9},{11,10},{12,13},{15,14},{16,17},{19,... | collective-permute-start | bytes 4718600 | tf_op jit(solution)/shard_map/ppermute | solution.py:146
  205.8 145.2 %all-gather.11.cloned.1.call-start = ((), (), s32[]{:S(2)}) async-start(), calls=%async_computation.2 | async-start | bytes 13107200 | tf_op jit(solution)/shard_map/all_gather | solution.py:147
  209.1 58.3 %copy-start.24 = (s32[4]{0:T(128)S(1)}, s32[4]{0:T(128)}, u32[]{:S(2)}) copy-start(s32[4]{0:T(128)} %constant.7.clone) | copy-start | bytes 52
  209.1 47.1 %collective-permute-start.6 = (bf16[16,256,256]{2,1,0:T(8,128)(2,1)S(1)}, bf16[16,256,256]{2,1,0:T(8,128)(2,1)S(1)}, u32[]{:S(2)}, u32[]{:S(2)}) collective-permute-start(bf16[16,256,256]{2,1,0:T(8,128)(2,1)S(1)} %slice.48), channel_id=1, source_target_pairs={{1,0},{2,3},{5,4},{6,7},{9,8},{10,11},{13,12},{14,15},{17,16},{18,... | collective-permute-start | bytes 6291464 | tf_op jit(solution)/shard_map/ppermute | solution.py:146
  210.4 94.8 %collective-permute-start.8 = (bf16[32,256,256]{2,1,0:T(8,128)(2,1)}, bf16[32,256,256]{2,1,0:T(8,128)(2,1)}, u32[]{:S(2)}, u32[]{:S(2)}) collective-permute-start(bf16[32,256,256]{2,1,0:T(8,128)(2,1)} %slice.43), channel_id=1, source_target_pairs={{1,2},{2,1},{5,6},{6,5},{9,10},{10,9},{13,14},{14,13},{17,18},{18,... | collective-permute-start | bytes 12582920 | tf_op jit(solution)/shard_map/ppermute | solution.py:146
  213.1 92.1 %collective-permute-start.7 = (bf16[28,256,256]{2,1,0:T(8,128)(2,1)}, bf16[28,256,256]{2,1,0:T(8,128)(2,1)}, u32[]{:S(2)}, u32[]{:S(2)}) collective-permute-start(bf16[28,256,256]{2,1,0:T(8,128)(2,1)} %slice.45), channel_id=1, source_target_pairs={{0,1},{3,2},{4,5},{7,6},{8,9},{11,10},{12,13},{15,14},{16,17},{19,... | collective-permute-start | bytes 11010056 | tf_op jit(solution)/shard_map/ppermute | solution.py:146
  260.6 46.5 %collective-permute-start.10 = (bf16[16,256,256]{2,1,0:T(8,128)(2,1)}, bf16[16,256,256]{2,1,0:T(8,128)(2,1)S(1)}, u32[]{:S(2)}, u32[]{:S(2)}) collective-permute-start(bf16[16,256,256]{2,1,0:T(8,128)(2,1)} %slice.49), channel_id=1, source_target_pairs={{1,0},{2,3},{5,4},{6,7},{9,8},{10,11},{13,12},{14,15},{17,16},{18,... | collective-permute-start | bytes 6291464 | tf_op jit(solution)/shard_map/ppermute | solution.py:146
  261.9 43.3 %collective-permute-start.9 = (bf16[4,256,256]{2,1,0:T(8,128)(2,1)S(1)}, bf16[4,256,256]{2,1,0:T(8,128)(2,1)}, u32[]{:S(2)}, u32[]{:S(2)}) collective-permute-start(bf16[4,256,256]{2,1,0:T(8,128)(2,1)S(1)} %slice.44), channel_id=1, source_target_pairs={{0,1},{3,2},{4,5},{7,6},{8,9},{11,10},{12,13},{15,14},{16,17},{19,... | collective-permute-start | bytes 1572872 | tf_op jit(solution)/shard_map/ppermute | solution.py:146
  267.4 1.8 copy-start.20
  280.0 32.3 %copy-start.4 = (f32[16,256,256]{2,1,0:T(8,128)}, f32[16,256,256]{2,1,0:T(8,128)S(1)}, u32[]{:S(2)}) copy-start(f32[16,256,256]{2,1,0:T(8,128)S(1)} %tiles.12.refs_0_) | copy-start | bytes 12582916
  307.1 5.2 %copy-start.17 = (bf16[16,256,256]{2,1,0:T(8,128)(2,1)}, bf16[16,256,256]{2,1,0:T(8,128)(2,1)S(1)}, u32[]{:S(2)}) copy-start(bf16[16,256,256]{2,1,0:T(8,128)(2,1)S(1)} %collective-permute-done.10.refs_5_) | copy-start | bytes 6291460
  307.1 10.8 %collective-permute-start.12 = (bf16[4,256,256]{2,1,0:T(8,128)(2,1)}, bf16[4,256,256]{2,1,0:T(8,128)(2,1)}, u32[]{:S(2)}, u32[]{:S(2)}) collective-permute-start(bf16[4,256,256]{2,1,0:T(8,128)(2,1)} %collective-permute-done.9.refs_1_), channel_id=1, source_target_pairs={{1,2},{2,1},{5,6},{6,5},{9,10},{10,9},{13,14},{14,13},{17,18},{18,... | collective-permute-start | bytes 1572872 | tf_op jit(solution)/shard_map/ppermute | solution.py:146
  312.3 20.9 %collective-permute-start.11 = (bf16[8,256,256]{2,1,0:T(8,128)(2,1)}, bf16[8,256,256]{2,1,0:T(8,128)(2,1)S(1)}, u32[]{:S(2)}, u32[]{:S(2)}) collective-permute-start(bf16[8,256,256]{2,1,0:T(8,128)(2,1)} %get-tuple-element.73), channel_id=1, source_target_pairs={{1,2},{2,1},{5,6},{6,5},{9,10},{10,9},{13,14},{14,13},{17,18},{18,... | collective-permute-start | bytes 3145736 | tf_op jit(solution)/shard_map/ppermute | solution.py:146
  314.9 35.0 %collective-permute-start.13 = (bf16[8,256,256]{2,1,0:T(8,128)(2,1)}, bf16[8,256,256]{2,1,0:T(8,128)(2,1)S(1)}, u32[]{:S(2)}, u32[]{:S(2)}) collective-permute-start(bf16[8,256,256]{2,1,0:T(8,128)(2,1)} %get-tuple-element.72), channel_id=1, source_target_pairs={{1,2},{2,1},{5,6},{6,5},{9,10},{10,9},{13,14},{14,13},{17,18},{18,... | collective-permute-start | bytes 3145736 | tf_op jit(solution)/shard_map/ppermute | solution.py:146
  315.7 48.0 %collective-permute-start.15 = (bf16[8,256,256]{2,1,0:T(8,128)(2,1)}, bf16[8,256,256]{2,1,0:T(8,128)(2,1)S(1)}, u32[]{:S(2)}, u32[]{:S(2)}) collective-permute-start(bf16[8,256,256]{2,1,0:T(8,128)(2,1)} %get-tuple-element.71), channel_id=1, source_target_pairs={{1,2},{2,1},{5,6},{6,5},{9,10},{10,9},{13,14},{14,13},{17,18},{18,... | collective-permute-start | bytes 3145736 | tf_op jit(solution)/shard_map/ppermute | solution.py:146
  316.4 72.2 %collective-permute-start.17 = (bf16[4,256,256]{2,1,0:T(8,128)(2,1)}, bf16[4,256,256]{2,1,0:T(8,128)(2,1)}, u32[]{:S(2)}, u32[]{:S(2)}) collective-permute-start(bf16[4,256,256]{2,1,0:T(8,128)(2,1)} %slice.53), channel_id=1, source_target_pairs={{1,2},{2,1},{5,6},{6,5},{9,10},{10,9},{13,14},{14,13},{17,18},{18,... | collective-permute-start | bytes 1572872 | tf_op jit(solution)/shard_map/ppermute | solution.py:146
  317.9 3.4 copy-start.1
  321.3 2.8 copy-start.3
  327.1 6.1 %slice-start = ((s8[6291456]{0:T(1024)(128)(4,1)}), s8[4194304]{0:T(1024)(128)(4,1)S(1)}, s32[]{:S(2)}) async-start(s8[6291456]{0:T(1024)(128)(4,1)} %bitcast.12), calls=%async_computation.3 | async-start | bytes 8388608
  327.3 5.9 %slice-start.1 = ((s8[6291456]{0:T(1024)(128)(4,1)}), s8[2097152]{0:T(1024)(128)(4,1)S(1)}, s32[]{:S(2)}) async-start(s8[6291456]{0:T(1024)(128)(4,1)} %bitcast.12), calls=%async_computation.4 | async-start | bytes 4194304
  327.3 23.8 %collective-permute-start.14 = (f16[5,256,256]{2,1,0:T(8,128)(2,1)S(1)}, f16[5,256,256]{2,1,0:T(8,128)(2,1)}, u32[]{:S(2)}, u32[]{:S(2)}) collective-permute-start(f16[5,256,256]{2,1,0:T(8,128)(2,1)S(1)} %pad_maximum_fusion), channel_id=1, source_target_pairs={{1,0},{2,3},{5,4},{6,7},{9,8},{10,11},{13,12},{14,15},{17,16},{18,... | collective-permute-start | bytes 1966088 | tf_op jit(solution)/shard_map/ppermute | solution.py:146
  336.9 2.5 copy-start.18
  338.1 33.0 %collective-permute-start.16 = (f16[8,256,256]{2,1,0:T(8,128)(2,1)}, f16[8,256,256]{2,1,0:T(8,128)(2,1)}, u32[]{:S(2)}, u32[]{:S(2)}) collective-permute-start(f16[8,256,256]{2,1,0:T(8,128)(2,1)} %subtract_convert_fusion.2), channel_id=1, source_target_pairs={{1,0},{2,3},{5,4},{6,7},{9,8},{10,11},{13,12},{14,15},{17,16},{18,... | collective-permute-start | bytes 3145736 | tf_op jit(solution)/shard_map/ppermute | solution.py:146
  347.9 2.0 copy-start.6
  351.1 3.4 copy-start.2
  359.8 59.4 %copy-start.21 = (f32[256,256]{1,0:T(8,128)}, f32[256,256]{1,0:T(8,128)S(1)}, u32[]{:S(2)}) copy-start(f32[256,256]{1,0:T(8,128)S(1)} %fusion) | copy-start | bytes 786436
  362.3 38.1 %collective-permute-start.18 = (f16[8,256,256]{2,1,0:T(8,128)(2,1)S(1)}, f16[8,256,256]{2,1,0:T(8,128)(2,1)S(1)}, u32[]{:S(2)}, u32[]{:S(2)}) collective-permute-start(f16[8,256,256]{2,1,0:T(8,128)(2,1)S(1)} %subtract_convert_fusion.1), channel_id=1, source_target_pairs={{1,0},{2,3},{5,4},{6,7},{9,8},{10,11},{13,12},{14,15},{17,16},{18,... | collective-permute-start | bytes 3145736 | tf_op jit(solution)/shard_map/ppermute | solution.py:146
  363.6 11.7 %copy-start.12 = (bf16[8,256,256]{2,1,0:T(8,128)(2,1)}, bf16[8,256,256]{2,1,0:T(8,128)(2,1)S(1)}, u32[]{:S(2)}) copy-start(bf16[8,256,256]{2,1,0:T(8,128)(2,1)S(1)} %collective-permute-done.15.refs_3_) | copy-start | bytes 3145732
  378.6 40.5 %collective-permute-start.19 = (f16[8,256,256]{2,1,0:T(8,128)(2,1)S(1)}, f16[8,256,256]{2,1,0:T(8,128)(2,1)S(1)}, u32[]{:S(2)}, u32[]{:S(2)}) collective-permute-start(f16[8,256,256]{2,1,0:T(8,128)(2,1)S(1)} %subtract_convert_fusion), channel_id=1, source_target_pairs={{1,0},{2,3},{5,4},{6,7},{9,8},{10,11},{13,12},{14,15},{17,16},{18,... | collective-permute-start | bytes 3145736 | tf_op jit(solution)/shard_map/ppermute | solution.py:146
  404.8 17.4 %copy-start.13 = (bf16[8,256,256]{2,1,0:T(8,128)(2,1)S(1)}, bf16[8,256,256]{2,1,0:T(8,128)(2,1)}, u32[]{:S(2)}) copy-start(bf16[8,256,256]{2,1,0:T(8,128)(2,1)} %copy-done.12) | copy-start | bytes 3145732
  420.9 11.4 %collective-permute-start.20 = (f16[4,256,256]{2,1,0:T(8,128)(2,1)}, f16[4,256,256]{2,1,0:T(8,128)(2,1)}, u32[]{:S(2)}, u32[]{:S(2)}) collective-permute-start(f16[4,256,256]{2,1,0:T(8,128)(2,1)} %subtract_convert_fusion.3), channel_id=1, source_target_pairs={{1,0},{2,3},{5,4},{6,7},{9,8},{10,11},{13,12},{14,15},{17,16},{18,... | collective-permute-start | bytes 1572872 | tf_op jit(solution)/shard_map/ppermute | solution.py:146
  427.8 4.5 copy-start.22
  427.8 5.6 %copy-start.5 = (f32[16,256,256]{2,1,0:T(8,128)S(1)}, f32[16,256,256]{2,1,0:T(8,128)}, u32[]{:S(2)}) copy-start(f32[16,256,256]{2,1,0:T(8,128)} %copy-done.4) | copy-start | bytes 12582916
  427.8 5.7 %copy-start.7 = (f32[16,256,256]{2,1,0:T(8,128)S(1)}, f32[16,256,256]{2,1,0:T(8,128)}, u32[]{:S(2)}) copy-start(f32[16,256,256]{2,1,0:T(8,128)} %copy-done.6) | copy-start | bytes 12582916
  431.5 2.0 copy-start.14
  433.5 1.6 copy-start.8
  435.1 1.6 copy-start.10
  436.7 1.6 copy-start.11
  (5 other events, 6.4 us)
Sparse Core Ops, SparseCore 0:
  8.9 204.2 all-gather.6
  214.7 46.3 all-gather.8
  262.7 70.1 all-gather.10

commit v3 on v2

v3 whole, which is shorter than its diff:
```python
import functools

import jax
import jax.numpy as jnp
from jax import lax
from jax.experimental import pallas as pl
from jax.experimental.pallas import tpu as pltpu
from jax.sharding import PartitionSpec as P

EPS = 1e-5
HALF_SCALE = 16.0


def gathered(left_proj, right_proj):
    full_left = lax.all_gather(left_proj, "col", axis=2, tiled=True)
    full_right = lax.all_gather(right_proj, "row", axis=2, tiled=True)
    triangle = jnp.einsum("cik,cjk->cij", full_left, full_right, preferred_element_type=jnp.float32)
    channel_mean = jnp.mean(triangle, axis=0, keepdims=True)
    centered = triangle - channel_mean
    channel_var = jnp.mean(centered * centered, axis=0, keepdims=True)
    return centered / jnp.sqrt(channel_var + EPS)


def dot_nt(a, b):
    return lax.dot_general(a, b, (((1,), (1,)), ((), ())), preferred_element_type=jnp.float32)


def params(limit):
    return pltpu.CompilerParams(vmem_limit_bytes=limit * 1024 * 1024, dimension_semantics=("arbitrary",))


def tiles_kernel(step, scale, groups, order, inner, *refs):
    *lefts, right, out = refs
    for c in range(step):
        acc, at = None, 0
        for turn, begins in enumerate(groups):
            one = lefts[at][c]
            for k, begin in enumerate(begins[1:], 1):
                other = inner[0] != 1 if begin is None else pl.program_id(0) >= begin
                one = jnp.where(other, lefts[at + k][c], one)
            at += len(begins)
            term = dot_nt(one, right[order[turn], c])
            acc = term if acc is None else acc + term
        out[c] = acc if scale == 1.0 else acc * scale


def tiles(order, inner, lefts, right, right_at, n, scale=1.0):
    step = 4
    arrays, specs, groups = [], [], []
    rows, depth = lefts[0][0][0].shape[1:]
    cols = right.shape[2]

    def block(index):
        specs.append(pl.BlockSpec((step, rows, depth), lambda c, order, inner: (index(c, inner[0]), 0, 0)))

    for group in lefts:
        if isinstance(group[0], tuple):
            (array, at), *outer = group
            arrays.append(array)
            if not outer:
                block(lambda c, flag, at=at // step: at + c)
            else:
                arrays.append(outer[0][0])
                block(lambda c, flag, at=at // step: at + c * flag)
                block(lambda c, flag, at=outer[0][1] // step: at + c * (1 - flag))
            groups.append((0, None)[: len(group)])
        else:
            begins, begin = [], 0
            for array in group:
                count = array.shape[0] // step
                block(lambda c, flag, begin=begin, count=count: jnp.clip(c - begin, 0, count - 1))
                arrays.append(array)
                begins.append(begin)
                begin += count
            groups.append(tuple(begins))
    specs.append(pl.BlockSpec((4, step, cols, depth), lambda c, *_: (0, right_at // step + c, 0, 0)))
    return pl.pallas_call(
        functools.partial(tiles_kernel, step, scale, tuple(groups)),
        grid_spec=pltpu.PrefetchScalarGridSpec(
            num_scalar_prefetch=2,
            grid=(n // step,),
            in_specs=specs,
            out_specs=pl.BlockSpec((step, rows, cols), lambda c, *_: (c, 0, 0)),
        ),
        out_shape=jax.ShapeDtypeStruct((n, rows, cols), jnp.float32),
        compiler_params=params(32),
        cost_estimate=pl.CostEstimate(
            flops=8 * n * rows * cols * depth,
            bytes_accessed=n * (4 * (rows + cols) * depth * 2 + rows * cols * 4),
            transcendentals=0,
        ),
        name="tiles",
    )(order, inner, *arrays, right)


def norm_kernel(both, mine, inner, offset, first, second, *refs):
    *refs, out = refs
    shared, own, sent = refs[:both], refs[both : both + mine], refs[both + mine :]
    share = 1.0 / out.shape[0]

    def write(parts):
        sums, squares = first[...], second[...]
        for part in parts:
            for c in range(part.shape[0]):
                apart = part[c] - offset[...]
                sums += apart
                squares += apart * apart
        shift = sums * share
        channel_var = jnp.maximum(squares * share - shift * shift, 0.0)
        channel_mean = offset[...] + shift
        factor = 1.0 / jnp.sqrt(channel_var + EPS)
        at = 0
        for part in [*shared, *parts]:
            for c in range(part.shape[0]):
                out[at + c] = (part[c] - channel_mean) * factor
            at += part.shape[0]

    @pl.when(inner[0] == 1)
    def _():
        write(own)

    @pl.when(inner[0] != 1)
    def _():
        write(sent)


def norm(inner, stats, shared, own, sent):
    rows, cols = shared[0].shape[1:]
    channels = sum(part.shape[0] for part in [*shared, *own])
    step = 32
    spec = lambda part, used: pl.BlockSpec((part.shape[0], step, cols), lambda i, inner: (0, i * used(inner[0]), 0))
    specs = [pl.BlockSpec((step, cols), lambda i, inner: (i, 0)) for _ in stats]
    specs += [spec(part, lambda flag: 1) for part in shared]
    specs += [spec(part, lambda flag: flag) for part in own]
    specs += [spec(part, lambda flag: 1 - flag) for part in sent]
    size = channels * rows * cols
    return pl.pallas_call(
        functools.partial(norm_kernel, len(shared), len(own)),
        grid_spec=pltpu.PrefetchScalarGridSpec(
            num_scalar_prefetch=1,
            grid=(rows // step,),
            in_specs=specs,
            out_specs=pl.BlockSpec((channels, step, cols), lambda i, inner: (0, i, 0)),
        ),
        out_shape=jax.ShapeDtypeStruct((channels, rows, cols), jnp.float32),
        compiler_params=params(44),
        cost_estimate=pl.CostEstimate(flops=5 * size, bytes_accessed=8 * size, transcendentals=0),
        name="norm",
    )(inner, *stats, *shared, *own, *sent)


SWAP = [(0, 1), (1, 0), (2, 3), (3, 2)]
INWARD = [(0, 1), (3, 2)]
OUTWARD = [(1, 0), (2, 3)]
MIDDLE = [(1, 2), (2, 1)]


def after(block, *done):
    return lax.optimization_barrier((block, *done))[0] if done else block


def line(left, right):
    col = lax.axis_index("col")
    is_inner = (col == 1) | (col == 2)
    inner = is_inner.astype(jnp.int32).reshape(1)
    order = (col ^ jnp.where(is_inner, jnp.array([0, 1, 3, 2], jnp.int32), jnp.array([0, 1, 2, 3], jnp.int32))).astype(jnp.int32)
    unit = left.shape[0] // 16
    near_n, far_n = 8 * unit, 8 * unit
    near_sizes, sizes = [4 * unit, 4 * unit], [2 * unit] * 4

    cut = lambda array, at, n: lax.slice_in_dim(array, at, at + n, axis=0)
    pieces = lambda array, at, counts: [cut(array, at + sum(counts[:k]), n) for k, n in enumerate(counts)]
    go = lambda block, pairs: lax.ppermute(block, "col", pairs)
    rows_of = lambda block: lax.all_gather(block, "row", axis=0, tiled=False)

    right_own = rows_of(right)
    first = cut(left, 0, near_n)
    e_n, p2_n = go(first, SWAP), go(first, MIDDLE)
    left_on = after(left, first)
    second, *split = cut(left_on, near_n, far_n), *pieces(left_on, near_n, [sizes[0], far_n - sizes[0]])
    third = cut(after(right, first), near_n, far_n)
    ended = (e_n, second, *split, third)

    p3_n = go(after(e_n, *ended), MIDDLE)
    r_f = go(after(third, *ended, p2_n), INWARD)
    q2_n = go(after(p2_n, *ended), OUTWARD)
    ended = (p3_n, q2_n)

    right_f = rows_of(after(r_f, *ended))
    p2_f = go(after(second, *ended), MIDDLE)
    e_f = [go(after(split[0], *ended), INWARD)]
    e_f.append(go(after(split[1], *ended, e_f[0]), INWARD))
    q3_na = go(cut(after(p3_n, *ended), 0, near_sizes[0]), OUTWARD)
    q3_nb = go(cut(after(p3_n, *ended, q3_na, right_own), *near_sizes), OUTWARD)

    def near(at, q3, n, *done):
        blocks = [[(after(left, *done), at)], [(e_n, at)], [(p2_n, at), (q2_n, at)], [(p3_n, at), (q3, 0)]]
        return tiles(order, inner, blocks, right_own, at, n)

    def stats_of(offset, block, first, second):
        apart = block - offset
        return first + jnp.sum(apart, axis=0), second + jnp.sum(apart * apart, axis=0)

    near_a = near(0, q3_na, near_sizes[0])
    offset = jnp.mean(near_a, axis=0)
    there = (offset * HALF_SCALE).astype(jnp.float16)
    here = go(there, INWARD)
    stats = stats_of(offset, near_a, 0.0, 0.0)
    p3 = [go(after(e_f[0], there), MIDDLE)]
    ended = (p2_f, *e_f)
    p3 += [go(block, MIDDLE) for block in pieces(after(e_f[1], *ended), 0, sizes[1:])]
    sent, payloads, returned, at = [], [], [], 0
    for j, n in enumerate(sizes):
        waits = [*payloads[-1:], *returned[: max(j - 1, 0)], *([near_b] if j == 1 else []), *([q3_nb] if j == 0 else [])]
        blocks = [[(second, at)], [(e_f[1], at - sizes[0]) if j else (e_f[0], 0)], [(p2_f, at)], [(after(p3[j], *waits), 0)]]
        tile = tiles(order, inner, blocks, right_f, at, n, HALF_SCALE)
        payload = (tile - here.astype(jnp.float32)).astype(jnp.float16)
        payloads.append(payload)
        if j == 0:
            near_b = near(near_sizes[0], q3_nb, near_sizes[1], payload)
            stats = stats_of(offset, near_b, *stats)
        ties = [(), (near_b, *returned), (*stats, *returned[1:]), returned[2:]][j]
        arrived = go(after(payload, *ties), OUTWARD)
        returned.append(arrived)
        back = after(arrived, *sent[-1:])
        sent.append((back.astype(jnp.float32) + there.astype(jnp.float32)) * (1.0 / HALF_SCALE))
        at += n
    own = tiles(order, inner, [[(after(second, payloads[-1]), 0)], e_f, [(p2_f, 0)], p3], right_own, near_n, far_n)
    return norm(inner, (offset, *stats), [near_a, near_b], [own], sent)


def solution(mesh):
    placed = (P("ens", "row", "col"), P("ens", "col", "row"))
    per_device = line if mesh.shape["col"] == 4 and mesh.shape["row"] == 4 else gathered
    return jax.shard_map(
        per_device, mesh=mesh, in_specs=placed, out_specs=P("ens", "row", "col"), check_vma=False
    )
```

time: 457 us -> 449 us (0.982)
  Pallas kernels: 66.5 us -> 59.4 us
    pallas_call x12 -> x7, Pallas kernels: 56.8 us -> 47.9 us  [tiles(): pl.pallas_call(functools.partial(tiles_kernel, step, scale, tuple(groups)...]
    mul x8 -> x4, other arithmetic: 8.66 us -> 0.91 us  [line(): (back.astype(jnp.float32) + there.astype(jnp.float32)) * (1.0 / HALF_SCALE)]
    ppermute x21 -> x19, waiting for transfers between devices: 264 us -> 261 us  [line(): go = lambda block, pairs: lax.ppermute(block, 'col', pairs)]
    slice x10 -> x8, local copies, waits for them, and re-layouts: 19.7 us -> 20.7 us  [line(): cut = lambda array, at, n: lax.slice_in_dim(array, at, at + n, axis=0)]
    unnamed x58 -> x56, local copies, waits for them, and re-layouts: 27.7 us -> 27.1 us
    ppermute x21 -> x19, starting transfers between devices: 51.1 us -> 50.6 us  [line(): go = lambda block, pairs: lax.ppermute(block, 'col', pairs)]
  transfers between devices with their start and end apart: 24 -> 21, of which waited for: 10 -> 12; matrix products, arithmetic and copies ran while one was open for 6% -> 7% of each run, Pallas kernels for 12% -> 11%
where the time goes in v3:
time: 449 us; the launch traced here: 445 us
  waiting for transfers between devices  265 us (59%)
  Pallas kernels  59.4 us (13%)
  starting transfers between devices  50.7 us (11%)
  local copies, waits for them, and re-layouts  47.7 us (11%)
  between operations  13.9 us (3%)
  other arithmetic  8.93 us (2%)
    ppermute x19, waiting for transfers between devices, line(): go = lambda block, pairs: lax.ppermute(block, 'col', pairs)  261 us
    ppermute x19, starting transfers between devices, line(): go = lambda block, pairs: lax.ppermute(block, 'col', pairs)  50.6 us
    pallas_call x7, Pallas kernels, tiles(): pl.pallas_call(functools.partial(tiles_kernel, step, scale, tuple(groups)...  47.9 us
    unnamed x56, local copies, waits for them, and re-layouts  27.1 us
    slice x8, local copies, waits for them, and re-layouts, line(): cut = lambda array, at, n: lax.slice_in_dim(array, at, at + n, axis=0)  20.7 us
    pallas_call x1, Pallas kernels, norm(): pl.pallas_call(functools.partial(norm_kernel, len(shared), len(own)), gri...  11.5 us
  transfers between devices with their start and end apart: 21, of which 12 were waited for; matrix products, arithmetic and copies ran while one was open for 7% of the time, Pallas kernels for 11%

profile of v3, /device:TPU:0, one launch (start us, length us, event | category | flops | bytes accessed | tf_op | source)
XLA Modules:
  0.0 445.4 jit_solution(3063317605784899695)
XLA Ops:
  7.3 4.9 %slice.30 = bf16[32,256,256]{2,1,0:T(8,128)(2,1)} slice(bf16[64,256,256]{2,1,0:T(8,128)(2,1)} %refs_0_.2), slice={[0:32], [0:256], [0:256]} | slice | bytes 8388608 | tf_op jit(solution)/shard_map/slice | solution.py:171
  12.2 3.0 collective-permute-start
  16.2 6.6 %slice.31.refs_0_ = bf16[32,256,256]{2,1,0:T(8,128)(2,1)} slice(bf16[64,256,256]{2,1,0:T(8,128)(2,1)} %refs_0_.2), slice={[32:64], [0:256], [0:256]} | slice | bytes 8388608 | tf_op jit(solution)/shard_map/slice | solution.py:171
  22.8 2.1 slice.33
  25.4 80.6 %collective-permute-done.refs_1_ = bf16[32,256,256]{2,1,0:T(8,128)(2,1)S(1)} collective-permute-done((bf16[32,256,256]{2,1,0:T(8,128)(2,1)}, bf16[32,256,256]{2,1,0:T(8,128)(2,1)S(1)}, u32[]{:S(2)}, u32[]{:S(2)}) %collective-permute-start) | collective-permute-done | bytes 4194336 | tf_op jit(solution)/shard_map/ppermute | solution.py:173
  107.4 2.0 copy-done.8
  110.3 2.0 copy-done.5
  112.3 12.0 %collective-permute-start.9 = (bf16[32,256,256]{2,1,0:T(8,128)(2,1)S(1)}, bf16[32,256,256]{2,1,0:T(8,128)(2,1)}, u32[]{:S(2)}, u32[]{:S(2)}) collective-permute-start(bf16[32,256,256]{2,1,0:T(8,128)(2,1)S(1)} %slice.34), channel_id=1, source_target_pairs={{0,1},{3,2},{4,5},{7,6},{8,9},{11,10},{12,13},{15,14},{16,17},{19,... | collective-permute-start | bytes 12582920 | tf_op jit(solution)/shard_map/ppermute | solution.py:173
  124.2 77.9 %collective-permute-done.2.refs_3_ = bf16[32,256,256]{2,1,0:T(8,128)(2,1)S(1)} collective-permute-done((bf16[32,256,256]{2,1,0:T(8,128)(2,1)S(1)}, bf16[32,256,256]{2,1,0:T(8,128)(2,1)S(1)}, u32[]{:S(2)}, u32[]{:S(2)}) %collective-permute-start.2) | collective-permute-done | bytes 4194336 | tf_op jit(solution)/shard_map/ppermute | solution.py:173
  202.1 2.0 copy-done.11
  204.1 2.0 copy-done.19
  206.1 4.5 %collective-permute-done.9 = bf16[32,256,256]{2,1,0:T(8,128)(2,1)} collective-permute-done((bf16[32,256,256]{2,1,0:T(8,128)(2,1)S(1)}, bf16[32,256,256]{2,1,0:T(8,128)(2,1)}, u32[]{:S(2)}, u32[]{:S(2)}) %collective-permute-start.9) | collective-permute-done | bytes 4194336 | tf_op jit(solution)/shard_map/ppermute | solution.py:173
  210.6 5.5 %collective-permute-start.5 = (bf16[8,256,256]{2,1,0:T(8,128)(2,1)S(1)}, bf16[8,256,256]{2,1,0:T(8,128)(2,1)}, u32[]{:S(2)}, u32[]{:S(2)}) collective-permute-start(bf16[8,256,256]{2,1,0:T(8,128)(2,1)S(1)} %slice.32), channel_id=1, source_target_pairs={{0,1},{3,2},{4,5},{7,6},{8,9},{11,10},{12,13},{15,14},{16,17},{19,... | collective-permute-start | bytes 3145736 | tf_op jit(solution)/shard_map/ppermute | solution.py:173
  216.1 2.7 collective-permute-start.6
  218.8 1.7 slice.35
  220.6 1.3 collective-permute-start.4
  221.9 13.4 %collective-permute-done.5.refs_1_ = bf16[8,256,256]{2,1,0:T(8,128)(2,1)} collective-permute-done((bf16[8,256,256]{2,1,0:T(8,128)(2,1)S(1)}, bf16[8,256,256]{2,1,0:T(8,128)(2,1)}, u32[]{:S(2)}, u32[]{:S(2)}) %collective-permute-start.5) | collective-permute-done | bytes 1048608 | tf_op jit(solution)/shard_map/ppermute | solution.py:173
  235.2 4.7 %collective-permute-start.11 = (bf16[24,256,256]{2,1,0:T(8,128)(2,1)}, bf16[24,256,256]{2,1,0:T(8,128)(2,1)S(1)}, u32[]{:S(2)}, u32[]{:S(2)}) collective-permute-start(bf16[24,256,256]{2,1,0:T(8,128)(2,1)} %slice.33), channel_id=1, source_target_pairs={{0,1},{3,2},{4,5},{7,6},{8,9},{11,10},{12,13},{15,14},{16,17},{19,... | collective-permute-start | bytes 9437192 | tf_op jit(solution)/shard_map/ppermute | solution.py:173
  239.9 27.3 %collective-permute-done.4.refs_5_ = bf16[16,256,256]{2,1,0:T(8,128)(2,1)S(1)} collective-permute-done((bf16[16,256,256]{2,1,0:T(8,128)(2,1)S(1)}, bf16[16,256,256]{2,1,0:T(8,128)(2,1)S(1)}, u32[]{:S(2)}, u32[]{:S(2)}) %collective-permute-start.4) | collective-permute-done | bytes 2097184 | tf_op jit(solution)/shard_map/ppermute | solution.py:173
  267.3 1.4 copy-done.17
  268.6 3.1 slice.36
  273.0 2.2 copy-done.6
  275.3 2.2 copy-done.9
  277.5 2.2 copy-done.12
  279.6 1.6 copy-done.18
  281.2 6.9 %tiles.7.refs_0_ = f32[16,256,256]{2,1,0:T(8,128)S(1)} custom-call(s32[4]{0:T(128)S(1)} %fusion.order, s32[1]{0:T(128)} %bitcast.inner, bf16[64,256,256]{2,1,0:T(8,128)(2,1)} %refs_0_.2, bf16[32,256,256]{2,1,0:T(8,128)(2,1)S(1)} %copy-done.6, bf16[32,256,256]{2,1,0:T(8,128)(2,1)S(1)} %copy-done.9, bf16[32,256,256]{2,1,0:T(8,128)(2,1)S(1)} %copy-done.12, ...), custom_call_target="tpu_custom_call" | custom-call | flops 2147483648 | bytes 20971520 | tf_op jit(solution)/shard_map/tiles/pallas_call | solution.py:77
  288.2 2.0 copy-done.2
  290.1 3.2 reduce_sum.45
  293.3 1.8 fusion.1
  295.9 8.3 %collective-permute-done.11.refs_1_.refs_2_ = bf16[24,256,256]{2,1,0:T(8,128)(2,1)S(1)} collective-permute-done((bf16[24,256,256]{2,1,0:T(8,128)(2,1)}, bf16[24,256,256]{2,1,0:T(8,128)(2,1)S(1)}, u32[]{:S(2)}, u32[]{:S(2)}) %collective-permute-start.11) | collective-permute-done | bytes 3145760 | tf_op jit(solution)/shard_map/ppermute | solution.py:173
  304.2 8.0 %collective-permute-start.10 = (f16[256,256]{1,0:T(8,128)(2,1)S(1)}, f16[256,256]{1,0:T(8,128)(2,1)S(1)}, u32[]{:S(2)}, u32[]{:S(2)}) collective-permute-start(f16[256,256]{1,0:T(8,128)(2,1)S(1)} %get-tuple-element.62), channel_id=1, source_target_pairs={{0,1},{3,2},{4,5},{7,6},{8,9},{11,10},{12,13},{15,14},{16,17},{19,... | collective-permute-start | bytes 393224 | tf_op jit(solution)/shard_map/ppermute | solution.py:173
  312.2 1.8 fusion.2
  313.9 1.6 collective-permute-start.14
  317.9 2.8 all-gather.7.cloned.1.call-done
  320.7 2.2 copy-done
  324.1 4.4 tiles.8
  328.8 1.3 collective-permute-start.15
  330.9 2.2 copy-done.10
  333.1 7.5 %tiles.9.refs_1_ = f32[16,256,256]{2,1,0:T(8,128)S(1)} custom-call(s32[4]{0:T(128)S(1)} %fusion.order, s32[1]{0:T(128)} %bitcast.inner, bf16[64,256,256]{2,1,0:T(8,128)(2,1)} %refs_0_.2, bf16[32,256,256]{2,1,0:T(8,128)(2,1)S(1)} %copy-done.7, bf16[32,256,256]{2,1,0:T(8,128)(2,1)S(1)} %copy-done.10, bf16[32,256,256]{2,1,0:T(8,128)(2,1)S(1)} %copy-done.13, ...), custom_call_target="tpu_custom_call" | custom-call | flops 2147483648 | bytes 20971520 | tf_op jit(solution)/shard_map/tiles/pallas_call | solution.py:77
  340.7 6.0 %tiles.10 = f32[8,256,256]{2,1,0:T(8,128)S(1)} custom-call(s32[4]{0:T(128)S(1)} %fusion.order, s32[1]{0:T(128)} %bitcast.inner, bf16[32,256,256]{2,1,0:T(8,128)(2,1)S(1)} %copy-done.1, bf16[24,256,256]{2,1,0:T(8,128)(2,1)S(1)} %collective-permute-done.11.refs_1_.refs_2_, bf16[32,256,256]{2,1,0:T(8,128)(2,1)} %collective-permute-done.6.refs_2_.refs_3_, ...), custom_call_target="tpu_custom_call" | custom-call | flops 1073741824 | bytes 10485760 | tf_op jit(solution)/shard_map/tiles/pallas_call | solution.py:77
  346.9 14.5 %collective-permute-done.15 = f16[8,256,256]{2,1,0:T(8,128)(2,1)S(1)} collective-permute-done((f16[8,256,256]{2,1,0:T(8,128)(2,1)S(1)}, f16[8,256,256]{2,1,0:T(8,128)(2,1)S(1)}, u32[]{:S(2)}, u32[]{:S(2)}) %collective-permute-start.15) | collective-permute-done | bytes 1048608 | tf_op jit(solution)/shard_map/ppermute | solution.py:173
  364.8 3.9 tiles.11
  368.9 15.8 %collective-permute-done.16 = f16[8,256,256]{2,1,0:T(8,128)(2,1)S(1)} collective-permute-done((f16[8,256,256]{2,1,0:T(8,128)(2,1)S(1)}, f16[8,256,256]{2,1,0:T(8,128)(2,1)S(1)}, u32[]{:S(2)}, u32[]{:S(2)}) %collective-permute-start.16) | collective-permute-done | bytes 1048608 | tf_op jit(solution)/shard_map/ppermute | solution.py:173
  384.8 1.5 collective-permute-start.17
  386.2 3.9 tiles.12
  390.4 17.7 %collective-permute-done.17 = f16[8,256,256]{2,1,0:T(8,128)(2,1)S(1)} collective-permute-done((f16[8,256,256]{2,1,0:T(8,128)(2,1)S(1)}, f16[8,256,256]{2,1,0:T(8,128)(2,1)S(1)}, u32[]{:S(2)}, u32[]{:S(2)}) %collective-permute-start.17) | collective-permute-done | bytes 1048608 | tf_op jit(solution)/shard_map/ppermute | solution.py:173
  410.9 15.3 %tiles.13.refs_2_ = f32[32,256,256]{2,1,0:T(8,128)} custom-call(s32[4]{0:T(128)S(1)} %fusion.order, s32[1]{0:T(128)} %bitcast.inner, bf16[32,256,256]{2,1,0:T(8,128)(2,1)S(1)} %copy-done.1, bf16[8,256,256]{2,1,0:T(8,128)(2,1)} %collective-permute-done.5.refs_1_, bf16[24,256,256]{2,1,0:T(8,128)(2,1)S(1)} %collective-permute-done.11.refs_1_.refs_2_, ...), custom_call_target="tpu_custom_call" | custom-call | flops 4294967296 | bytes 41943040 | tf_op jit(solution)/shard_map/tiles/pallas_call | solution.py:77
  427.1 11.5 %norm.1 = f32[64,256,256]{2,1,0:T(8,128)} custom-call(s32[1]{0:T(128)} %bitcast.inner, f32[256,256]{1,0:T(8,128)S(1)} %get-tuple-element.66.offset, f32[256,256]{1,0:T(8,128)S(1)} %add.14.first, f32[256,256]{1,0:T(8,128)S(1)} %add.15.second, f32[16,256,256]{2,1,0:T(8,128)} %copy-done.2, f32[16,256,256]{2,1,0:T(8,128)} %copy-done.4, ...), custom_call_target="tpu_custom_call" | custom-call | flops 20971520 | bytes 33554432 | tf_op jit(solution)/shard_map/norm/pallas_call | solution.py:137
  (85 shorter events, 18.8 us)
Async XLA Ops:
  6.5 262.1 %all-gather.5.cloned.1.call-start = ((), (), s32[]{:S(2)}) async-start(), calls=%async_computation | async-start | bytes 41943040 | tf_op jit(solution)/shard_map/all_gather | solution.py:174
  7.3 313.4 %all-gather.7.cloned.1.call-start = ((), (), s32[]{:S(2)}) async-start(), calls=%async_computation.1 | async-start | bytes 20971520 | tf_op jit(solution)/shard_map/all_gather | solution.py:174
  7.3 15.5 %slice-start = ((s8[8388608]{0:T(1024)(128)(4,1)}), s8[4194304]{0:T(1024)(128)(4,1)S(1)}, s32[]{:S(2)}) async-start(s8[8388608]{0:T(1024)(128)(4,1)} %bitcast.10), calls=%async_computation.2 | async-start | bytes 8388608
  7.3 17.7 %slice-start.2 = ((s8[8388608]{0:T(1024)(128)(4,1)}), s8[4194304]{0:T(1024)(128)(4,1)S(1)}, s32[]{:S(2)}) async-start(s8[8388608]{0:T(1024)(128)(4,1)} %bitcast.12), calls=%async_computation.4 | async-start | bytes 8388608
  12.2 10.5 %slice-start.1 = ((s8[8388608]{0:T(1024)(128)(4,1)}), s8[4194304]{0:T(1024)(128)(4,1)S(1)}, s32[]{:S(2)}) async-start(s8[8388608]{0:T(1024)(128)(4,1)} %bitcast.10), calls=%async_computation.3 | async-start | bytes 8388608
  12.2 12.7 %slice-start.3 = ((s8[8388608]{0:T(1024)(128)(4,1)}), s8[4194304]{0:T(1024)(128)(4,1)S(1)}, s32[]{:S(2)}) async-start(s8[8388608]{0:T(1024)(128)(4,1)} %bitcast.12), calls=%async_computation.5 | async-start | bytes 8388608
  12.2 93.8 %collective-permute-start = (bf16[32,256,256]{2,1,0:T(8,128)(2,1)}, bf16[32,256,256]{2,1,0:T(8,128)(2,1)S(1)}, u32[]{:S(2)}, u32[]{:S(2)}) collective-permute-start(bf16[32,256,256]{2,1,0:T(8,128)(2,1)} %slice.30), channel_id=1, source_target_pairs={{0,1},{1,0},{2,3},{3,2},{4,5},{5,4},{6,7},{7,6},{8,9},{9,8},{10,11... | collective-permute-start | bytes 12582920 | tf_op jit(solution)/shard_map/ppermute | solution.py:173
  15.3 90.8 %collective-permute-start.1 = (bf16[32,256,256]{2,1,0:T(8,128)(2,1)}, bf16[32,256,256]{2,1,0:T(8,128)(2,1)S(1)}, u32[]{:S(2)}, u32[]{:S(2)}) collective-permute-start(bf16[32,256,256]{2,1,0:T(8,128)(2,1)} %slice.30), channel_id=1, source_target_pairs={{1,2},{2,1},{5,6},{6,5},{9,10},{10,9},{13,14},{14,13},{17,18},{18,... | collective-permute-start | bytes 12582920 | tf_op jit(solution)/shard_map/ppermute | solution.py:173
  106.1 96.1 %collective-permute-start.2 = (bf16[32,256,256]{2,1,0:T(8,128)(2,1)S(1)}, bf16[32,256,256]{2,1,0:T(8,128)(2,1)S(1)}, u32[]{:S(2)}, u32[]{:S(2)}) collective-permute-start(bf16[32,256,256]{2,1,0:T(8,128)(2,1)S(1)} %collective-permute-done.1.refs_2_), channel_id=1, source_target_pairs={{1,0},{2,3},{5,4},{6,7},{9,8},{10,11},{13,12},{14,15},{17,16},{18,... | collective-permute-start | bytes 12582920 | tf_op jit(solution)/shard_map/ppermute | solution.py:173
  107.3 2.0 copy-start.8
  109.3 94.8 %collective-permute-start.3 = (bf16[32,256,256]{2,1,0:T(8,128)(2,1)S(1)}, bf16[32,256,256]{2,1,0:T(8,128)(2,1)S(1)}, u32[]{:S(2)}, u32[]{:S(2)}) collective-permute-start(bf16[32,256,256]{2,1,0:T(8,128)(2,1)S(1)} %collective-permute-done.refs_1_), channel_id=1, source_target_pairs={{1,2},{2,1},{5,6},{6,5},{9,10},{10,9},{13,14},{14,13},{17,18},{18,... | collective-permute-start | bytes 12582920 | tf_op jit(solution)/shard_map/ppermute | solution.py:173
  110.2 2.0 copy-start.5
  112.3 98.3 %collective-permute-start.9 = (bf16[32,256,256]{2,1,0:T(8,128)(2,1)S(1)}, bf16[32,256,256]{2,1,0:T(8,128)(2,1)}, u32[]{:S(2)}, u32[]{:S(2)}) collective-permute-start(bf16[32,256,256]{2,1,0:T(8,128)(2,1)S(1)} %slice.34), channel_id=1, source_target_pairs={{0,1},{3,2},{4,5},{7,6},{8,9},{11,10},{12,13},{15,14},{16,17},{19,... | collective-permute-start | bytes 12582920 | tf_op jit(solution)/shard_map/ppermute | solution.py:173
  202.1 2.0 copy-start.11
  204.1 2.0 copy-start.19
  210.6 24.6 %collective-permute-start.5 = (bf16[8,256,256]{2,1,0:T(8,128)(2,1)S(1)}, bf16[8,256,256]{2,1,0:T(8,128)(2,1)}, u32[]{:S(2)}, u32[]{:S(2)}) collective-permute-start(bf16[8,256,256]{2,1,0:T(8,128)(2,1)S(1)} %slice.32), channel_id=1, source_target_pairs={{0,1},{3,2},{4,5},{7,6},{8,9},{11,10},{12,13},{15,14},{16,17},{19,... | collective-permute-start | bytes 3145736 | tf_op jit(solution)/shard_map/ppermute | solution.py:173
  216.1 79.7 %collective-permute-start.6 = (bf16[32,256,256]{2,1,0:T(8,128)(2,1)}, bf16[32,256,256]{2,1,0:T(8,128)(2,1)}, u32[]{:S(2)}, u32[]{:S(2)}) collective-permute-start(bf16[32,256,256]{2,1,0:T(8,128)(2,1)} %slice.31.refs_0_), channel_id=1, source_target_pairs={{1,2},{2,1},{5,6},{6,5},{9,10},{10,9},{13,14},{14,13},{17,18},{18,... | collective-permute-start | bytes 12582920 | tf_op jit(solution)/shard_map/ppermute | solution.py:173
  220.6 46.7 %collective-permute-start.4 = (bf16[16,256,256]{2,1,0:T(8,128)(2,1)S(1)}, bf16[16,256,256]{2,1,0:T(8,128)(2,1)S(1)}, u32[]{:S(2)}, u32[]{:S(2)}) collective-permute-start(bf16[16,256,256]{2,1,0:T(8,128)(2,1)S(1)} %slice.35), channel_id=1, source_target_pairs={{1,0},{2,3},{5,4},{6,7},{9,8},{10,11},{13,12},{14,15},{17,16},{18,... | collective-permute-start | bytes 6291464 | tf_op jit(solution)/shard_map/ppermute | solution.py:173
  235.2 68.9 %collective-permute-start.11 = (bf16[24,256,256]{2,1,0:T(8,128)(2,1)}, bf16[24,256,256]{2,1,0:T(8,128)(2,1)S(1)}, u32[]{:S(2)}, u32[]{:S(2)}) collective-permute-start(bf16[24,256,256]{2,1,0:T(8,128)(2,1)} %slice.33), channel_id=1, source_target_pairs={{0,1},{3,2},{4,5},{7,6},{8,9},{11,10},{12,13},{15,14},{16,17},{19,... | collective-permute-start | bytes 9437192 | tf_op jit(solution)/shard_map/ppermute | solution.py:173
  267.2 1.4 copy-start.17
  268.6 4.4 copy-start.23
  271.7 46.2 %collective-permute-start.8 = (bf16[16,256,256]{2,1,0:T(8,128)(2,1)}, bf16[16,256,256]{2,1,0:T(8,128)(2,1)}, u32[]{:S(2)}, u32[]{:S(2)}) collective-permute-start(bf16[16,256,256]{2,1,0:T(8,128)(2,1)} %slice.36), channel_id=1, source_target_pairs={{1,0},{2,3},{5,4},{6,7},{9,8},{10,11},{13,12},{14,15},{17,16},{18,... | collective-permute-start | bytes 6291464 | tf_op jit(solution)/shard_map/ppermute | solution.py:173
  273.0 2.2 copy-start.6
  275.3 2.2 copy-start.9
  277.4 2.2 copy-start.12
  279.6 1.6 copy-start.18
  288.2 2.0 copy-start.2
  295.1 21.1 %collective-permute-start.7 = (bf16[8,256,256]{2,1,0:T(8,128)(2,1)}, bf16[8,256,256]{2,1,0:T(8,128)(2,1)S(1)}, u32[]{:S(2)}, u32[]{:S(2)}) collective-permute-start(bf16[8,256,256]{2,1,0:T(8,128)(2,1)} %collective-permute-done.5.refs_1_), channel_id=1, source_target_pairs={{1,2},{2,1},{5,6},{6,5},{9,10},{10,9},{13,14},{14,13},{17,18},{18,... | collective-permute-start | bytes 3145736 | tf_op jit(solution)/shard_map/ppermute | solution.py:173
  304.2 11.4 %collective-permute-start.10 = (f16[256,256]{1,0:T(8,128)(2,1)S(1)}, f16[256,256]{1,0:T(8,128)(2,1)S(1)}, u32[]{:S(2)}, u32[]{:S(2)}) collective-permute-start(f16[256,256]{1,0:T(8,128)(2,1)S(1)} %get-tuple-element.62), channel_id=1, source_target_pairs={{0,1},{3,2},{4,5},{7,6},{8,9},{11,10},{12,13},{15,14},{16,17},{19,... | collective-permute-start | bytes 393224 | tf_op jit(solution)/shard_map/ppermute | solution.py:173
  313.9 26.7 %collective-permute-start.14 = (bf16[8,256,256]{2,1,0:T(8,128)(2,1)}, bf16[8,256,256]{2,1,0:T(8,128)(2,1)}, u32[]{:S(2)}, u32[]{:S(2)}) collective-permute-start(bf16[8,256,256]{2,1,0:T(8,128)(2,1)} %get-tuple-element.63), channel_id=1, source_target_pairs={{1,2},{2,1},{5,6},{6,5},{9,10},{10,9},{13,14},{14,13},{17,18},{18,... | collective-permute-start | bytes 3145736 | tf_op jit(solution)/shard_map/ppermute | solution.py:173
  320.7 2.2 copy-start
  322.9 1.2 copy-start.15
  324.1 4.4 copy-start.21
  324.1 6.8 %copy-start.7 = (bf16[32,256,256]{2,1,0:T(8,128)(2,1)S(1)}, bf16[32,256,256]{2,1,0:T(8,128)(2,1)}, u32[]{:S(2)}) copy-start(bf16[32,256,256]{2,1,0:T(8,128)(2,1)} %copy-done.5) | copy-start | bytes 12582916
  324.1 6.8 %copy-start.13 = (bf16[32,256,256]{2,1,0:T(8,128)(2,1)S(1)}, bf16[32,256,256]{2,1,0:T(8,128)(2,1)}, u32[]{:S(2)}) copy-start(bf16[32,256,256]{2,1,0:T(8,128)(2,1)} %copy-done.11) | copy-start | bytes 12582916
  328.8 32.6 %collective-permute-start.15 = (f16[8,256,256]{2,1,0:T(8,128)(2,1)S(1)}, f16[8,256,256]{2,1,0:T(8,128)(2,1)S(1)}, u32[]{:S(2)}, u32[]{:S(2)}) collective-permute-start(f16[8,256,256]{2,1,0:T(8,128)(2,1)S(1)} %subtract_convert_fusion.3), channel_id=1, source_target_pairs={{1,0},{2,3},{5,4},{6,7},{9,8},{10,11},{13,12},{14,15},{17,16},{18,... | collective-permute-start | bytes 3145736 | tf_op jit(solution)/shard_map/ppermute | solution.py:173
  330.1 34.6 %collective-permute-start.13 = (bf16[8,256,256]{2,1,0:T(8,128)(2,1)}, bf16[8,256,256]{2,1,0:T(8,128)(2,1)S(1)}, u32[]{:S(2)}, u32[]{:S(2)}) collective-permute-start(bf16[8,256,256]{2,1,0:T(8,128)(2,1)} %get-tuple-element.64), channel_id=1, source_target_pairs={{1,2},{2,1},{5,6},{6,5},{9,10},{10,9},{13,14},{14,13},{17,18},{18,... | collective-permute-start | bytes 3145736 | tf_op jit(solution)/shard_map/ppermute | solution.py:173
  330.9 2.2 copy-start.10
  333.1 7.6 %copy-start.1 = (bf16[32,256,256]{2,1,0:T(8,128)(2,1)S(1)}, bf16[32,256,256]{2,1,0:T(8,128)(2,1)}, u32[]{:S(2)}) copy-start(bf16[32,256,256]{2,1,0:T(8,128)(2,1)} %slice.31.refs_0_) | copy-start | bytes 12582916
  340.6 22.8 %copy-start.4 = (f32[16,256,256]{2,1,0:T(8,128)}, f32[16,256,256]{2,1,0:T(8,128)S(1)}, u32[]{:S(2)}) copy-start(f32[16,256,256]{2,1,0:T(8,128)S(1)} %tiles.9.refs_1_) | copy-start | bytes 12582916
  340.7 22.8 %copy-start.3 = (f32[16,256,256]{2,1,0:T(8,128)S(1)}, f32[16,256,256]{2,1,0:T(8,128)}, u32[]{:S(2)}) copy-start(f32[16,256,256]{2,1,0:T(8,128)} %copy-done.2) | copy-start | bytes 12582916
  346.6 16.1 %copy-start.22 = (bf16[8,256,256]{2,1,0:T(8,128)(2,1)S(1)}, bf16[8,256,256]{2,1,0:T(8,128)(2,1)}, u32[]{:S(2)}) copy-start(bf16[8,256,256]{2,1,0:T(8,128)(2,1)} %get-tuple-element.65) | copy-start | bytes 3145732
  361.4 23.3 %collective-permute-start.16 = (f16[8,256,256]{2,1,0:T(8,128)(2,1)S(1)}, f16[8,256,256]{2,1,0:T(8,128)(2,1)S(1)}, u32[]{:S(2)}, u32[]{:S(2)}) collective-permute-start(f16[8,256,256]{2,1,0:T(8,128)(2,1)S(1)} %subtract_convert_fusion.2), channel_id=1, source_target_pairs={{1,0},{2,3},{5,4},{6,7},{9,8},{10,11},{13,12},{14,15},{17,16},{18,... | collective-permute-start | bytes 3145736 | tf_op jit(solution)/shard_map/ppermute | solution.py:173
  362.7 23.5 %collective-permute-start.12 = (bf16[8,256,256]{2,1,0:T(8,128)(2,1)S(1)}, bf16[8,256,256]{2,1,0:T(8,128)(2,1)S(1)}, u32[]{:S(2)}, u32[]{:S(2)}) collective-permute-start(bf16[8,256,256]{2,1,0:T(8,128)(2,1)S(1)} %copy-done.22), channel_id=1, source_target_pairs={{1,2},{2,1},{5,6},{6,5},{9,10},{10,9},{13,14},{14,13},{17,18},{18,... | collective-permute-start | bytes 3145736 | tf_op jit(solution)/shard_map/ppermute | solution.py:173
  384.8 23.3 %collective-permute-start.17 = (f16[8,256,256]{2,1,0:T(8,128)(2,1)S(1)}, f16[8,256,256]{2,1,0:T(8,128)(2,1)S(1)}, u32[]{:S(2)}, u32[]{:S(2)}) collective-permute-start(f16[8,256,256]{2,1,0:T(8,128)(2,1)S(1)} %subtract_convert_fusion.1), channel_id=1, source_target_pairs={{1,0},{2,3},{5,4},{6,7},{9,8},{10,11},{13,12},{14,15},{17,16},{18,... | collective-permute-start | bytes 3145736 | tf_op jit(solution)/shard_map/ppermute | solution.py:173
  390.1 19.2 %copy-start.20 = (f32[256,256]{1,0:T(8,128)S(1)}, f32[256,256]{1,0:T(8,128)}, u32[]{:S(2)}) copy-start(f32[256,256]{1,0:T(8,128)} %get-tuple-element.61) | copy-start | bytes 786436
  408.1 18.8 %collective-permute-start.18 = (f16[8,256,256]{2,1,0:T(8,128)(2,1)S(1)}, f16[8,256,256]{2,1,0:T(8,128)(2,1)S(1)}, u32[]{:S(2)}, u32[]{:S(2)}) collective-permute-start(f16[8,256,256]{2,1,0:T(8,128)(2,1)S(1)} %subtract_convert_fusion), channel_id=1, source_target_pairs={{1,0},{2,3},{5,4},{6,7},{9,8},{10,11},{13,12},{14,15},{17,16},{18,... | collective-permute-start | bytes 3145736 | tf_op jit(solution)/shard_map/ppermute | solution.py:173
  409.6 1.2 copy-start.16
  (1 other events, 1.0 us)
Sparse Core Ops, SparseCore 0:
  8.9 204.2 all-gather.4
  214.7 105.9 all-gather.6

commit v4 on v3

--- a/solution.py
+++ b/solution.py
@@ -83,7 +83,7 @@
             out_specs=pl.BlockSpec((step, rows, cols), lambda c, *_: (c, 0, 0)),
         ),
         out_shape=jax.ShapeDtypeStruct((n, rows, cols), jnp.float32),
-        compiler_params=params(32),
+        compiler_params=params(48),
         cost_estimate=pl.CostEstimate(
             flops=8 * n * rows * cols * depth,
             bytes_accessed=n * (4 * (rows + cols) * depth * 2 + rows * cols * 4),

time: 449 us -> 446 us (level)
  local copies, waits for them, and re-layouts: 47.7 us -> 23.2 us
  waiting for transfers between devices: 265 us -> 279 us
  Pallas kernels: 59.4 us -> 65.5 us
    unnamed x56 -> x24, local copies, waits for them, and re-layouts: 27.1 us -> 2.75 us
    all_gather x2, waiting for transfers between devices: 2.79 us -> 9.82 us  [line(): rows_of = lambda block: lax.all_gather(block, 'row', axis=0, tiled=False)]
    ppermute x19, waiting for transfers between devices: 261 us -> 268 us  [line(): go = lambda block, pairs: lax.ppermute(block, 'col', pairs)]
    pallas_call x7, Pallas kernels: 47.9 us -> 54 us  [tiles(): pl.pallas_call(functools.partial(tiles_kernel, step, scale, tuple(groups)...]
  transfers between devices with their start and end apart: 21 -> 21, of which waited for: 12 -> 11; matrix products, arithmetic and copies ran while one was open for 7% -> 7% of each run, Pallas kernels for 11% -> 12%
where the time goes in v4:
time: 446 us; the launch traced here: 441 us
  waiting for transfers between devices  279 us (63%)
  Pallas kernels  65.5 us (15%)
  starting transfers between devices  49.3 us (11%)
  local copies, waits for them, and re-layouts  23.2 us (5%)
  between operations  13.8 us (3%)
  other arithmetic  10.3 us (2%)
    ppermute x19, waiting for transfers between devices, line(): go = lambda block, pairs: lax.ppermute(block, 'col', pairs)  268 us
    pallas_call x7, Pallas kernels, tiles(): pl.pallas_call(functools.partial(tiles_kernel, step, scale, tuple(groups)...  54 us
    ppermute x19, starting transfers between devices, line(): go = lambda block, pairs: lax.ppermute(block, 'col', pairs)  49.2 us
    slice x8, local copies, waits for them, and re-layouts, line(): cut = lambda array, at, n: lax.slice_in_dim(array, at, at + n, axis=0)  20.4 us
    pallas_call x1, Pallas kernels, norm(): pl.pallas_call(functools.partial(norm_kernel, len(shared), len(own)), gri...  11.5 us
    all_gather x2, waiting for transfers between devices, line(): rows_of = lambda block: lax.all_gather(block, 'row', axis=0, tiled=False)  9.82 us
  transfers between devices with their start and end apart: 21, of which 11 were waited for; matrix products, arithmetic and copies ran while one was open for 7% of the time, Pallas kernels for 12%

profile of v4, /device:TPU:0, one launch (start us, length us, event | category | flops | bytes accessed | tf_op | source)
XLA Modules:
  0.0 440.7 jit_solution(2386013715409441653)
XLA Ops:
  7.3 2.6 slice.30
  10.0 3.1 collective-permute-start
  13.1 1.1 collective-permute-start.1
  14.1 5.1 %slice.31.refs_0_ = bf16[32,256,256]{2,1,0:T(8,128)(2,1)} slice(bf16[64,256,256]{2,1,0:T(8,128)(2,1)} %refs_0_.2), slice={[32:64], [0:256], [0:256]} | slice | bytes 8388608 | tf_op jit(solution)/shard_map/slice | solution.py:171
  19.2 1.1 slice.32
  20.4 2.5 slice.33
  23.3 80.3 %collective-permute-done.refs_1_ = bf16[32,256,256]{2,1,0:T(8,128)(2,1)S(1)} collective-permute-done((bf16[32,256,256]{2,1,0:T(8,128)(2,1)S(1)}, bf16[32,256,256]{2,1,0:T(8,128)(2,1)S(1)}, u32[]{:S(2)}, u32[]{:S(2)}) %collective-permute-start) | collective-permute-done | bytes 4194336 | tf_op jit(solution)/shard_map/ppermute | solution.py:173
  103.6 1.3 collective-permute-start.2
  105.6 2.6 collective-permute-start.3
  108.3 9.5 %collective-permute-start.9 = (bf16[32,256,256]{2,1,0:T(8,128)(2,1)S(1)}, bf16[32,256,256]{2,1,0:T(8,128)(2,1)}, u32[]{:S(2)}, u32[]{:S(2)}) collective-permute-start(bf16[32,256,256]{2,1,0:T(8,128)(2,1)S(1)} %slice.34), channel_id=1, source_target_pairs={{0,1},{3,2},{4,5},{7,6},{8,9},{11,10},{12,13},{15,14},{16,17},{19,... | collective-permute-start | bytes 12582920 | tf_op jit(solution)/shard_map/ppermute | solution.py:173
  117.8 82.1 %collective-permute-done.2.refs_3_ = bf16[32,256,256]{2,1,0:T(8,128)(2,1)S(1)} collective-permute-done((bf16[32,256,256]{2,1,0:T(8,128)(2,1)S(1)}, bf16[32,256,256]{2,1,0:T(8,128)(2,1)S(1)}, u32[]{:S(2)}, u32[]{:S(2)}) %collective-permute-start.2) | collective-permute-done | bytes 4194336 | tf_op jit(solution)/shard_map/ppermute | solution.py:173
  199.9 2.0 copy-done.4
  201.9 2.4 collective-permute-done.9
  204.3 4.6 %collective-permute-start.5 = (bf16[8,256,256]{2,1,0:T(8,128)(2,1)}, bf16[8,256,256]{2,1,0:T(8,128)(2,1)S(1)}, u32[]{:S(2)}, u32[]{:S(2)}) collective-permute-start(bf16[8,256,256]{2,1,0:T(8,128)(2,1)} %slice.32), channel_id=1, source_target_pairs={{0,1},{3,2},{4,5},{7,6},{8,9},{11,10},{12,13},{15,14},{16,17},{19,... | collective-permute-start | bytes 3145736 | tf_op jit(solution)/shard_map/ppermute | solution.py:173
  208.8 2.7 collective-permute-start.6
  211.5 1.9 slice.35
  213.4 1.3 collective-permute-start.4
  214.7 14.5 %collective-permute-done.5.refs_1_ = bf16[8,256,256]{2,1,0:T(8,128)(2,1)S(1)} collective-permute-done((bf16[8,256,256]{2,1,0:T(8,128)(2,1)}, bf16[8,256,256]{2,1,0:T(8,128)(2,1)S(1)}, u32[]{:S(2)}, u32[]{:S(2)}) %collective-permute-start.5) | collective-permute-done | bytes 1048608 | tf_op jit(solution)/shard_map/ppermute | solution.py:173
  229.2 5.9 %collective-permute-start.11 = (bf16[24,256,256]{2,1,0:T(8,128)(2,1)}, bf16[24,256,256]{2,1,0:T(8,128)(2,1)}, u32[]{:S(2)}, u32[]{:S(2)}) collective-permute-start(bf16[24,256,256]{2,1,0:T(8,128)(2,1)} %slice.33), channel_id=1, source_target_pairs={{0,1},{3,2},{4,5},{7,6},{8,9},{11,10},{12,13},{15,14},{16,17},{19,... | collective-permute-start | bytes 9437192 | tf_op jit(solution)/shard_map/ppermute | solution.py:173
  235.1 24.8 %collective-permute-done.4.refs_5_ = bf16[16,256,256]{2,1,0:T(8,128)(2,1)S(1)} collective-permute-done((bf16[16,256,256]{2,1,0:T(8,128)(2,1)S(1)}, bf16[16,256,256]{2,1,0:T(8,128)(2,1)S(1)}, u32[]{:S(2)}, u32[]{:S(2)}) %collective-permute-start.4) | collective-permute-done | bytes 2097184 | tf_op jit(solution)/shard_map/ppermute | solution.py:173
  259.9 3.1 slice.36
  263.1 1.3 collective-permute-start.8
  264.4 9.5 %tiles.7.refs_0_ = f32[16,256,256]{2,1,0:T(8,128)} custom-call(s32[4]{0:T(128)S(1)} %fusion.order, s32[1]{0:T(128)} %bitcast.inner, bf16[64,256,256]{2,1,0:T(8,128)(2,1)} %refs_0_.2, bf16[32,256,256]{2,1,0:T(8,128)(2,1)} %copy-done.2, bf16[32,256,256]{2,1,0:T(8,128)(2,1)} %copy-done.3, bf16[32,256,256]{2,1,0:T(8,128)(2,1)} %copy-done.4, ...), custom_call_target="tpu_custom_call" | custom-call | flops 2147483648 | bytes 20971520 | tf_op jit(solution)/shard_map/tiles/pallas_call | solution.py:77
  273.9 2.7 reduce_sum.45
  276.5 0.7 fusion.1
  278.0 20.0 %collective-permute-done.11.refs_1_.refs_2_ = bf16[24,256,256]{2,1,0:T(8,128)(2,1)} collective-permute-done((bf16[24,256,256]{2,1,0:T(8,128)(2,1)}, bf16[24,256,256]{2,1,0:T(8,128)(2,1)}, u32[]{:S(2)}, u32[]{:S(2)}) %collective-permute-start.11) | collective-permute-done | bytes 3145760 | tf_op jit(solution)/shard_map/ppermute | solution.py:173
  298.0 7.8 %collective-permute-start.10 = (f16[256,256]{1,0:T(8,128)(2,1)S(1)}, f16[256,256]{1,0:T(8,128)(2,1)S(1)}, u32[]{:S(2)}, u32[]{:S(2)}) collective-permute-start(f16[256,256]{1,0:T(8,128)(2,1)S(1)} %get-tuple-element.62), channel_id=1, source_target_pairs={{0,1},{3,2},{4,5},{7,6},{8,9},{11,10},{12,13},{15,14},{16,17},{19,... | collective-permute-start | bytes 393224 | tf_op jit(solution)/shard_map/ppermute | solution.py:173
  305.8 3.6 fusion.2
  310.9 9.8 %all-gather.7.cloned.1.call-done = bf16[128,256,256]{2,1,0:T(8,128)(2,1)} async-done(((bf16[32,256,256]{2,1,0:T(8,128)(2,1)}), bf16[128,256,256]{2,1,0:T(8,128)(2,1)}) %all-gather.7.cloned.1.call-update) | async-done | bytes 16777232 | tf_op jit(solution)/shard_map/all_gather | solution.py:174
  320.7 4.2 tiles.8
  324.9 1.2 subtract_convert_fusion.3
  326.1 1.3 collective-permute-start.15
  328.1 10.0 %tiles.9.refs_1_ = f32[16,256,256]{2,1,0:T(8,128)} custom-call(s32[4]{0:T(128)S(1)} %fusion.order, s32[1]{0:T(128)} %bitcast.inner, bf16[64,256,256]{2,1,0:T(8,128)(2,1)} %refs_0_.2, bf16[32,256,256]{2,1,0:T(8,128)(2,1)} %copy-done.2, bf16[32,256,256]{2,1,0:T(8,128)(2,1)} %copy-done.3, bf16[32,256,256]{2,1,0:T(8,128)(2,1)} %copy-done.4, ...), custom_call_target="tpu_custom_call" | custom-call | flops 2147483648 | bytes 20971520 | tf_op jit(solution)/shard_map/tiles/pallas_call | solution.py:77
  338.2 4.8 %tiles.10 = f32[8,256,256]{2,1,0:T(8,128)S(1)} custom-call(s32[4]{0:T(128)S(1)} %fusion.order, s32[1]{0:T(128)} %bitcast.inner, bf16[32,256,256]{2,1,0:T(8,128)(2,1)} %slice.31.refs_0_, bf16[24,256,256]{2,1,0:T(8,128)(2,1)} %collective-permute-done.11.refs_1_.refs_2_, bf16[32,256,256]{2,1,0:T(8,128)(2,1)} %collective-permute-done.6.refs_2_.refs_3_, ...), custom_call_target="tpu_custom_call" | custom-call | flops 1073741824 | bytes 10485760 | tf_op jit(solution)/shard_map/tiles/pallas_call | solution.py:77
  343.0 1.2 subtract_convert_fusion.2
  344.2 9.4 %collective-permute-done.15 = f16[8,256,256]{2,1,0:T(8,128)(2,1)} collective-permute-done((f16[8,256,256]{2,1,0:T(8,128)(2,1)}, f16[8,256,256]{2,1,0:T(8,128)(2,1)}, u32[]{:S(2)}, u32[]{:S(2)}) %collective-permute-start.15) | collective-permute-done | bytes 1048608 | tf_op jit(solution)/shard_map/ppermute | solution.py:173
  353.6 1.3 collective-permute-start.16
  355.7 1.1 multiply_reduce_fusion
  356.9 4.5 %tiles.11 = f32[8,256,256]{2,1,0:T(8,128)S(1)} custom-call(s32[4]{0:T(128)S(1)} %fusion.order, s32[1]{0:T(128)} %bitcast.inner, bf16[32,256,256]{2,1,0:T(8,128)(2,1)} %slice.31.refs_0_, bf16[24,256,256]{2,1,0:T(8,128)(2,1)} %collective-permute-done.11.refs_1_.refs_2_, bf16[32,256,256]{2,1,0:T(8,128)(2,1)} %collective-permute-done.6.refs_2_.refs_3_, ...), custom_call_target="tpu_custom_call" | custom-call | flops 1073741824 | bytes 10485760 | tf_op jit(solution)/shard_map/tiles/pallas_call | solution.py:77
  361.7 15.5 %collective-permute-done.16 = f16[8,256,256]{2,1,0:T(8,128)(2,1)S(1)} collective-permute-done((f16[8,256,256]{2,1,0:T(8,128)(2,1)}, f16[8,256,256]{2,1,0:T(8,128)(2,1)S(1)}, u32[]{:S(2)}, u32[]{:S(2)}) %collective-permute-start.16) | collective-permute-done | bytes 1048608 | tf_op jit(solution)/shard_map/ppermute | solution.py:173
  377.2 1.3 collective-permute-start.17
  378.5 4.5 %tiles.12 = f32[8,256,256]{2,1,0:T(8,128)S(1)} custom-call(s32[4]{0:T(128)S(1)} %fusion.order, s32[1]{0:T(128)} %bitcast.inner, bf16[32,256,256]{2,1,0:T(8,128)(2,1)} %slice.31.refs_0_, bf16[24,256,256]{2,1,0:T(8,128)(2,1)} %collective-permute-done.11.refs_1_.refs_2_, bf16[32,256,256]{2,1,0:T(8,128)(2,1)} %collective-permute-done.6.refs_2_.refs_3_, ...), custom_call_target="tpu_custom_call" | custom-call | flops 1073741824 | bytes 10485760 | tf_op jit(solution)/shard_map/tiles/pallas_call | solution.py:77
  383.3 17.2 %collective-permute-done.17 = f16[8,256,256]{2,1,0:T(8,128)(2,1)S(1)} collective-permute-done((f16[8,256,256]{2,1,0:T(8,128)(2,1)S(1)}, f16[8,256,256]{2,1,0:T(8,128)(2,1)S(1)}, u32[]{:S(2)}, u32[]{:S(2)}) %collective-permute-start.17) | collective-permute-done | bytes 1048608 | tf_op jit(solution)/shard_map/ppermute | solution.py:173
  400.5 1.5 collective-permute-start.18
  402.0 1.5 add_multiply_fusion.3.refs_3_
  403.7 16.5 %tiles.13.refs_2_ = f32[32,256,256]{2,1,0:T(8,128)} custom-call(s32[4]{0:T(128)S(1)} %fusion.order, s32[1]{0:T(128)} %bitcast.inner, bf16[32,256,256]{2,1,0:T(8,128)(2,1)} %slice.31.refs_0_, bf16[8,256,256]{2,1,0:T(8,128)(2,1)S(1)} %collective-permute-done.5.refs_1_, bf16[24,256,256]{2,1,0:T(8,128)(2,1)} %collective-permute-done.11.refs_1_.refs_2_, ...), custom_call_target="tpu_custom_call" | custom-call | flops 4294967296 | bytes 41943040 | tf_op jit(solution)/shard_map/tiles/pallas_call | solution.py:77
  420.4 1.8 collective-permute-done.18
  422.4 11.5 %norm.1 = f32[64,256,256]{2,1,0:T(8,128)} custom-call(s32[1]{0:T(128)} %bitcast.inner, f32[256,256]{1,0:T(8,128)S(1)} %get-tuple-element.66.offset, f32[256,256]{1,0:T(8,128)S(1)} %add.14.first, f32[256,256]{1,0:T(8,128)S(1)} %add.15.second, f32[16,256,256]{2,1,0:T(8,128)} %tiles.7.refs_0_, f32[16,256,256]{2,1,0:T(8,128)} %tiles.9.refs_1_, ...), custom_call_target="tpu_custom_call" | custom-call | flops 20971520 | bytes 33554432 | tf_op jit(solution)/shard_map/norm/pallas_call | solution.py:137
  (53 shorter events, 6.8 us)
Async XLA Ops:
  6.5 253.4 %all-gather.5.cloned.1.call-start = ((), (), s32[]{:S(2)}) async-start(), calls=%async_computation | async-start | bytes 41943040 | tf_op jit(solution)/shard_map/all_gather | solution.py:174
  7.3 313.4 %all-gather.7.cloned.1.call-start = ((), (), s32[]{:S(2)}) async-start(), calls=%async_computation.1 | async-start | bytes 20971520 | tf_op jit(solution)/shard_map/all_gather | solution.py:174
  7.3 11.9 %slice-start = ((s8[8388608]{0:T(1024)(128)(4,1)}), s8[4194304]{0:T(1024)(128)(4,1)S(1)}, s32[]{:S(2)}) async-start(s8[8388608]{0:T(1024)(128)(4,1)} %bitcast.10), calls=%async_computation.2 | async-start | bytes 8388608
  7.3 15.6 %slice-start.2 = ((s8[8388608]{0:T(1024)(128)(4,1)}), s8[4194304]{0:T(1024)(128)(4,1)S(1)}, s32[]{:S(2)}) async-start(s8[8388608]{0:T(1024)(128)(4,1)} %bitcast.12), calls=%async_computation.4 | async-start | bytes 8388608
  9.9 9.3 %slice-start.1 = ((s8[8388608]{0:T(1024)(128)(4,1)}), s8[4194304]{0:T(1024)(128)(4,1)S(1)}, s32[]{:S(2)}) async-start(s8[8388608]{0:T(1024)(128)(4,1)} %bitcast.10), calls=%async_computation.3 | async-start | bytes 8388608
  10.0 12.9 %slice-start.3 = ((s8[8388608]{0:T(1024)(128)(4,1)}), s8[4194304]{0:T(1024)(128)(4,1)S(1)}, s32[]{:S(2)}) async-start(s8[8388608]{0:T(1024)(128)(4,1)} %bitcast.12), calls=%async_computation.5 | async-start | bytes 8388608
  10.0 93.7 %collective-permute-start = (bf16[32,256,256]{2,1,0:T(8,128)(2,1)S(1)}, bf16[32,256,256]{2,1,0:T(8,128)(2,1)S(1)}, u32[]{:S(2)}, u32[]{:S(2)}) collective-permute-start(bf16[32,256,256]{2,1,0:T(8,128)(2,1)S(1)} %slice.30), channel_id=1, source_target_pairs={{0,1},{1,0},{2,3},{3,2},{4,5},{5,4},{6,7},{7,6},{8,9},{9,8},{10,11... | collective-permute-start | bytes 12582920 | tf_op jit(solution)/shard_map/ppermute | solution.py:173
  13.1 90.6 %collective-permute-start.1 = (bf16[32,256,256]{2,1,0:T(8,128)(2,1)S(1)}, bf16[32,256,256]{2,1,0:T(8,128)(2,1)S(1)}, u32[]{:S(2)}, u32[]{:S(2)}) collective-permute-start(bf16[32,256,256]{2,1,0:T(8,128)(2,1)S(1)} %slice.30), channel_id=1, source_target_pairs={{1,2},{2,1},{5,6},{6,5},{9,10},{10,9},{13,14},{14,13},{17,18},{18,... | collective-permute-start | bytes 12582920 | tf_op jit(solution)/shard_map/ppermute | solution.py:173
  103.6 2.0 copy-start.2
  103.6 96.2 %copy-start.3 = (bf16[32,256,256]{2,1,0:T(8,128)(2,1)}, bf16[32,256,256]{2,1,0:T(8,128)(2,1)S(1)}, u32[]{:S(2)}) copy-start(bf16[32,256,256]{2,1,0:T(8,128)(2,1)S(1)} %collective-permute-done.1.refs_2_) | copy-start | bytes 12582916
  103.6 96.2 %collective-permute-start.2 = (bf16[32,256,256]{2,1,0:T(8,128)(2,1)S(1)}, bf16[32,256,256]{2,1,0:T(8,128)(2,1)S(1)}, u32[]{:S(2)}, u32[]{:S(2)}) collective-permute-start(bf16[32,256,256]{2,1,0:T(8,128)(2,1)S(1)} %collective-permute-done.1.refs_2_), channel_id=1, source_target_pairs={{1,0},{2,3},{5,4},{6,7},{9,8},{10,11},{13,12},{14,15},{17,16},{18,... | collective-permute-start | bytes 12582920 | tf_op jit(solution)/shard_map/ppermute | solution.py:173
  105.6 94.2 %collective-permute-start.3 = (bf16[32,256,256]{2,1,0:T(8,128)(2,1)S(1)}, bf16[32,256,256]{2,1,0:T(8,128)(2,1)}, u32[]{:S(2)}, u32[]{:S(2)}) collective-permute-start(bf16[32,256,256]{2,1,0:T(8,128)(2,1)S(1)} %collective-permute-done.refs_1_), channel_id=1, source_target_pairs={{1,2},{2,1},{5,6},{6,5},{9,10},{10,9},{13,14},{14,13},{17,18},{18,... | collective-permute-start | bytes 12582920 | tf_op jit(solution)/shard_map/ppermute | solution.py:173
  108.3 95.9 %collective-permute-start.9 = (bf16[32,256,256]{2,1,0:T(8,128)(2,1)S(1)}, bf16[32,256,256]{2,1,0:T(8,128)(2,1)}, u32[]{:S(2)}, u32[]{:S(2)}) collective-permute-start(bf16[32,256,256]{2,1,0:T(8,128)(2,1)S(1)} %slice.34), channel_id=1, source_target_pairs={{0,1},{3,2},{4,5},{7,6},{8,9},{11,10},{12,13},{15,14},{16,17},{19,... | collective-permute-start | bytes 12582920 | tf_op jit(solution)/shard_map/ppermute | solution.py:173
  199.9 2.0 copy-start.4
  204.3 24.9 %collective-permute-start.5 = (bf16[8,256,256]{2,1,0:T(8,128)(2,1)}, bf16[8,256,256]{2,1,0:T(8,128)(2,1)S(1)}, u32[]{:S(2)}, u32[]{:S(2)}) collective-permute-start(bf16[8,256,256]{2,1,0:T(8,128)(2,1)} %slice.32), channel_id=1, source_target_pairs={{0,1},{3,2},{4,5},{7,6},{8,9},{11,10},{12,13},{15,14},{16,17},{19,... | collective-permute-start | bytes 3145736 | tf_op jit(solution)/shard_map/ppermute | solution.py:173
  208.8 69.2 %collective-permute-start.6 = (bf16[32,256,256]{2,1,0:T(8,128)(2,1)}, bf16[32,256,256]{2,1,0:T(8,128)(2,1)}, u32[]{:S(2)}, u32[]{:S(2)}) collective-permute-start(bf16[32,256,256]{2,1,0:T(8,128)(2,1)} %slice.31.refs_0_), channel_id=1, source_target_pairs={{1,2},{2,1},{5,6},{6,5},{9,10},{10,9},{13,14},{14,13},{17,18},{18,... | collective-permute-start | bytes 12582920 | tf_op jit(solution)/shard_map/ppermute | solution.py:173
  213.4 46.5 %collective-permute-start.4 = (bf16[16,256,256]{2,1,0:T(8,128)(2,1)S(1)}, bf16[16,256,256]{2,1,0:T(8,128)(2,1)S(1)}, u32[]{:S(2)}, u32[]{:S(2)}) collective-permute-start(bf16[16,256,256]{2,1,0:T(8,128)(2,1)S(1)} %slice.35), channel_id=1, source_target_pairs={{1,0},{2,3},{5,4},{6,7},{9,8},{10,11},{13,12},{14,15},{17,16},{18,... | collective-permute-start | bytes 6291464 | tf_op jit(solution)/shard_map/ppermute | solution.py:173
  229.2 68.8 %collective-permute-start.11 = (bf16[24,256,256]{2,1,0:T(8,128)(2,1)}, bf16[24,256,256]{2,1,0:T(8,128)(2,1)}, u32[]{:S(2)}, u32[]{:S(2)}) collective-permute-start(bf16[24,256,256]{2,1,0:T(8,128)(2,1)} %slice.33), channel_id=1, source_target_pairs={{0,1},{3,2},{4,5},{7,6},{8,9},{11,10},{12,13},{15,14},{16,17},{19,... | collective-permute-start | bytes 9437192 | tf_op jit(solution)/shard_map/ppermute | solution.py:173
  259.9 4.4 %copy-start.7 = (s32[4]{0:T(128)S(1)}, s32[4]{0:T(128)}, u32[]{:S(2)}) copy-start(s32[4]{0:T(128)} %constant.19.clone) | copy-start | bytes 52
  263.1 47.8 %collective-permute-start.8 = (bf16[16,256,256]{2,1,0:T(8,128)(2,1)}, bf16[16,256,256]{2,1,0:T(8,128)(2,1)}, u32[]{:S(2)}, u32[]{:S(2)}) collective-permute-start(bf16[16,256,256]{2,1,0:T(8,128)(2,1)} %slice.36), channel_id=1, source_target_pairs={{1,0},{2,3},{5,4},{6,7},{9,8},{10,11},{13,12},{14,15},{17,16},{18,... | collective-permute-start | bytes 6291464 | tf_op jit(solution)/shard_map/ppermute | solution.py:173
  277.3 33.6 %collective-permute-start.7 = (bf16[8,256,256]{2,1,0:T(8,128)(2,1)S(1)}, bf16[8,256,256]{2,1,0:T(8,128)(2,1)S(1)}, u32[]{:S(2)}, u32[]{:S(2)}) collective-permute-start(bf16[8,256,256]{2,1,0:T(8,128)(2,1)S(1)} %collective-permute-done.5.refs_1_), channel_id=1, source_target_pairs={{1,2},{2,1},{5,6},{6,5},{9,10},{10,9},{13,14},{14,13},{17,18},{18,... | collective-permute-start | bytes 3145736 | tf_op jit(solution)/shard_map/ppermute | solution.py:173
  298.0 12.1 %collective-permute-start.10 = (f16[256,256]{1,0:T(8,128)(2,1)S(1)}, f16[256,256]{1,0:T(8,128)(2,1)S(1)}, u32[]{:S(2)}, u32[]{:S(2)}) collective-permute-start(f16[256,256]{1,0:T(8,128)(2,1)S(1)} %get-tuple-element.62), channel_id=1, source_target_pairs={{0,1},{3,2},{4,5},{7,6},{8,9},{11,10},{12,13},{15,14},{16,17},{19,... | collective-permute-start | bytes 393224 | tf_op jit(solution)/shard_map/ppermute | solution.py:173
  309.4 28.8 %collective-permute-start.14 = (bf16[8,256,256]{2,1,0:T(8,128)(2,1)}, bf16[8,256,256]{2,1,0:T(8,128)(2,1)S(1)}, u32[]{:S(2)}, u32[]{:S(2)}) collective-permute-start(bf16[8,256,256]{2,1,0:T(8,128)(2,1)} %get-tuple-element.63), channel_id=1, source_target_pairs={{1,2},{2,1},{5,6},{6,5},{9,10},{10,9},{13,14},{14,13},{17,18},{18,... | collective-permute-start | bytes 3145736 | tf_op jit(solution)/shard_map/ppermute | solution.py:173
  320.7 4.2 copy-start.6
  326.1 27.5 %collective-permute-start.15 = (f16[8,256,256]{2,1,0:T(8,128)(2,1)}, f16[8,256,256]{2,1,0:T(8,128)(2,1)}, u32[]{:S(2)}, u32[]{:S(2)}) collective-permute-start(f16[8,256,256]{2,1,0:T(8,128)(2,1)} %subtract_convert_fusion.3), channel_id=1, source_target_pairs={{1,0},{2,3},{5,4},{6,7},{9,8},{10,11},{13,12},{14,15},{17,16},{18,... | collective-permute-start | bytes 3145736 | tf_op jit(solution)/shard_map/ppermute | solution.py:173
  327.4 29.5 %collective-permute-start.13 = (bf16[8,256,256]{2,1,0:T(8,128)(2,1)}, bf16[8,256,256]{2,1,0:T(8,128)(2,1)S(1)}, u32[]{:S(2)}, u32[]{:S(2)}) collective-permute-start(bf16[8,256,256]{2,1,0:T(8,128)(2,1)} %get-tuple-element.64), channel_id=1, source_target_pairs={{1,2},{2,1},{5,6},{6,5},{9,10},{10,9},{13,14},{14,13},{17,18},{18,... | collective-permute-start | bytes 3145736 | tf_op jit(solution)/shard_map/ppermute | solution.py:173
  338.2 17.5 %copy-start = (f32[16,256,256]{2,1,0:T(8,128)S(1)}, f32[16,256,256]{2,1,0:T(8,128)}, u32[]{:S(2)}) copy-start(f32[16,256,256]{2,1,0:T(8,128)} %tiles.7.refs_0_) | copy-start | bytes 12582916
  338.2 17.5 %copy-start.1 = (f32[16,256,256]{2,1,0:T(8,128)S(1)}, f32[16,256,256]{2,1,0:T(8,128)}, u32[]{:S(2)}) copy-start(f32[16,256,256]{2,1,0:T(8,128)} %tiles.9.refs_1_) | copy-start | bytes 12582916
  353.6 23.6 %collective-permute-start.16 = (f16[8,256,256]{2,1,0:T(8,128)(2,1)}, f16[8,256,256]{2,1,0:T(8,128)(2,1)S(1)}, u32[]{:S(2)}, u32[]{:S(2)}) collective-permute-start(f16[8,256,256]{2,1,0:T(8,128)(2,1)} %subtract_convert_fusion.2), channel_id=1, source_target_pairs={{1,0},{2,3},{5,4},{6,7},{9,8},{10,11},{13,12},{14,15},{17,16},{18,... | collective-permute-start | bytes 3145736 | tf_op jit(solution)/shard_map/ppermute | solution.py:173
  354.9 23.6 %collective-permute-start.12 = (bf16[8,256,256]{2,1,0:T(8,128)(2,1)}, bf16[8,256,256]{2,1,0:T(8,128)(2,1)S(1)}, u32[]{:S(2)}, u32[]{:S(2)}) collective-permute-start(bf16[8,256,256]{2,1,0:T(8,128)(2,1)} %get-tuple-element.65), channel_id=1, source_target_pairs={{1,2},{2,1},{5,6},{6,5},{9,10},{10,9},{13,14},{14,13},{17,18},{18,... | collective-permute-start | bytes 3145736 | tf_op jit(solution)/shard_map/ppermute | solution.py:173
  377.2 23.3 %collective-permute-start.17 = (f16[8,256,256]{2,1,0:T(8,128)(2,1)S(1)}, f16[8,256,256]{2,1,0:T(8,128)(2,1)S(1)}, u32[]{:S(2)}, u32[]{:S(2)}) collective-permute-start(f16[8,256,256]{2,1,0:T(8,128)(2,1)S(1)} %subtract_convert_fusion.1), channel_id=1, source_target_pairs={{1,0},{2,3},{5,4},{6,7},{9,8},{10,11},{13,12},{14,15},{17,16},{18,... | collective-permute-start | bytes 3145736 | tf_op jit(solution)/shard_map/ppermute | solution.py:173
  383.1 19.0 %copy-start.5 = (f32[256,256]{1,0:T(8,128)S(1)}, f32[256,256]{1,0:T(8,128)}, u32[]{:S(2)}) copy-start(f32[256,256]{1,0:T(8,128)} %get-tuple-element.61) | copy-start | bytes 786436
  400.5 21.6 %collective-permute-start.18 = (f16[8,256,256]{2,1,0:T(8,128)(2,1)S(1)}, f16[8,256,256]{2,1,0:T(8,128)(2,1)S(1)}, u32[]{:S(2)}, u32[]{:S(2)}) collective-permute-start(f16[8,256,256]{2,1,0:T(8,128)(2,1)S(1)} %subtract_convert_fusion), channel_id=1, source_target_pairs={{1,0},{2,3},{5,4},{6,7},{9,8},{10,11},{13,12},{14,15},{17,16},{18,... | collective-permute-start | bytes 3145736 | tf_op jit(solution)/shard_map/ppermute | solution.py:173
Sparse Core Ops, SparseCore 0:
  8.9 204.2 all-gather.4
  214.7 105.9 all-gather.6

commit v5 on v4

--- a/solution.py
+++ b/solution.py
@@ -9,6 +9,7 @@
 
 EPS = 1e-5
 HALF_SCALE = 16.0
+HALF_REACH = 32768.0
 
 
 def gathered(left_proj, right_proj):
@@ -29,8 +30,12 @@
     return pltpu.CompilerParams(vmem_limit_bytes=limit * 1024 * 1024, dimension_semantics=("arbitrary",))
 
 
-def tiles_kernel(step, scale, groups, order, inner, *refs):
-    *lefts, right, out = refs
+def tiles_kernel(step, scaled, groups, order, inner, *refs):
+    if scaled:
+        *lefts, right, offset, out, unit = refs
+        largest = jnp.zeros(out.shape[1:], jnp.float32)
+    else:
+        *lefts, right, out = refs
     for c in range(step):
         acc, at = None, 0
         for turn, begins in enumerate(groups):
@@ -41,10 +46,28 @@
             at += len(begins)
             term = dot_nt(one, right[order[turn], c])
             acc = term if acc is None else acc + term
-        out[c] = acc if scale == 1.0 else acc * scale
-
-
-def tiles(order, inner, lefts, right, right_at, n, scale=1.0):
+        if scaled:
+            acc = acc * HALF_SCALE - offset[...]
+            largest = jnp.maximum(largest, jnp.abs(acc))
+        out[c] = acc
+
+    if scaled:
+        here = jnp.full(unit.shape, jnp.max(largest), jnp.float32)
+
+        @pl.when(pl.program_id(0) == 0)
+        def _():
+            unit[...] = here
+
+        @pl.when(pl.program_id(0) != 0)
+        def _():
+            unit[...] = jnp.maximum(unit[...], here)
+
+        @pl.when(pl.program_id(0) == pl.num_programs(0) - 1)
+        def _():
+            unit[...] = jnp.exp2(jnp.ceil(jnp.log2(jnp.maximum(unit[...], 1e-30) * (1.0 / HALF_REACH))))
+
+
+def tiles(order, inner, lefts, right, right_at, n, offset=None):
     step = 4
     arrays, specs, groups = [], [], []
     rows, depth = lefts[0][0][0].shape[1:]
@@ -74,15 +97,23 @@
                 begin += count
             groups.append(tuple(begins))
     specs.append(pl.BlockSpec((4, step, cols, depth), lambda c, *_: (0, right_at // step + c, 0, 0)))
-    return pl.pallas_call(
-        functools.partial(tiles_kernel, step, scale, tuple(groups)),
+    out_specs = [pl.BlockSpec((step, rows, cols), lambda c, *_: (c, 0, 0))]
+    out_shape = [jax.ShapeDtypeStruct((n, rows, cols), jnp.float32)]
+    extra = []
+    if offset is not None:
+        extra.append(offset)
+        specs.append(pl.BlockSpec((rows, cols), lambda c, *_: (0, 0)))
+        out_specs.append(pl.BlockSpec((8, 128), lambda c, *_: (0, 0)))
+        out_shape.append(jax.ShapeDtypeStruct((8, 128), jnp.float32))
+    results = pl.pallas_call(
+        functools.partial(tiles_kernel, step, offset is not None, tuple(groups)),
         grid_spec=pltpu.PrefetchScalarGridSpec(
             num_scalar_prefetch=2,
             grid=(n // step,),
             in_specs=specs,
-            out_specs=pl.BlockSpec((step, rows, cols), lambda c, *_: (c, 0, 0)),
+            out_specs=out_specs,
         ),
-        out_shape=jax.ShapeDtypeStruct((n, rows, cols), jnp.float32),
+        out_shape=out_shape,
         compiler_params=params(48),
         cost_estimate=pl.CostEstimate(
             flops=8 * n * rows * cols * depth,
@@ -90,7 +121,8 @@
             transcendentals=0,
         ),
         name="tiles",
-    )(order, inner, *arrays, right)
+    )(order, inner, *arrays, right, *extra)
+    return results if extra else results[0]
 
 
 def norm_kernel(both, mine, inner, offset, first, second, *refs):
@@ -209,24 +241,36 @@
     p3 = [go(after(e_f[0], there), MIDDLE)]
     ended = (p2_f, *e_f)
     p3 += [go(block, MIDDLE) for block in pieces(after(e_f[1], *ended), 0, sizes[1:])]
-    sent, payloads, returned, at = [], [], [], 0
+
+    def mine(at, *done):
+        e = e_f if at == 0 else [(e_f[1], at - sizes[0])]
+        return [[(after(second, *done), at)], e, [(p2_f, at)], p3[: len(p3) // 2] if at == 0 else p3[len(p3) // 2 :]]
+
+    sent, payloads, returned, sizes_out, at = [], [], [], [], 0
     for j, n in enumerate(sizes):
         waits = [*payloads[-1:], *returned[: max(j - 1, 0)], *([near_b] if j == 1 else []), *([q3_nb] if j == 0 else [])]
         blocks = [[(second, at)], [(e_f[1], at - sizes[0]) if j else (e_f[0], 0)], [(p2_f, at)], [(after(p3[j], *waits), 0)]]
-        tile = tiles(order, inner, blocks, right_f, at, n, HALF_SCALE)
-        payload = (tile - here.astype(jnp.float32)).astype(jnp.float16)
+        tile, size = tiles(order, inner, blocks, right_f, at, n, here.astype(jnp.float32))
+        payload = (tile * (1.0 / size[0, 0])).astype(jnp.float16)
+        sizes_out.append(size)
         payloads.append(payload)
         if j == 0:
             near_b = near(near_sizes[0], q3_nb, near_sizes[1], payload)
             stats = stats_of(offset, near_b, *stats)
         ties = [(), (near_b, *returned), (*stats, *returned[1:]), returned[2:]][j]
+        if j == len(sizes) - 1:
+            own = [tiles(order, inner, mine(0, payloads[-2]), right_own, near_n, far_n // 2)]
+            ties = (*ties, *own)
+            units = go(jnp.concatenate(sizes_out, axis=0), OUTWARD)
+            ties = (*ties, units)
         arrived = go(after(payload, *ties), OUTWARD)
         returned.append(arrived)
-        back = after(arrived, *sent[-1:])
-        sent.append((back.astype(jnp.float32) + there.astype(jnp.float32)) * (1.0 / HALF_SCALE))
         at += n
-    own = tiles(order, inner, [[(after(second, payloads[-1]), 0)], e_f, [(p2_f, 0)], p3], right_own, near_n, far_n)
-    return norm(inner, (offset, *stats), [near_a, near_b], [own], sent)
+    for j, arrived in enumerate(returned):
+        back = after(arrived, *sent[-1:]).astype(jnp.float32) * units[8 * j, 0]
+        sent.append((back + there.astype(jnp.float32)) * (1.0 / HALF_SCALE))
+    own.append(tiles(order, inner, mine(far_n // 2, payloads[-1]), right_own, near_n + far_n // 2, far_n // 2))
+    return norm(inner, (offset, *stats), [near_a, near_b], own, sent)
 
 
 def solution(mesh):

time: 446 us -> 446 us (level)
  waiting for transfers between devices: 279 us -> 268 us
  local copies, waits for them, and re-layouts: 23.2 us -> 27.9 us
    ppermute x19 -> x20, waiting for transfers between devices: 268 us -> 258 us  [line(): go = lambda block, pairs: lax.ppermute(block, 'col', pairs)]
    unnamed x24 -> x36, local copies, waits for them, and re-layouts: 2.75 us -> 7.89 us
    pallas_call x7 -> x8, Pallas kernels: 54 us -> 56.8 us  [tiles(): pl.pallas_call(functools.partial(tiles_kernel, step, offset is not None,...]
    ppermute x19 -> x20, starting transfers between devices: 49.2 us -> 50.4 us  [line(): go = lambda block, pairs: lax.ppermute(block, 'col', pairs)]
  transfers between devices with their start and end apart: 21 -> 22, of which waited for: 11 -> 13; matrix products, arithmetic and copies ran while one was open for 7% -> 7% of each run, Pallas kernels for 12% -> 13%
where the time goes in v5:
time: 446 us; the launch traced here: 443 us
  waiting for transfers between devices  268 us (60%)
  Pallas kernels  68.2 us (15%)
  starting transfers between devices  50.4 us (11%)
  local copies, waits for them, and re-layouts  27.9 us (6%)
  between operations  16.8 us (4%)
  other arithmetic  12.1 us (3%)
    ppermute x20, waiting for transfers between devices, line(): go = lambda block, pairs: lax.ppermute(block, 'col', pairs)  258 us
    pallas_call x8, Pallas kernels, tiles(): pl.pallas_call(functools.partial(tiles_kernel, step, offset is not None,...  56.8 us
    ppermute x20, starting transfers between devices, line(): go = lambda block, pairs: lax.ppermute(block, 'col', pairs)  50.4 us
    slice x8, local copies, waits for them, and re-layouts, line(): cut = lambda array, at, n: lax.slice_in_dim(array, at, at + n, axis=0)  17.3 us
    pallas_call x1, Pallas kernels, norm(): pl.pallas_call(functools.partial(norm_kernel, len(shared), len(own)), gri...  11.4 us
    all_gather x2, waiting for transfers between devices, line(): rows_of = lambda block: lax.all_gather(block, 'row', axis=0, tiled=False)  9.27 us
  transfers between devices with their start and end apart: 22, of which 13 were waited for; matrix products, arithmetic and copies ran while one was open for 7% of the time, Pallas kernels for 13%

profile of v5, /device:TPU:0, one launch (start us, length us, event | category | flops | bytes accessed | tf_op | source)
XLA Modules:
  0.0 443.1 jit_solution(13471226630021604263)
XLA Ops:
  7.3 2.6 slice.54
  10.0 3.1 collective-permute-start
  14.1 5.1 %slice.55.refs_0_ = bf16[32,256,256]{2,1,0:T(8,128)(2,1)} slice(bf16[64,256,256]{2,1,0:T(8,128)(2,1)} %refs_0_.2), slice={[32:64], [0:256], [0:256]} | slice | bytes 8388608 | tf_op jit(solution)/shard_map/slice | solution.py:203
  19.3 2.6 slice.57
  22.3 81.3 %collective-permute-done.refs_1_ = bf16[32,256,256]{2,1,0:T(8,128)(2,1)S(1)} collective-permute-done((bf16[32,256,256]{2,1,0:T(8,128)(2,1)S(1)}, bf16[32,256,256]{2,1,0:T(8,128)(2,1)S(1)}, u32[]{:S(2)}, u32[]{:S(2)}) %collective-permute-start) | collective-permute-done | bytes 4194336 | tf_op jit(solution)/shard_map/ppermute | solution.py:205
  103.6 1.3 collective-permute-start.2
  105.6 2.6 collective-permute-start.3
  108.3 9.5 %collective-permute-start.9 = (bf16[32,256,256]{2,1,0:T(8,128)(2,1)S(1)}, bf16[32,256,256]{2,1,0:T(8,128)(2,1)}, u32[]{:S(2)}, u32[]{:S(2)}) collective-permute-start(bf16[32,256,256]{2,1,0:T(8,128)(2,1)S(1)} %slice.58), channel_id=1, source_target_pairs={{0,1},{3,2},{4,5},{7,6},{8,9},{11,10},{12,13},{15,14},{16,17},{19,... | collective-permute-start | bytes 12582920 | tf_op jit(solution)/shard_map/ppermute | solution.py:205
  117.8 82.1 %collective-permute-done.2.refs_3_ = bf16[32,256,256]{2,1,0:T(8,128)(2,1)S(1)} collective-permute-done((bf16[32,256,256]{2,1,0:T(8,128)(2,1)S(1)}, bf16[32,256,256]{2,1,0:T(8,128)(2,1)S(1)}, u32[]{:S(2)}, u32[]{:S(2)}) %collective-permute-start.2) | collective-permute-done | bytes 4194336 | tf_op jit(solution)/shard_map/ppermute | solution.py:205
  199.9 2.0 copy-done.11
  201.9 2.3 collective-permute-done.9
  204.3 5.5 %collective-permute-start.5 = (bf16[8,256,256]{2,1,0:T(8,128)(2,1)S(1)}, bf16[8,256,256]{2,1,0:T(8,128)(2,1)}, u32[]{:S(2)}, u32[]{:S(2)}) collective-permute-start(bf16[8,256,256]{2,1,0:T(8,128)(2,1)S(1)} %slice.56), channel_id=1, source_target_pairs={{0,1},{3,2},{4,5},{7,6},{8,9},{11,10},{12,13},{15,14},{16,17},{19,... | collective-permute-start | bytes 3145736 | tf_op jit(solution)/shard_map/ppermute | solution.py:205
  209.7 2.6 collective-permute-start.6
  212.4 1.7 slice.59
  214.1 1.3 collective-permute-start.4
  215.4 13.5 %collective-permute-done.5.refs_1_ = bf16[8,256,256]{2,1,0:T(8,128)(2,1)} collective-permute-done((bf16[8,256,256]{2,1,0:T(8,128)(2,1)S(1)}, bf16[8,256,256]{2,1,0:T(8,128)(2,1)}, u32[]{:S(2)}, u32[]{:S(2)}) %collective-permute-start.5) | collective-permute-done | bytes 1048608 | tf_op jit(solution)/shard_map/ppermute | solution.py:205
  228.9 4.7 %collective-permute-start.11 = (bf16[24,256,256]{2,1,0:T(8,128)(2,1)}, bf16[24,256,256]{2,1,0:T(8,128)(2,1)S(1)}, u32[]{:S(2)}, u32[]{:S(2)}) collective-permute-start(bf16[24,256,256]{2,1,0:T(8,128)(2,1)} %slice.57), channel_id=1, source_target_pairs={{0,1},{3,2},{4,5},{7,6},{8,9},{11,10},{12,13},{15,14},{16,17},{19,... | collective-permute-start | bytes 9437192 | tf_op jit(solution)/shard_map/ppermute | solution.py:205
  233.6 27.3 %collective-permute-done.4.refs_5_ = bf16[16,256,256]{2,1,0:T(8,128)(2,1)S(1)} collective-permute-done((bf16[16,256,256]{2,1,0:T(8,128)(2,1)S(1)}, bf16[16,256,256]{2,1,0:T(8,128)(2,1)S(1)}, u32[]{:S(2)}, u32[]{:S(2)}) %collective-permute-start.4) | collective-permute-done | bytes 2097184 | tf_op jit(solution)/shard_map/ppermute | solution.py:205
  260.8 1.3 copy-done.5
  262.1 3.1 slice.60
  265.2 1.3 collective-permute-start.8
  266.6 1.6 copy-done.6
  268.1 9.7 %tiles.8.refs_0_ = f32[16,256,256]{2,1,0:T(8,128)} custom-call(s32[4]{0:T(128)S(1)} %fusion.order, s32[1]{0:T(128)} %bitcast.inner, bf16[64,256,256]{2,1,0:T(8,128)(2,1)} %refs_0_.2, bf16[32,256,256]{2,1,0:T(8,128)(2,1)} %copy-done.9, bf16[32,256,256]{2,1,0:T(8,128)(2,1)} %copy-done.10, bf16[32,256,256]{2,1,0:T(8,128)(2,1)} %copy-done.11, ...), custom_call_target="tpu_custom_call" | custom-call | flops 2147483648 | bytes 20971520 | tf_op jit(solution)/shard_map/tiles/pallas_call | solution.py:108
  277.9 3.2 reduce_sum.45
  281.1 1.8 fusion.1
  283.6 14.2 %collective-permute-done.11.refs_1_.refs_2_ = bf16[24,256,256]{2,1,0:T(8,128)(2,1)S(1)} collective-permute-done((bf16[24,256,256]{2,1,0:T(8,128)(2,1)}, bf16[24,256,256]{2,1,0:T(8,128)(2,1)S(1)}, u32[]{:S(2)}, u32[]{:S(2)}) %collective-permute-start.11) | collective-permute-done | bytes 3145760 | tf_op jit(solution)/shard_map/ppermute | solution.py:205
  297.8 8.0 %collective-permute-start.10 = (f16[256,256]{1,0:T(8,128)(2,1)S(1)}, f16[256,256]{1,0:T(8,128)(2,1)S(1)}, u32[]{:S(2)}, u32[]{:S(2)}) collective-permute-start(f16[256,256]{1,0:T(8,128)(2,1)S(1)} %get-tuple-element.80), channel_id=1, source_target_pairs={{0,1},{3,2},{4,5},{7,6},{8,9},{11,10},{12,13},{15,14},{16,17},{19,... | collective-permute-start | bytes 393224 | tf_op jit(solution)/shard_map/ppermute | solution.py:205
  305.8 1.7 fusion.2
  309.3 2.1 collective-permute-done.8.refs_5_
  311.4 9.3 %all-gather.7.cloned.1.call-done = bf16[128,256,256]{2,1,0:T(8,128)(2,1)} async-done(((bf16[32,256,256]{2,1,0:T(8,128)(2,1)}), bf16[128,256,256]{2,1,0:T(8,128)(2,1)}) %all-gather.7.cloned.1.call-update) | async-done | bytes 16777232 | tf_op jit(solution)/shard_map/all_gather | solution.py:206
  321.9 4.7 %tiles.9 = (f32[8,256,256]{2,1,0:T(8,128)S(1)}, f32[8,128]{1,0:T(8,128)S(1)}) custom-call(s32[4]{0:T(128)S(1)} %fusion.order, s32[1]{0:T(128)} %bitcast.inner, bf16[32,256,256]{2,1,0:T(8,128)(2,1)} %slice.55.refs_0_, bf16[8,256,256]{2,1,0:T(8,128)(2,1)} %collective-permute-done.5.refs_1_, bf16[32,256,256]{2,1,0:T(8,128)(2,1)} %collective-permute-done.6.refs_2_.refs_3_, ...), custom_call_target="tpu_custom_call" | custom-call | flops 1073741824 | bytes 10485760 | tf_op jit(solution)/shard_map/tiles/pallas_call | solution.py:108
  328.3 1.3 collective-permute-start.14
  330.3 10.0 %tiles.10.refs_1_ = f32[16,256,256]{2,1,0:T(8,128)} custom-call(s32[4]{0:T(128)S(1)} %fusion.order, s32[1]{0:T(128)} %bitcast.inner, bf16[64,256,256]{2,1,0:T(8,128)(2,1)} %refs_0_.2, bf16[32,256,256]{2,1,0:T(8,128)(2,1)} %copy-done.9, bf16[32,256,256]{2,1,0:T(8,128)(2,1)} %copy-done.10, bf16[32,256,256]{2,1,0:T(8,128)(2,1)} %copy-done.11, ...), custom_call_target="tpu_custom_call" | custom-call | flops 2147483648 | bytes 20971520 | tf_op jit(solution)/shard_map/tiles/pallas_call | solution.py:108
  340.3 5.0 %tiles.11 = (f32[8,256,256]{2,1,0:T(8,128)S(1)}, f32[8,128]{1,0:T(8,128)S(1)}) custom-call(s32[4]{0:T(128)S(1)} %fusion.order, s32[1]{0:T(128)} %bitcast.inner, bf16[32,256,256]{2,1,0:T(8,128)(2,1)} %slice.55.refs_0_, bf16[24,256,256]{2,1,0:T(8,128)(2,1)} %copy-done, bf16[32,256,256]{2,1,0:T(8,128)(2,1)} %collective-permute-done.6.refs_2_.refs_3_, ...), custom_call_target="tpu_custom_call" | custom-call | flops 1073741824 | bytes 10485760 | tf_op jit(solution)/shard_map/tiles/pallas_call | solution.py:108
  346.5 1.3 multiply_convert_fusion.2
  347.8 7.7 %collective-permute-done.14 = f16[8,256,256]{2,1,0:T(8,128)(2,1)S(1)} collective-permute-done((f16[8,256,256]{2,1,0:T(8,128)(2,1)S(1)}, f16[8,256,256]{2,1,0:T(8,128)(2,1)S(1)}, u32[]{:S(2)}, u32[]{:S(2)}) %collective-permute-start.14) | collective-permute-done | bytes 1048608 | tf_op jit(solution)/shard_map/ppermute | solution.py:205
  355.5 1.3 collective-permute-start.16
  358.8 4.8 %tiles.12 = (f32[8,256,256]{2,1,0:T(8,128)S(1)}, f32[8,128]{1,0:T(8,128)S(1)}) custom-call(s32[4]{0:T(128)S(1)} %fusion.order, s32[1]{0:T(128)} %bitcast.inner, bf16[32,256,256]{2,1,0:T(8,128)(2,1)} %slice.55.refs_0_, bf16[24,256,256]{2,1,0:T(8,128)(2,1)} %copy-done, bf16[32,256,256]{2,1,0:T(8,128)(2,1)} %collective-permute-done.6.refs_2_.refs_3_, ...), custom_call_target="tpu_custom_call" | custom-call | flops 1073741824 | bytes 10485760 | tf_op jit(solution)/shard_map/tiles/pallas_call | solution.py:108
  364.9 14.1 %collective-permute-done.16 = f16[8,256,256]{2,1,0:T(8,128)(2,1)S(1)} collective-permute-done((f16[8,256,256]{2,1,0:T(8,128)(2,1)}, f16[8,256,256]{2,1,0:T(8,128)(2,1)S(1)}, u32[]{:S(2)}, u32[]{:S(2)}) %collective-permute-start.16) | collective-permute-done | bytes 1048608 | tf_op jit(solution)/shard_map/ppermute | solution.py:205
  379.0 1.5 collective-permute-start.18
  380.5 9.2 %tiles.13.refs_2_ = f32[16,256,256]{2,1,0:T(8,128)} custom-call(s32[4]{0:T(128)S(1)} %fusion.order, s32[1]{0:T(128)} %bitcast.inner, bf16[32,256,256]{2,1,0:T(8,128)(2,1)} %slice.55.refs_0_, bf16[8,256,256]{2,1,0:T(8,128)(2,1)} %collective-permute-done.5.refs_1_, bf16[24,256,256]{2,1,0:T(8,128)(2,1)} %copy-done, ...), custom_call_target="tpu_custom_call" | custom-call | flops 2147483648 | bytes 20971520 | tf_op jit(solution)/shard_map/tiles/pallas_call | solution.py:108
  389.7 4.8 %tiles.14 = (f32[8,256,256]{2,1,0:T(8,128)S(1)}, f32[8,128]{1,0:T(8,128)S(1)}) custom-call(s32[4]{0:T(128)S(1)} %fusion.order, s32[1]{0:T(128)} %bitcast.inner, bf16[32,256,256]{2,1,0:T(8,128)(2,1)} %slice.55.refs_0_, bf16[24,256,256]{2,1,0:T(8,128)(2,1)} %copy-done, bf16[32,256,256]{2,1,0:T(8,128)(2,1)} %collective-permute-done.6.refs_2_.refs_3_, ...), custom_call_target="tpu_custom_call" | custom-call | flops 1073741824 | bytes 10485760 | tf_op jit(solution)/shard_map/tiles/pallas_call | solution.py:108
  395.9 1.3 collective-permute-start.17
  397.5 5.1 %collective-permute-done.17 = f32[32,128]{1,0:T(8,128)S(1)} collective-permute-done((f32[32,128]{1,0:T(8,128)S(1)}, f32[32,128]{1,0:T(8,128)S(1)}, u32[]{:S(2)}, u32[]{:S(2)}) %collective-permute-start.17) | collective-permute-done | bytes 16416 | tf_op jit(solution)/shard_map/ppermute | solution.py:205
  402.6 1.3 collective-permute-start.19
  403.9 8.7 %tiles.15.refs_3_ = f32[16,256,256]{2,1,0:T(8,128)} custom-call(s32[4]{0:T(128)S(1)} %fusion.order, s32[1]{0:T(128)} %bitcast.inner, bf16[32,256,256]{2,1,0:T(8,128)(2,1)} %slice.55.refs_0_, bf16[24,256,256]{2,1,0:T(8,128)(2,1)S(1)} %copy-done.1, bf16[32,256,256]{2,1,0:T(8,128)(2,1)} %collective-permute-done.6.refs_2_.refs_3_, ...), custom_call_target="tpu_custom_call" | custom-call | flops 2147483648 | bytes 20971520 | tf_op jit(solution)/shard_map/tiles/pallas_call | solution.py:108
  416.0 7.9 %collective-permute-done.19 = f16[8,256,256]{2,1,0:T(8,128)(2,1)S(1)} collective-permute-done((f16[8,256,256]{2,1,0:T(8,128)(2,1)S(1)}, f16[8,256,256]{2,1,0:T(8,128)(2,1)S(1)}, u32[]{:S(2)}, u32[]{:S(2)}) %collective-permute-start.19) | collective-permute-done | bytes 1048608 | tf_op jit(solution)/shard_map/ppermute | solution.py:205
  424.9 11.4 %norm.1 = f32[64,256,256]{2,1,0:T(8,128)} custom-call(s32[1]{0:T(128)} %bitcast.inner, f32[256,256]{1,0:T(8,128)S(1)} %get-tuple-element.84.offset, f32[256,256]{1,0:T(8,128)S(1)} %add.14.first, f32[256,256]{1,0:T(8,128)S(1)} %add.15.second, f32[16,256,256]{2,1,0:T(8,128)} %tiles.8.refs_0_, f32[16,256,256]{2,1,0:T(8,128)} %tiles.10.refs_1_, ...), custom_call_target="tpu_custom_call" | custom-call | flops 20971520 | bytes 33554432 | tf_op jit(solution)/shard_map/norm/pallas_call | solution.py:169
  (74 shorter events, 16.8 us)
Async XLA Ops:
  6.5 255.6 %all-gather.5.cloned.1.call-start = ((), (), s32[]{:S(2)}) async-start(), calls=%async_computation | async-start | bytes 41943040 | tf_op jit(solution)/shard_map/all_gather | solution.py:206
  7.3 313.4 %all-gather.7.cloned.1.call-start = ((), (), s32[]{:S(2)}) async-start(), calls=%async_computation.1 | async-start | bytes 20971520 | tf_op jit(solution)/shard_map/all_gather | solution.py:206
  7.3 11.9 %slice-start = ((s8[8388608]{0:T(1024)(128)(4,1)}), s8[4194304]{0:T(1024)(128)(4,1)S(1)}, s32[]{:S(2)}) async-start(s8[8388608]{0:T(1024)(128)(4,1)} %bitcast.19), calls=%async_computation.2 | async-start | bytes 8388608
  7.3 14.6 %slice-start.2 = ((s8[8388608]{0:T(1024)(128)(4,1)}), s8[4194304]{0:T(1024)(128)(4,1)S(1)}, s32[]{:S(2)}) async-start(s8[8388608]{0:T(1024)(128)(4,1)} %bitcast.21), calls=%async_computation.4 | async-start | bytes 8388608
  9.9 9.3 %slice-start.1 = ((s8[8388608]{0:T(1024)(128)(4,1)}), s8[4194304]{0:T(1024)(128)(4,1)S(1)}, s32[]{:S(2)}) async-start(s8[8388608]{0:T(1024)(128)(4,1)} %bitcast.19), calls=%async_computation.3 | async-start | bytes 8388608
  10.0 11.9 %slice-start.3 = ((s8[8388608]{0:T(1024)(128)(4,1)}), s8[4194304]{0:T(1024)(128)(4,1)S(1)}, s32[]{:S(2)}) async-start(s8[8388608]{0:T(1024)(128)(4,1)} %bitcast.21), calls=%async_computation.5 | async-start | bytes 8388608
  10.0 93.7 %collective-permute-start = (bf16[32,256,256]{2,1,0:T(8,128)(2,1)S(1)}, bf16[32,256,256]{2,1,0:T(8,128)(2,1)S(1)}, u32[]{:S(2)}, u32[]{:S(2)}) collective-permute-start(bf16[32,256,256]{2,1,0:T(8,128)(2,1)S(1)} %slice.54), channel_id=1, source_target_pairs={{0,1},{1,0},{2,3},{3,2},{4,5},{5,4},{6,7},{7,6},{8,9},{9,8},{10,11... | collective-permute-start | bytes 12582920 | tf_op jit(solution)/shard_map/ppermute | solution.py:205
  13.1 90.6 %collective-permute-start.1 = (bf16[32,256,256]{2,1,0:T(8,128)(2,1)S(1)}, bf16[32,256,256]{2,1,0:T(8,128)(2,1)S(1)}, u32[]{:S(2)}, u32[]{:S(2)}) collective-permute-start(bf16[32,256,256]{2,1,0:T(8,128)(2,1)S(1)} %slice.54), channel_id=1, source_target_pairs={{1,2},{2,1},{5,6},{6,5},{9,10},{10,9},{13,14},{14,13},{17,18},{18,... | collective-permute-start | bytes 12582920 | tf_op jit(solution)/shard_map/ppermute | solution.py:205
  103.6 2.0 copy-start.9
  103.6 96.2 %copy-start.10 = (bf16[32,256,256]{2,1,0:T(8,128)(2,1)}, bf16[32,256,256]{2,1,0:T(8,128)(2,1)S(1)}, u32[]{:S(2)}) copy-start(bf16[32,256,256]{2,1,0:T(8,128)(2,1)S(1)} %collective-permute-done.1.refs_2_) | copy-start | bytes 12582916
  103.6 96.2 %collective-permute-start.2 = (bf16[32,256,256]{2,1,0:T(8,128)(2,1)S(1)}, bf16[32,256,256]{2,1,0:T(8,128)(2,1)S(1)}, u32[]{:S(2)}, u32[]{:S(2)}) collective-permute-start(bf16[32,256,256]{2,1,0:T(8,128)(2,1)S(1)} %collective-permute-done.1.refs_2_), channel_id=1, source_target_pairs={{1,0},{2,3},{5,4},{6,7},{9,8},{10,11},{13,12},{14,15},{17,16},{18,... | collective-permute-start | bytes 12582920 | tf_op jit(solution)/shard_map/ppermute | solution.py:205
  105.6 94.2 %collective-permute-start.3 = (bf16[32,256,256]{2,1,0:T(8,128)(2,1)S(1)}, bf16[32,256,256]{2,1,0:T(8,128)(2,1)}, u32[]{:S(2)}, u32[]{:S(2)}) collective-permute-start(bf16[32,256,256]{2,1,0:T(8,128)(2,1)S(1)} %collective-permute-done.refs_1_), channel_id=1, source_target_pairs={{1,2},{2,1},{5,6},{6,5},{9,10},{10,9},{13,14},{14,13},{17,18},{18,... | collective-permute-start | bytes 12582920 | tf_op jit(solution)/shard_map/ppermute | solution.py:205
  108.3 95.9 %collective-permute-start.9 = (bf16[32,256,256]{2,1,0:T(8,128)(2,1)S(1)}, bf16[32,256,256]{2,1,0:T(8,128)(2,1)}, u32[]{:S(2)}, u32[]{:S(2)}) collective-permute-start(bf16[32,256,256]{2,1,0:T(8,128)(2,1)S(1)} %slice.58), channel_id=1, source_target_pairs={{0,1},{3,2},{4,5},{7,6},{8,9},{11,10},{12,13},{15,14},{16,17},{19,... | collective-permute-start | bytes 12582920 | tf_op jit(solution)/shard_map/ppermute | solution.py:205
  199.9 2.0 copy-start.11
  204.3 24.6 %collective-permute-start.5 = (bf16[8,256,256]{2,1,0:T(8,128)(2,1)S(1)}, bf16[8,256,256]{2,1,0:T(8,128)(2,1)}, u32[]{:S(2)}, u32[]{:S(2)}) collective-permute-start(bf16[8,256,256]{2,1,0:T(8,128)(2,1)S(1)} %slice.56), channel_id=1, source_target_pairs={{0,1},{3,2},{4,5},{7,6},{8,9},{11,10},{12,13},{15,14},{16,17},{19,... | collective-permute-start | bytes 3145736 | tf_op jit(solution)/shard_map/ppermute | solution.py:205
  209.7 73.8 %collective-permute-start.6 = (bf16[32,256,256]{2,1,0:T(8,128)(2,1)}, bf16[32,256,256]{2,1,0:T(8,128)(2,1)}, u32[]{:S(2)}, u32[]{:S(2)}) collective-permute-start(bf16[32,256,256]{2,1,0:T(8,128)(2,1)} %slice.55.refs_0_), channel_id=1, source_target_pairs={{1,2},{2,1},{5,6},{6,5},{9,10},{10,9},{13,14},{14,13},{17,18},{18,... | collective-permute-start | bytes 12582920 | tf_op jit(solution)/shard_map/ppermute | solution.py:205
  214.1 46.7 %collective-permute-start.4 = (bf16[16,256,256]{2,1,0:T(8,128)(2,1)S(1)}, bf16[16,256,256]{2,1,0:T(8,128)(2,1)S(1)}, u32[]{:S(2)}, u32[]{:S(2)}) collective-permute-start(bf16[16,256,256]{2,1,0:T(8,128)(2,1)S(1)} %slice.59), channel_id=1, source_target_pairs={{1,0},{2,3},{5,4},{6,7},{9,8},{10,11},{13,12},{14,15},{17,16},{18,... | collective-permute-start | bytes 6291464 | tf_op jit(solution)/shard_map/ppermute | solution.py:205
  228.9 68.9 %collective-permute-start.11 = (bf16[24,256,256]{2,1,0:T(8,128)(2,1)}, bf16[24,256,256]{2,1,0:T(8,128)(2,1)S(1)}, u32[]{:S(2)}, u32[]{:S(2)}) collective-permute-start(bf16[24,256,256]{2,1,0:T(8,128)(2,1)} %slice.57), channel_id=1, source_target_pairs={{0,1},{3,2},{4,5},{7,6},{8,9},{11,10},{12,13},{15,14},{16,17},{19,... | collective-permute-start | bytes 9437192 | tf_op jit(solution)/shard_map/ppermute | solution.py:205
  260.8 1.3 copy-start.5
  262.1 4.4 copy-start.13
  265.2 46.2 %collective-permute-start.8 = (bf16[16,256,256]{2,1,0:T(8,128)(2,1)}, bf16[16,256,256]{2,1,0:T(8,128)(2,1)}, u32[]{:S(2)}, u32[]{:S(2)}) collective-permute-start(bf16[16,256,256]{2,1,0:T(8,128)(2,1)} %slice.60), channel_id=1, source_target_pairs={{1,0},{2,3},{5,4},{6,7},{9,8},{10,11},{13,12},{14,15},{17,16},{18,... | collective-permute-start | bytes 6291464 | tf_op jit(solution)/shard_map/ppermute | solution.py:205
  266.6 1.6 copy-start.6
  282.9 25.4 %collective-permute-start.7 = (bf16[8,256,256]{2,1,0:T(8,128)(2,1)}, bf16[8,256,256]{2,1,0:T(8,128)(2,1)S(1)}, u32[]{:S(2)}, u32[]{:S(2)}) collective-permute-start(bf16[8,256,256]{2,1,0:T(8,128)(2,1)} %collective-permute-done.5.refs_1_), channel_id=1, source_target_pairs={{1,2},{2,1},{5,6},{6,5},{9,10},{10,9},{13,14},{14,13},{17,18},{18,... | collective-permute-start | bytes 3145736 | tf_op jit(solution)/shard_map/ppermute | solution.py:205
  297.8 9.7 %copy-start = (bf16[24,256,256]{2,1,0:T(8,128)(2,1)}, bf16[24,256,256]{2,1,0:T(8,128)(2,1)S(1)}, u32[]{:S(2)}) copy-start(bf16[24,256,256]{2,1,0:T(8,128)(2,1)S(1)} %collective-permute-done.11.refs_1_.refs_2_) | copy-start | bytes 9437188
  297.8 10.5 %collective-permute-start.10 = (f16[256,256]{1,0:T(8,128)(2,1)S(1)}, f16[256,256]{1,0:T(8,128)(2,1)S(1)}, u32[]{:S(2)}, u32[]{:S(2)}) collective-permute-start(f16[256,256]{1,0:T(8,128)(2,1)S(1)} %get-tuple-element.80), channel_id=1, source_target_pairs={{0,1},{3,2},{4,5},{7,6},{8,9},{11,10},{12,13},{15,14},{16,17},{19,... | collective-permute-start | bytes 393224 | tf_op jit(solution)/shard_map/ppermute | solution.py:205
  307.5 32.8 %collective-permute-start.13 = (bf16[8,256,256]{2,1,0:T(8,128)(2,1)}, bf16[8,256,256]{2,1,0:T(8,128)(2,1)S(1)}, u32[]{:S(2)}, u32[]{:S(2)}) collective-permute-start(bf16[8,256,256]{2,1,0:T(8,128)(2,1)} %get-tuple-element.82), channel_id=1, source_target_pairs={{1,2},{2,1},{5,6},{6,5},{9,10},{10,9},{13,14},{14,13},{17,18},{18,... | collective-permute-start | bytes 3145736 | tf_op jit(solution)/shard_map/ppermute | solution.py:205
  308.3 1.0 copy-start.2
  320.7 1.2 copy-start.3
  328.3 27.2 %collective-permute-start.14 = (f16[8,256,256]{2,1,0:T(8,128)(2,1)S(1)}, f16[8,256,256]{2,1,0:T(8,128)(2,1)S(1)}, u32[]{:S(2)}, u32[]{:S(2)}) collective-permute-start(f16[8,256,256]{2,1,0:T(8,128)(2,1)S(1)} %multiply_convert_fusion.3), channel_id=1, source_target_pairs={{1,0},{2,3},{5,4},{6,7},{9,8},{10,11},{13,12},{14,15},{17,16},{18,... | collective-permute-start | bytes 3145736 | tf_op jit(solution)/shard_map/ppermute | solution.py:205
  329.6 29.2 %collective-permute-start.12 = (bf16[8,256,256]{2,1,0:T(8,128)(2,1)}, bf16[8,256,256]{2,1,0:T(8,128)(2,1)S(1)}, u32[]{:S(2)}, u32[]{:S(2)}) collective-permute-start(bf16[8,256,256]{2,1,0:T(8,128)(2,1)} %get-tuple-element.83), channel_id=1, source_target_pairs={{1,2},{2,1},{5,6},{6,5},{9,10},{10,9},{13,14},{14,13},{17,18},{18,... | collective-permute-start | bytes 3145736 | tf_op jit(solution)/shard_map/ppermute | solution.py:205
  340.3 17.2 %copy-start.7 = (f32[16,256,256]{2,1,0:T(8,128)S(1)}, f32[16,256,256]{2,1,0:T(8,128)}, u32[]{:S(2)}) copy-start(f32[16,256,256]{2,1,0:T(8,128)} %tiles.8.refs_0_) | copy-start | bytes 12582916
  340.3 17.2 %copy-start.8 = (f32[16,256,256]{2,1,0:T(8,128)S(1)}, f32[16,256,256]{2,1,0:T(8,128)}, u32[]{:S(2)}) copy-start(f32[16,256,256]{2,1,0:T(8,128)} %tiles.10.refs_1_) | copy-start | bytes 12582916
  355.5 23.5 %collective-permute-start.16 = (f16[8,256,256]{2,1,0:T(8,128)(2,1)}, f16[8,256,256]{2,1,0:T(8,128)(2,1)S(1)}, u32[]{:S(2)}, u32[]{:S(2)}) collective-permute-start(f16[8,256,256]{2,1,0:T(8,128)(2,1)} %multiply_convert_fusion.2), channel_id=1, source_target_pairs={{1,0},{2,3},{5,4},{6,7},{9,8},{10,11},{13,12},{14,15},{17,16},{18,... | collective-permute-start | bytes 3145736 | tf_op jit(solution)/shard_map/ppermute | solution.py:205
  356.8 32.9 %collective-permute-start.15 = (bf16[8,256,256]{2,1,0:T(8,128)(2,1)}, bf16[8,256,256]{2,1,0:T(8,128)(2,1)S(1)}, u32[]{:S(2)}, u32[]{:S(2)}) collective-permute-start(bf16[8,256,256]{2,1,0:T(8,128)(2,1)} %get-tuple-element.81), channel_id=1, source_target_pairs={{1,2},{2,1},{5,6},{6,5},{9,10},{10,9},{13,14},{14,13},{17,18},{18,... | collective-permute-start | bytes 3145736 | tf_op jit(solution)/shard_map/ppermute | solution.py:205
  363.5 17.0 %copy-start.4 = (bf16[8,256,256]{2,1,0:T(8,128)(2,1)S(1)}, bf16[8,256,256]{2,1,0:T(8,128)(2,1)}, u32[]{:S(2)}) copy-start(bf16[8,256,256]{2,1,0:T(8,128)(2,1)} %copy-done.2) | copy-start | bytes 3145732
  379.0 23.6 %collective-permute-start.18 = (f16[8,256,256]{2,1,0:T(8,128)(2,1)S(1)}, f16[8,256,256]{2,1,0:T(8,128)(2,1)S(1)}, u32[]{:S(2)}, u32[]{:S(2)}) collective-permute-start(f16[8,256,256]{2,1,0:T(8,128)(2,1)S(1)} %multiply_convert_fusion.1), channel_id=1, source_target_pairs={{1,0},{2,3},{5,4},{6,7},{9,8},{10,11},{13,12},{14,15},{17,16},{18,... | collective-permute-start | bytes 3145736 | tf_op jit(solution)/shard_map/ppermute | solution.py:205
  394.4 9.5 %copy-start.1 = (bf16[24,256,256]{2,1,0:T(8,128)(2,1)S(1)}, bf16[24,256,256]{2,1,0:T(8,128)(2,1)}, u32[]{:S(2)}) copy-start(bf16[24,256,256]{2,1,0:T(8,128)(2,1)} %copy-done) | copy-start | bytes 9437188
  395.9 6.7 %collective-permute-start.17 = (f32[32,128]{1,0:T(8,128)S(1)}, f32[32,128]{1,0:T(8,128)S(1)}, u32[]{:S(2)}, u32[]{:S(2)}) collective-permute-start(f32[32,128]{1,0:T(8,128)S(1)} %pad_maximum_fusion), channel_id=1, source_target_pairs={{1,0},{2,3},{5,4},{6,7},{9,8},{10,11},{13,12},{14,15},{17,16},{18,... | collective-permute-start | bytes 49160 | tf_op jit(solution)/shard_map/ppermute | solution.py:205
  397.5 15.7 %copy-start.12 = (f32[256,256]{1,0:T(8,128)S(1)}, f32[256,256]{1,0:T(8,128)}, u32[]{:S(2)}) copy-start(f32[256,256]{1,0:T(8,128)} %get-tuple-element.79) | copy-start | bytes 786436
  402.6 21.3 %collective-permute-start.19 = (f16[8,256,256]{2,1,0:T(8,128)(2,1)S(1)}, f16[8,256,256]{2,1,0:T(8,128)(2,1)S(1)}, u32[]{:S(2)}, u32[]{:S(2)}) collective-permute-start(f16[8,256,256]{2,1,0:T(8,128)(2,1)S(1)} %multiply_convert_fusion), channel_id=1, source_target_pairs={{1,0},{2,3},{5,4},{6,7},{9,8},{10,11},{13,12},{14,15},{17,16},{18,... | collective-permute-start | bytes 3145736 | tf_op jit(solution)/shard_map/ppermute | solution.py:205
Sparse Core Ops, SparseCore 0:
  8.9 204.2 all-gather.4
  214.7 105.9 all-gather.6

commit v6 on v5

--- a/solution.py
+++ b/solution.py
@@ -175,7 +175,7 @@
             out_specs=pl.BlockSpec((channels, step, cols), lambda i, inner: (0, i, 0)),
         ),
         out_shape=jax.ShapeDtypeStruct((channels, rows, cols), jnp.float32),
-        compiler_params=params(44),
+        compiler_params=params(26),
         cost_estimate=pl.CostEstimate(flops=5 * size, bytes_accessed=8 * size, transcendentals=0),
         name="norm",
     )(inner, *stats, *shared, *own, *sent)

time: 446 us -> 444 us (level)
  waiting for transfers between devices: 268 us -> 259 us
  other arithmetic: 12.1 us -> 20.5 us
    ppermute x20, waiting for transfers between devices: 258 us -> 249 us  [line(): go = lambda block, pairs: lax.ppermute(block, 'col', pairs)]
    convert_element_type x4, other arithmetic: 2.1 us -> 7.21 us  [line(): payload = (tile * (1.0 / size[0, 0])).astype(jnp.float16)]
    unnamed x36 -> x52, local copies, waits for them, and re-layouts: 7.89 us -> 10.5 us
  transfers between devices with their start and end apart: 22 -> 22, of which waited for: 13 -> 13; matrix products, arithmetic and copies ran while one was open for 7% -> 9% of each run, Pallas kernels for 13% -> 13%
where the time goes in v6:
time: 444 us; the launch traced here: 443 us
  waiting for transfers between devices  259 us (58%)
  Pallas kernels  65.2 us (15%)
  starting transfers between devices  50.5 us (11%)
  local copies, waits for them, and re-layouts  30.6 us (7%)
  other arithmetic  20.5 us (5%)
  between operations  16.9 us (4%)
    ppermute x20, waiting for transfers between devices, line(): go = lambda block, pairs: lax.ppermute(block, 'col', pairs)  249 us
    pallas_call x8, Pallas kernels, tiles(): pl.pallas_call(functools.partial(tiles_kernel, step, offset is not None,...  56.8 us
    ppermute x20, starting transfers between devices, line(): go = lambda block, pairs: lax.ppermute(block, 'col', pairs)  50.5 us
    slice x8, local copies, waits for them, and re-layouts, line(): cut = lambda array, at, n: lax.slice_in_dim(array, at, at + n, axis=0)  17.3 us
    unnamed x52, local copies, waits for them, and re-layouts  10.5 us
    all_gather x2, waiting for transfers between devices, line(): rows_of = lambda block: lax.all_gather(block, 'row', axis=0, tiled=False)  9.25 us
  transfers between devices with their start and end apart: 22, of which 13 were waited for; matrix products, arithmetic and copies ran while one was open for 9% of the time, Pallas kernels for 13%

profile of v6, /device:TPU:0, one launch (start us, length us, event | category | flops | bytes accessed | tf_op | source)
XLA Modules:
  0.0 442.8 jit_solution(2029725247855368288)
XLA Ops:
  7.3 2.6 slice.54
  10.0 3.1 collective-permute-start
  14.1 5.1 %slice.55.refs_0_ = bf16[32,256,256]{2,1,0:T(8,128)(2,1)} slice(bf16[64,256,256]{2,1,0:T(8,128)(2,1)} %refs_0_.2), slice={[32:64], [0:256], [0:256]} | slice | bytes 8388608 | tf_op jit(solution)/shard_map/slice | solution.py:203
  19.3 2.6 slice.57
  22.3 81.3 %collective-permute-done.refs_1_ = bf16[32,256,256]{2,1,0:T(8,128)(2,1)S(1)} collective-permute-done((bf16[32,256,256]{2,1,0:T(8,128)(2,1)S(1)}, bf16[32,256,256]{2,1,0:T(8,128)(2,1)S(1)}, u32[]{:S(2)}, u32[]{:S(2)}) %collective-permute-start) | collective-permute-done | bytes 4194336 | tf_op jit(solution)/shard_map/ppermute | solution.py:205
  105.6 2.6 collective-permute-start.3
  108.3 9.6 %collective-permute-start.9 = (bf16[32,256,256]{2,1,0:T(8,128)(2,1)S(1)}, bf16[32,256,256]{2,1,0:T(8,128)(2,1)}, u32[]{:S(2)}, u32[]{:S(2)}) collective-permute-start(bf16[32,256,256]{2,1,0:T(8,128)(2,1)S(1)} %slice.58), channel_id=1, source_target_pairs={{0,1},{3,2},{4,5},{7,6},{8,9},{11,10},{12,13},{15,14},{16,17},{19,... | collective-permute-start | bytes 12582920 | tf_op jit(solution)/shard_map/ppermute | solution.py:205
  117.9 82.0 %collective-permute-done.2.refs_3_ = bf16[32,256,256]{2,1,0:T(8,128)(2,1)S(1)} collective-permute-done((bf16[32,256,256]{2,1,0:T(8,128)(2,1)S(1)}, bf16[32,256,256]{2,1,0:T(8,128)(2,1)S(1)}, u32[]{:S(2)}, u32[]{:S(2)}) %collective-permute-start.2) | collective-permute-done | bytes 4194336 | tf_op jit(solution)/shard_map/ppermute | solution.py:205
  199.9 2.0 copy-done.15
  201.8 2.4 collective-permute-done.9
  204.3 5.5 %collective-permute-start.5 = (bf16[8,256,256]{2,1,0:T(8,128)(2,1)S(1)}, bf16[8,256,256]{2,1,0:T(8,128)(2,1)}, u32[]{:S(2)}, u32[]{:S(2)}) collective-permute-start(bf16[8,256,256]{2,1,0:T(8,128)(2,1)S(1)} %slice.56), channel_id=1, source_target_pairs={{0,1},{3,2},{4,5},{7,6},{8,9},{11,10},{12,13},{15,14},{16,17},{19,... | collective-permute-start | bytes 3145736 | tf_op jit(solution)/shard_map/ppermute | solution.py:205
  209.7 2.7 collective-permute-start.6
  212.4 1.7 slice.59
  214.1 1.3 collective-permute-start.4
  215.4 13.4 %collective-permute-done.5.refs_1_ = bf16[8,256,256]{2,1,0:T(8,128)(2,1)} collective-permute-done((bf16[8,256,256]{2,1,0:T(8,128)(2,1)S(1)}, bf16[8,256,256]{2,1,0:T(8,128)(2,1)}, u32[]{:S(2)}, u32[]{:S(2)}) %collective-permute-start.5) | collective-permute-done | bytes 1048608 | tf_op jit(solution)/shard_map/ppermute | solution.py:205
  228.9 4.7 %collective-permute-start.11 = (bf16[24,256,256]{2,1,0:T(8,128)(2,1)}, bf16[24,256,256]{2,1,0:T(8,128)(2,1)S(1)}, u32[]{:S(2)}, u32[]{:S(2)}) collective-permute-start(bf16[24,256,256]{2,1,0:T(8,128)(2,1)} %slice.57), channel_id=1, source_target_pairs={{0,1},{3,2},{4,5},{7,6},{8,9},{11,10},{12,13},{15,14},{16,17},{19,... | collective-permute-start | bytes 9437192 | tf_op jit(solution)/shard_map/ppermute | solution.py:205
  233.6 27.3 %collective-permute-done.4.refs_5_ = bf16[16,256,256]{2,1,0:T(8,128)(2,1)S(1)} collective-permute-done((bf16[16,256,256]{2,1,0:T(8,128)(2,1)S(1)}, bf16[16,256,256]{2,1,0:T(8,128)(2,1)S(1)}, u32[]{:S(2)}, u32[]{:S(2)}) %collective-permute-start.4) | collective-permute-done | bytes 2097184 | tf_op jit(solution)/shard_map/ppermute | solution.py:205
  260.8 1.3 copy-done.9
  262.2 3.1 slice.60
  266.6 1.6 copy-done.10
  268.2 9.7 %tiles.8.refs_0_ = f32[16,256,256]{2,1,0:T(8,128)} custom-call(s32[4]{0:T(128)S(1)} %fusion.order, s32[1]{0:T(128)} %bitcast.inner, bf16[64,256,256]{2,1,0:T(8,128)(2,1)} %refs_0_.2, bf16[32,256,256]{2,1,0:T(8,128)(2,1)} %copy-done.13, bf16[32,256,256]{2,1,0:T(8,128)(2,1)} %copy-done.14, bf16[32,256,256]{2,1,0:T(8,128)(2,1)} %copy-done.15, ...), custom_call_target="tpu_custom_call" | custom-call | flops 2147483648 | bytes 20971520 | tf_op jit(solution)/shard_map/tiles/pallas_call | solution.py:108
  277.9 3.2 reduce_sum.45
  281.0 1.8 fusion.1
  283.6 14.2 %collective-permute-done.11.refs_1_.refs_2_ = bf16[24,256,256]{2,1,0:T(8,128)(2,1)S(1)} collective-permute-done((bf16[24,256,256]{2,1,0:T(8,128)(2,1)}, bf16[24,256,256]{2,1,0:T(8,128)(2,1)S(1)}, u32[]{:S(2)}, u32[]{:S(2)}) %collective-permute-start.11) | collective-permute-done | bytes 3145760 | tf_op jit(solution)/shard_map/ppermute | solution.py:205
  297.8 8.0 %collective-permute-start.10 = (f16[256,256]{1,0:T(8,128)(2,1)S(1)}, f16[256,256]{1,0:T(8,128)(2,1)S(1)}, u32[]{:S(2)}, u32[]{:S(2)}) collective-permute-start(f16[256,256]{1,0:T(8,128)(2,1)S(1)} %get-tuple-element.80), channel_id=1, source_target_pairs={{0,1},{3,2},{4,5},{7,6},{8,9},{11,10},{12,13},{15,14},{16,17},{19,... | collective-permute-start | bytes 393224 | tf_op jit(solution)/shard_map/ppermute | solution.py:205
  305.8 1.7 fusion.2
  309.3 2.1 collective-permute-done.8.refs_5_
  311.4 9.3 %all-gather.7.cloned.1.call-done = bf16[128,256,256]{2,1,0:T(8,128)(2,1)} async-done(((bf16[32,256,256]{2,1,0:T(8,128)(2,1)}), bf16[128,256,256]{2,1,0:T(8,128)(2,1)}) %all-gather.7.cloned.1.call-update) | async-done | bytes 16777232 | tf_op jit(solution)/shard_map/all_gather | solution.py:206
  321.9 4.7 %tiles.9 = (f32[8,256,256]{2,1,0:T(8,128)S(1)}, f32[8,128]{1,0:T(8,128)S(1)}) custom-call(s32[4]{0:T(128)S(1)} %fusion.order, s32[1]{0:T(128)} %bitcast.inner, bf16[32,256,256]{2,1,0:T(8,128)(2,1)} %slice.55.refs_0_, bf16[8,256,256]{2,1,0:T(8,128)(2,1)} %collective-permute-done.5.refs_1_, bf16[32,256,256]{2,1,0:T(8,128)(2,1)} %collective-permute-done.6.refs_2_.refs_3_, ...), custom_call_target="tpu_custom_call" | custom-call | flops 1073741824 | bytes 10485760 | tf_op jit(solution)/shard_map/tiles/pallas_call | solution.py:108
  328.2 1.3 collective-permute-start.14
  330.2 10.1 %tiles.10.refs_1_ = f32[16,256,256]{2,1,0:T(8,128)} custom-call(s32[4]{0:T(128)S(1)} %fusion.order, s32[1]{0:T(128)} %bitcast.inner, bf16[64,256,256]{2,1,0:T(8,128)(2,1)} %refs_0_.2, bf16[32,256,256]{2,1,0:T(8,128)(2,1)} %copy-done.13, bf16[32,256,256]{2,1,0:T(8,128)(2,1)} %copy-done.14, bf16[32,256,256]{2,1,0:T(8,128)(2,1)} %copy-done.15, ...), custom_call_target="tpu_custom_call" | custom-call | flops 2147483648 | bytes 20971520 | tf_op jit(solution)/shard_map/tiles/pallas_call | solution.py:108
  340.3 5.0 %tiles.11 = (f32[8,256,256]{2,1,0:T(8,128)S(1)}, f32[8,128]{1,0:T(8,128)S(1)}) custom-call(s32[4]{0:T(128)S(1)} %fusion.order, s32[1]{0:T(128)} %bitcast.inner, bf16[32,256,256]{2,1,0:T(8,128)(2,1)} %slice.55.refs_0_, bf16[24,256,256]{2,1,0:T(8,128)(2,1)} %copy-done, bf16[32,256,256]{2,1,0:T(8,128)(2,1)} %collective-permute-done.6.refs_2_.refs_3_, ...), custom_call_target="tpu_custom_call" | custom-call | flops 1073741824 | bytes 10485760 | tf_op jit(solution)/shard_map/tiles/pallas_call | solution.py:108
  347.8 7.6 %collective-permute-done.14 = f16[8,256,256]{2,1,0:T(8,128)(2,1)S(1)} collective-permute-done((f16[8,256,256]{2,1,0:T(8,128)(2,1)S(1)}, f16[8,256,256]{2,1,0:T(8,128)(2,1)S(1)}, u32[]{:S(2)}, u32[]{:S(2)}) %collective-permute-start.14) | collective-permute-done | bytes 1048608 | tf_op jit(solution)/shard_map/ppermute | solution.py:205
  358.7 4.8 %tiles.12 = (f32[8,256,256]{2,1,0:T(8,128)S(1)}, f32[8,128]{1,0:T(8,128)S(1)}) custom-call(s32[4]{0:T(128)S(1)} %fusion.order, s32[1]{0:T(128)} %bitcast.inner, bf16[32,256,256]{2,1,0:T(8,128)(2,1)} %slice.55.refs_0_, bf16[24,256,256]{2,1,0:T(8,128)(2,1)} %copy-done, bf16[32,256,256]{2,1,0:T(8,128)(2,1)} %collective-permute-done.6.refs_2_.refs_3_, ...), custom_call_target="tpu_custom_call" | custom-call | flops 1073741824 | bytes 10485760 | tf_op jit(solution)/shard_map/tiles/pallas_call | solution.py:108
  363.4 1.3 copy-done.12
  366.0 2.8 multiply_convert_fusion.1
  368.8 9.9 %collective-permute-done.16 = f16[8,256,256]{2,1,0:T(8,128)(2,1)S(1)} collective-permute-done((f16[8,256,256]{2,1,0:T(8,128)(2,1)}, f16[8,256,256]{2,1,0:T(8,128)(2,1)S(1)}, u32[]{:S(2)}, u32[]{:S(2)}) %collective-permute-start.16) | collective-permute-done | bytes 1048608 | tf_op jit(solution)/shard_map/ppermute | solution.py:205
  378.7 1.5 collective-permute-start.18
  380.2 9.2 %tiles.13.refs_2_ = f32[16,256,256]{2,1,0:T(8,128)} custom-call(s32[4]{0:T(128)S(1)} %fusion.order, s32[1]{0:T(128)} %bitcast.inner, bf16[32,256,256]{2,1,0:T(8,128)(2,1)} %slice.55.refs_0_, bf16[8,256,256]{2,1,0:T(8,128)(2,1)} %collective-permute-done.5.refs_1_, bf16[24,256,256]{2,1,0:T(8,128)(2,1)} %copy-done, ...), custom_call_target="tpu_custom_call" | custom-call | flops 2147483648 | bytes 20971520 | tf_op jit(solution)/shard_map/tiles/pallas_call | solution.py:108
  389.4 4.8 %tiles.14 = (f32[8,256,256]{2,1,0:T(8,128)S(1)}, f32[8,128]{1,0:T(8,128)S(1)}) custom-call(s32[4]{0:T(128)S(1)} %fusion.order, s32[1]{0:T(128)} %bitcast.inner, bf16[32,256,256]{2,1,0:T(8,128)(2,1)} %slice.55.refs_0_, bf16[24,256,256]{2,1,0:T(8,128)(2,1)} %copy-done, bf16[32,256,256]{2,1,0:T(8,128)(2,1)} %collective-permute-done.6.refs_2_.refs_3_, ...), custom_call_target="tpu_custom_call" | custom-call | flops 1073741824 | bytes 10485760 | tf_op jit(solution)/shard_map/tiles/pallas_call | solution.py:108
  394.1 1.3 copy-done.11
  398.3 2.8 multiply_convert_fusion
  401.2 2.4 collective-permute-done.17
  404.9 8.7 %tiles.15.refs_3_ = f32[16,256,256]{2,1,0:T(8,128)} custom-call(s32[4]{0:T(128)S(1)} %fusion.order, s32[1]{0:T(128)} %bitcast.inner, bf16[32,256,256]{2,1,0:T(8,128)(2,1)} %slice.55.refs_0_, bf16[24,256,256]{2,1,0:T(8,128)(2,1)S(1)} %copy-done.1, bf16[32,256,256]{2,1,0:T(8,128)(2,1)} %collective-permute-done.6.refs_2_.refs_3_, ...), custom_call_target="tpu_custom_call" | custom-call | flops 2147483648 | bytes 20971520 | tf_op jit(solution)/shard_map/tiles/pallas_call | solution.py:108
  416.2 2.8 add_multiply_fusion.1.refs_6_
  419.0 6.3 %collective-permute-done.19 = f16[8,256,256]{2,1,0:T(8,128)(2,1)} collective-permute-done((f16[8,256,256]{2,1,0:T(8,128)(2,1)}, f16[8,256,256]{2,1,0:T(8,128)(2,1)}, u32[]{:S(2)}, u32[]{:S(2)}) %collective-permute-start.19) | collective-permute-done | bytes 1048608 | tf_op jit(solution)/shard_map/ppermute | solution.py:205
  425.4 2.2 add_multiply_fusion.refs_7_
  427.6 8.3 %norm.1 = f32[64,256,256]{2,1,0:T(8,128)} custom-call(s32[1]{0:T(128)} %bitcast.inner, f32[256,256]{1,0:T(8,128)S(1)} %get-tuple-element.84.offset, f32[256,256]{1,0:T(8,128)S(1)} %add.14.first, f32[256,256]{1,0:T(8,128)S(1)} %add.15.second, f32[16,256,256]{2,1,0:T(8,128)S(1)} %copy-done.2, f32[16,256,256]{2,1,0:T(8,128)S(1)} %copy-done.3, ...), custom_call_target="tpu_custom_call" | custom-call | flops 20971520 | bytes 33554432 | tf_op jit(solution)/shard_map/norm/pallas_call | solution.py:169
  (90 shorter events, 22.4 us)
Async XLA Ops:
  6.5 255.6 %all-gather.5.cloned.1.call-start = ((), (), s32[]{:S(2)}) async-start(), calls=%async_computation | async-start | bytes 41943040 | tf_op jit(solution)/shard_map/all_gather | solution.py:206
  7.3 313.4 %all-gather.7.cloned.1.call-start = ((), (), s32[]{:S(2)}) async-start(), calls=%async_computation.1 | async-start | bytes 20971520 | tf_op jit(solution)/shard_map/all_gather | solution.py:206
  7.3 11.9 %slice-start = ((s8[8388608]{0:T(1024)(128)(4,1)}), s8[4194304]{0:T(1024)(128)(4,1)S(1)}, s32[]{:S(2)}) async-start(s8[8388608]{0:T(1024)(128)(4,1)} %bitcast.19), calls=%async_computation.2 | async-start | bytes 8388608
  7.3 14.6 %slice-start.2 = ((s8[8388608]{0:T(1024)(128)(4,1)}), s8[4194304]{0:T(1024)(128)(4,1)S(1)}, s32[]{:S(2)}) async-start(s8[8388608]{0:T(1024)(128)(4,1)} %bitcast.21), calls=%async_computation.4 | async-start | bytes 8388608
  9.9 9.3 %slice-start.1 = ((s8[8388608]{0:T(1024)(128)(4,1)}), s8[4194304]{0:T(1024)(128)(4,1)S(1)}, s32[]{:S(2)}) async-start(s8[8388608]{0:T(1024)(128)(4,1)} %bitcast.19), calls=%async_computation.3 | async-start | bytes 8388608
  10.0 11.9 %slice-start.3 = ((s8[8388608]{0:T(1024)(128)(4,1)}), s8[4194304]{0:T(1024)(128)(4,1)S(1)}, s32[]{:S(2)}) async-start(s8[8388608]{0:T(1024)(128)(4,1)} %bitcast.21), calls=%async_computation.5 | async-start | bytes 8388608
  10.0 93.7 %collective-permute-start = (bf16[32,256,256]{2,1,0:T(8,128)(2,1)S(1)}, bf16[32,256,256]{2,1,0:T(8,128)(2,1)S(1)}, u32[]{:S(2)}, u32[]{:S(2)}) collective-permute-start(bf16[32,256,256]{2,1,0:T(8,128)(2,1)S(1)} %slice.54), channel_id=1, source_target_pairs={{0,1},{1,0},{2,3},{3,2},{4,5},{5,4},{6,7},{7,6},{8,9},{9,8},{10,11... | collective-permute-start | bytes 12582920 | tf_op jit(solution)/shard_map/ppermute | solution.py:205
  13.1 90.6 %collective-permute-start.1 = (bf16[32,256,256]{2,1,0:T(8,128)(2,1)S(1)}, bf16[32,256,256]{2,1,0:T(8,128)(2,1)S(1)}, u32[]{:S(2)}, u32[]{:S(2)}) collective-permute-start(bf16[32,256,256]{2,1,0:T(8,128)(2,1)S(1)} %slice.54), channel_id=1, source_target_pairs={{1,2},{2,1},{5,6},{6,5},{9,10},{10,9},{13,14},{14,13},{17,18},{18,... | collective-permute-start | bytes 12582920 | tf_op jit(solution)/shard_map/ppermute | solution.py:205
  103.6 2.0 copy-start.13
  103.6 96.2 %copy-start.14 = (bf16[32,256,256]{2,1,0:T(8,128)(2,1)}, bf16[32,256,256]{2,1,0:T(8,128)(2,1)S(1)}, u32[]{:S(2)}) copy-start(bf16[32,256,256]{2,1,0:T(8,128)(2,1)S(1)} %collective-permute-done.1.refs_2_) | copy-start | bytes 12582916
  103.6 96.2 %collective-permute-start.2 = (bf16[32,256,256]{2,1,0:T(8,128)(2,1)S(1)}, bf16[32,256,256]{2,1,0:T(8,128)(2,1)S(1)}, u32[]{:S(2)}, u32[]{:S(2)}) collective-permute-start(bf16[32,256,256]{2,1,0:T(8,128)(2,1)S(1)} %collective-permute-done.1.refs_2_), channel_id=1, source_target_pairs={{1,0},{2,3},{5,4},{6,7},{9,8},{10,11},{13,12},{14,15},{17,16},{18,... | collective-permute-start | bytes 12582920 | tf_op jit(solution)/shard_map/ppermute | solution.py:205
  105.6 94.2 %collective-permute-start.3 = (bf16[32,256,256]{2,1,0:T(8,128)(2,1)S(1)}, bf16[32,256,256]{2,1,0:T(8,128)(2,1)}, u32[]{:S(2)}, u32[]{:S(2)}) collective-permute-start(bf16[32,256,256]{2,1,0:T(8,128)(2,1)S(1)} %collective-permute-done.refs_1_), channel_id=1, source_target_pairs={{1,2},{2,1},{5,6},{6,5},{9,10},{10,9},{13,14},{14,13},{17,18},{18,... | collective-permute-start | bytes 12582920 | tf_op jit(solution)/shard_map/ppermute | solution.py:205
  108.3 96.0 %collective-permute-start.9 = (bf16[32,256,256]{2,1,0:T(8,128)(2,1)S(1)}, bf16[32,256,256]{2,1,0:T(8,128)(2,1)}, u32[]{:S(2)}, u32[]{:S(2)}) collective-permute-start(bf16[32,256,256]{2,1,0:T(8,128)(2,1)S(1)} %slice.58), channel_id=1, source_target_pairs={{0,1},{3,2},{4,5},{7,6},{8,9},{11,10},{12,13},{15,14},{16,17},{19,... | collective-permute-start | bytes 12582920 | tf_op jit(solution)/shard_map/ppermute | solution.py:205
  199.9 2.0 copy-start.15
  204.3 24.6 %collective-permute-start.5 = (bf16[8,256,256]{2,1,0:T(8,128)(2,1)S(1)}, bf16[8,256,256]{2,1,0:T(8,128)(2,1)}, u32[]{:S(2)}, u32[]{:S(2)}) collective-permute-start(bf16[8,256,256]{2,1,0:T(8,128)(2,1)S(1)} %slice.56), channel_id=1, source_target_pairs={{0,1},{3,2},{4,5},{7,6},{8,9},{11,10},{12,13},{15,14},{16,17},{19,... | collective-permute-start | bytes 3145736 | tf_op jit(solution)/shard_map/ppermute | solution.py:205
  209.7 73.9 %collective-permute-start.6 = (bf16[32,256,256]{2,1,0:T(8,128)(2,1)}, bf16[32,256,256]{2,1,0:T(8,128)(2,1)}, u32[]{:S(2)}, u32[]{:S(2)}) collective-permute-start(bf16[32,256,256]{2,1,0:T(8,128)(2,1)} %slice.55.refs_0_), channel_id=1, source_target_pairs={{1,2},{2,1},{5,6},{6,5},{9,10},{10,9},{13,14},{14,13},{17,18},{18,... | collective-permute-start | bytes 12582920 | tf_op jit(solution)/shard_map/ppermute | solution.py:205
  214.1 46.7 %collective-permute-start.4 = (bf16[16,256,256]{2,1,0:T(8,128)(2,1)S(1)}, bf16[16,256,256]{2,1,0:T(8,128)(2,1)S(1)}, u32[]{:S(2)}, u32[]{:S(2)}) collective-permute-start(bf16[16,256,256]{2,1,0:T(8,128)(2,1)S(1)} %slice.59), channel_id=1, source_target_pairs={{1,0},{2,3},{5,4},{6,7},{9,8},{10,11},{13,12},{14,15},{17,16},{18,... | collective-permute-start | bytes 6291464 | tf_op jit(solution)/shard_map/ppermute | solution.py:205
  228.9 68.9 %collective-permute-start.11 = (bf16[24,256,256]{2,1,0:T(8,128)(2,1)}, bf16[24,256,256]{2,1,0:T(8,128)(2,1)S(1)}, u32[]{:S(2)}, u32[]{:S(2)}) collective-permute-start(bf16[24,256,256]{2,1,0:T(8,128)(2,1)} %slice.57), channel_id=1, source_target_pairs={{0,1},{3,2},{4,5},{7,6},{8,9},{11,10},{12,13},{15,14},{16,17},{19,... | collective-permute-start | bytes 9437192 | tf_op jit(solution)/shard_map/ppermute | solution.py:205
  260.8 1.3 copy-start.9
  262.2 4.4 copy-start.21
  265.3 46.2 %collective-permute-start.8 = (bf16[16,256,256]{2,1,0:T(8,128)(2,1)}, bf16[16,256,256]{2,1,0:T(8,128)(2,1)}, u32[]{:S(2)}, u32[]{:S(2)}) collective-permute-start(bf16[16,256,256]{2,1,0:T(8,128)(2,1)} %slice.60), channel_id=1, source_target_pairs={{1,0},{2,3},{5,4},{6,7},{9,8},{10,11},{13,12},{14,15},{17,16},{18,... | collective-permute-start | bytes 6291464 | tf_op jit(solution)/shard_map/ppermute | solution.py:205
  266.6 1.6 copy-start.10
  282.9 25.4 %collective-permute-start.7 = (bf16[8,256,256]{2,1,0:T(8,128)(2,1)}, bf16[8,256,256]{2,1,0:T(8,128)(2,1)S(1)}, u32[]{:S(2)}, u32[]{:S(2)}) collective-permute-start(bf16[8,256,256]{2,1,0:T(8,128)(2,1)} %collective-permute-done.5.refs_1_), channel_id=1, source_target_pairs={{1,2},{2,1},{5,6},{6,5},{9,10},{10,9},{13,14},{14,13},{17,18},{18,... | collective-permute-start | bytes 3145736 | tf_op jit(solution)/shard_map/ppermute | solution.py:205
  297.8 9.7 %copy-start = (bf16[24,256,256]{2,1,0:T(8,128)(2,1)}, bf16[24,256,256]{2,1,0:T(8,128)(2,1)S(1)}, u32[]{:S(2)}) copy-start(bf16[24,256,256]{2,1,0:T(8,128)(2,1)S(1)} %collective-permute-done.11.refs_1_.refs_2_) | copy-start | bytes 9437188
  297.8 10.5 %collective-permute-start.10 = (f16[256,256]{1,0:T(8,128)(2,1)S(1)}, f16[256,256]{1,0:T(8,128)(2,1)S(1)}, u32[]{:S(2)}, u32[]{:S(2)}) collective-permute-start(f16[256,256]{1,0:T(8,128)(2,1)S(1)} %get-tuple-element.80), channel_id=1, source_target_pairs={{0,1},{3,2},{4,5},{7,6},{8,9},{11,10},{12,13},{15,14},{16,17},{19,... | collective-permute-start | bytes 393224 | tf_op jit(solution)/shard_map/ppermute | solution.py:205
  307.5 32.8 %collective-permute-start.13 = (bf16[8,256,256]{2,1,0:T(8,128)(2,1)}, bf16[8,256,256]{2,1,0:T(8,128)(2,1)S(1)}, u32[]{:S(2)}, u32[]{:S(2)}) collective-permute-start(bf16[8,256,256]{2,1,0:T(8,128)(2,1)} %get-tuple-element.82), channel_id=1, source_target_pairs={{1,2},{2,1},{5,6},{6,5},{9,10},{10,9},{13,14},{14,13},{17,18},{18,... | collective-permute-start | bytes 3145736 | tf_op jit(solution)/shard_map/ppermute | solution.py:205
  308.3 1.0 copy-start.6
  320.7 1.2 copy-start.7
  328.2 27.2 %collective-permute-start.14 = (f16[8,256,256]{2,1,0:T(8,128)(2,1)S(1)}, f16[8,256,256]{2,1,0:T(8,128)(2,1)S(1)}, u32[]{:S(2)}, u32[]{:S(2)}) collective-permute-start(f16[8,256,256]{2,1,0:T(8,128)(2,1)S(1)} %multiply_convert_fusion.3), channel_id=1, source_target_pairs={{1,0},{2,3},{5,4},{6,7},{9,8},{10,11},{13,12},{14,15},{17,16},{18,... | collective-permute-start | bytes 3145736 | tf_op jit(solution)/shard_map/ppermute | solution.py:205
  329.5 29.2 %collective-permute-start.12 = (bf16[8,256,256]{2,1,0:T(8,128)(2,1)}, bf16[8,256,256]{2,1,0:T(8,128)(2,1)S(1)}, u32[]{:S(2)}, u32[]{:S(2)}) collective-permute-start(bf16[8,256,256]{2,1,0:T(8,128)(2,1)} %get-tuple-element.83), channel_id=1, source_target_pairs={{1,2},{2,1},{5,6},{6,5},{9,10},{10,9},{13,14},{14,13},{17,18},{18,... | collective-permute-start | bytes 3145736 | tf_op jit(solution)/shard_map/ppermute | solution.py:205
  340.3 17.2 %copy-start.2 = (f32[16,256,256]{2,1,0:T(8,128)S(1)}, f32[16,256,256]{2,1,0:T(8,128)}, u32[]{:S(2)}) copy-start(f32[16,256,256]{2,1,0:T(8,128)} %tiles.8.refs_0_) | copy-start | bytes 12582916
  340.3 17.2 %copy-start.3 = (f32[16,256,256]{2,1,0:T(8,128)S(1)}, f32[16,256,256]{2,1,0:T(8,128)}, u32[]{:S(2)}) copy-start(f32[16,256,256]{2,1,0:T(8,128)} %tiles.10.refs_1_) | copy-start | bytes 12582916
  355.4 3.2 copy-start.17
  355.4 23.3 %collective-permute-start.16 = (f16[8,256,256]{2,1,0:T(8,128)(2,1)}, f16[8,256,256]{2,1,0:T(8,128)(2,1)S(1)}, u32[]{:S(2)}, u32[]{:S(2)}) collective-permute-start(f16[8,256,256]{2,1,0:T(8,128)(2,1)} %multiply_convert_fusion.2), channel_id=1, source_target_pairs={{1,0},{2,3},{5,4},{6,7},{9,8},{10,11},{13,12},{14,15},{17,16},{18,... | collective-permute-start | bytes 3145736 | tf_op jit(solution)/shard_map/ppermute | solution.py:205
  356.7 32.7 %collective-permute-start.15 = (bf16[8,256,256]{2,1,0:T(8,128)(2,1)}, bf16[8,256,256]{2,1,0:T(8,128)(2,1)S(1)}, u32[]{:S(2)}, u32[]{:S(2)}) collective-permute-start(bf16[8,256,256]{2,1,0:T(8,128)(2,1)} %get-tuple-element.81), channel_id=1, source_target_pairs={{1,2},{2,1},{5,6},{6,5},{9,10},{10,9},{13,14},{14,13},{17,18},{18,... | collective-permute-start | bytes 3145736 | tf_op jit(solution)/shard_map/ppermute | solution.py:205
  363.4 1.3 copy-start.12
  364.8 15.4 %copy-start.8 = (bf16[8,256,256]{2,1,0:T(8,128)(2,1)S(1)}, bf16[8,256,256]{2,1,0:T(8,128)(2,1)}, u32[]{:S(2)}) copy-start(bf16[8,256,256]{2,1,0:T(8,128)(2,1)} %copy-done.6) | copy-start | bytes 3145732
  378.7 10.6 %copy-start.19 = (f16[8,256,256]{2,1,0:T(8,128)(2,1)}, f16[8,256,256]{2,1,0:T(8,128)(2,1)S(1)}, u32[]{:S(2)}) copy-start(f16[8,256,256]{2,1,0:T(8,128)(2,1)S(1)} %collective-permute-done.16) | copy-start | bytes 3145732
  378.7 24.9 %collective-permute-start.18 = (f16[8,256,256]{2,1,0:T(8,128)(2,1)}, f16[8,256,256]{2,1,0:T(8,128)(2,1)}, u32[]{:S(2)}, u32[]{:S(2)}) collective-permute-start(f16[8,256,256]{2,1,0:T(8,128)(2,1)} %multiply_convert_fusion.1), channel_id=1, source_target_pairs={{1,0},{2,3},{5,4},{6,7},{9,8},{10,11},{13,12},{14,15},{17,16},{18,... | collective-permute-start | bytes 3145736 | tf_op jit(solution)/shard_map/ppermute | solution.py:205
  394.1 1.3 copy-start.11
  395.5 9.4 %copy-start.1 = (bf16[24,256,256]{2,1,0:T(8,128)(2,1)S(1)}, bf16[24,256,256]{2,1,0:T(8,128)(2,1)}, u32[]{:S(2)}) copy-start(bf16[24,256,256]{2,1,0:T(8,128)(2,1)} %copy-done) | copy-start | bytes 9437188
  397.0 6.6 %collective-permute-start.17 = (f32[32,128]{1,0:T(8,128)S(1)}, f32[32,128]{1,0:T(8,128)S(1)}, u32[]{:S(2)}, u32[]{:S(2)}) collective-permute-start(f32[32,128]{1,0:T(8,128)S(1)} %pad_maximum_fusion), channel_id=1, source_target_pairs={{1,0},{2,3},{5,4},{6,7},{9,8},{10,11},{13,12},{14,15},{17,16},{18,... | collective-permute-start | bytes 49160 | tf_op jit(solution)/shard_map/ppermute | solution.py:205
  401.2 13.0 %copy-start.16 = (f32[256,256]{1,0:T(8,128)S(1)}, f32[256,256]{1,0:T(8,128)}, u32[]{:S(2)}) copy-start(f32[256,256]{1,0:T(8,128)} %get-tuple-element.79) | copy-start | bytes 786436
  401.2 13.0 %copy-start.18 = (f16[8,256,256]{2,1,0:T(8,128)(2,1)S(1)}, f16[8,256,256]{2,1,0:T(8,128)(2,1)}, u32[]{:S(2)}) copy-start(f16[8,256,256]{2,1,0:T(8,128)(2,1)} %copy-done.17) | copy-start | bytes 3145732
  403.6 21.8 %collective-permute-start.19 = (f16[8,256,256]{2,1,0:T(8,128)(2,1)}, f16[8,256,256]{2,1,0:T(8,128)(2,1)}, u32[]{:S(2)}, u32[]{:S(2)}) collective-permute-start(f16[8,256,256]{2,1,0:T(8,128)(2,1)} %multiply_convert_fusion), channel_id=1, source_target_pairs={{1,0},{2,3},{5,4},{6,7},{9,8},{10,11},{13,12},{14,15},{17,16},{18,... | collective-permute-start | bytes 3145736 | tf_op jit(solution)/shard_map/ppermute | solution.py:205
  413.6 1.5 copy-start.20
  415.1 12.5 %copy-start.5 = (f32[16,256,256]{2,1,0:T(8,128)S(1)}, f32[16,256,256]{2,1,0:T(8,128)}, u32[]{:S(2)}) copy-start(f32[16,256,256]{2,1,0:T(8,128)} %tiles.15.refs_3_) | copy-start | bytes 12582916
  416.2 11.4 %copy-start.4 = (f32[16,256,256]{2,1,0:T(8,128)S(1)}, f32[16,256,256]{2,1,0:T(8,128)}, u32[]{:S(2)}) copy-start(f32[16,256,256]{2,1,0:T(8,128)} %tiles.13.refs_2_) | copy-start | bytes 12582916
Sparse Core Ops, SparseCore 0:
  8.9 204.2 all-gather.4
  214.7 105.9 all-gather.6
